TPU v7x, 32 devices: a whole 2x2x4 slice. The times are simulated.
32 devices in a mesh: node: 8 (over z, y), local: 4 (over x, core).
Axes of the slice: x: 2, y: 2, z: 4, core: 2. Of those that a mesh axis runs over, the one named last changes fastest.
Arguments:
- tokens: bfloat16 [1024, 4096], P(('node', 'local')), may hold values from -6 to 6
- out_grad: bfloat16 [1024, 4096], P(('node', 'local')), may hold values from -6 to 6
- node_lists: int32 [1024, 4], P(('node', 'local')), may hold values from 0 to 7, as said below
- expert_local: int32 [1024, 8], P(('node', 'local')), may hold values from 0 to 15, as said below
- gate_fixed: int32 [1024, 8], P(('node', 'local')), may hold values from 4096 to 65535
- gate_weight: bfloat16 [32, 4096, 768], P(('node', 'local')), may hold values from -0.09375 to 0.09375
- up_weight: bfloat16 [32, 4096, 768], P(('node', 'local')), may hold values from -0.09375 to 0.09375
- down_weight: bfloat16 [32, 768, 4096], P(('node', 'local')), may hold values from -0.21875 to 0.21875
Outputs:
- token_grad: bfloat16 [1024, 4096], P(('node', 'local'))
- down_grad: bfloat16 [32, 768, 4096], P(('node', 'local'))
Inputs may be any that keep to these rules, and one draw needn't show every extreme that they name: `node_lists`: each row holds 4 different group numbers. `expert_local`: each row holds 8 different numbers.
All inputs are finite; a program needn't handle non-finite values.
Results may differ from a plain program's by a relative error of at most 0.0064.
Values may be sent and summed in bfloat16 or wider, within the bound.
No kernel may reach another device: no remote copies, remote signals or barrier semaphores. Data moves between devices by JAX's collectives and lax.ppermute only.
A program may use at most 128 MiB of HBM per device.

v0:
```python
import jax
import jax.numpy as jnp
from jax import lax
from jax.sharding import PartitionSpec as P


def expert_math(x_rows, dy_rows, w_gate_e, w_up_e, w_down_e):
    gate_act = jnp.dot(x_rows, w_gate_e, preferred_element_type=jnp.float32)
    up_act = jnp.dot(x_rows, w_up_e, preferred_element_type=jnp.float32)
    sig = jax.nn.sigmoid(gate_act)
    hidden = (gate_act * sig * up_act).astype(jnp.bfloat16)
    contract_rows = (((0,), (0,)), ((), ()))
    contract_last = (((1,), (1,)), ((), ()))
    down_local = lax.dot_general(
        hidden, dy_rows, contract_rows, preferred_element_type=jnp.float32
    ).astype(jnp.bfloat16)
    hidden_grad = lax.dot_general(
        dy_rows, w_down_e, contract_last, preferred_element_type=jnp.float32
    )
    gate_grad = (hidden_grad * up_act * sig * (1.0 + gate_act * (1.0 - sig))).astype(jnp.bfloat16)
    up_grad = (hidden_grad * gate_act * sig).astype(jnp.bfloat16)
    row_grad = (
        lax.dot_general(gate_grad, w_gate_e, contract_last, preferred_element_type=jnp.float32)
        + lax.dot_general(up_grad, w_up_e, contract_last, preferred_element_type=jnp.float32)
    ).astype(jnp.bfloat16)
    return (down_local, row_grad)


def body(
    tokens, out_grad, node_lists, expert_local, gate_fixed, gate_weight, up_weight, down_weight
):
    nodes = lax.axis_size("node")
    per_node = lax.axis_size("local")
    experts = nodes * per_node
    tok_dev, top_count = expert_local.shape
    width = tokens.shape[1]
    capacity = tok_dev * top_count // experts
    node_pick = jnp.take_along_axis(node_lists, expert_local // per_node, axis=1)
    expert_ids = (node_pick * per_node + expert_local % per_node).reshape(-1)
    onehot = (expert_ids[:, None] == jnp.arange(experts, dtype=jnp.int32)[None, :]).astype(
        jnp.int32
    )
    running = jnp.cumsum(onehot, axis=0)
    slot = jnp.sum(onehot * running, axis=1) - 1
    kept = slot < capacity
    position = jnp.where(kept, expert_ids * capacity + slot, experts * capacity)
    w_gate_e = gate_weight[0]
    w_up_e = up_weight[0]
    w_down_e = down_weight[0]
    gate_flat = gate_fixed.reshape(-1)
    table = jnp.full((experts * capacity,), -1, jnp.int32)
    table = table.at[position].set(jnp.arange(tok_dev * top_count, dtype=jnp.int32), mode="drop")
    valid = table >= 0
    safe = jnp.maximum(table, 0)
    rows = safe // top_count
    send_x = jnp.where(valid[:, None], tokens[rows], jnp.zeros((), jnp.bfloat16)).reshape(
        experts, capacity, width
    )
    gate_val = gate_flat[safe].astype(jnp.float32) * (1.0 / 65536.0)
    send_dy = jnp.where(valid[:, None], gate_val[:, None] * out_grad[rows].astype(jnp.float32), 0.0)
    send_dy = send_dy.astype(jnp.bfloat16).reshape(experts, capacity, width)
    recv_x, recv_dy = (
        lax.all_to_all(send_x, ("node", "local"), split_axis=0, concat_axis=0, tiled=True),
        lax.all_to_all(send_dy, ("node", "local"), split_axis=0, concat_axis=0, tiled=True),
    )
    x_rows = recv_x.reshape(experts * capacity, width)
    dy_rows = recv_dy.reshape(experts * capacity, width)
    down_local, row_grad = expert_math(x_rows, dy_rows, w_gate_e, w_up_e, w_down_e)
    returned = lax.all_to_all(
        row_grad.reshape(experts, capacity, width),
        ("node", "local"),
        split_axis=0,
        concat_axis=0,
        tiled=True,
    )
    returned = returned.reshape(experts * capacity, width)
    lookup = jnp.where(kept, position, 0)
    picked = jnp.where(kept[:, None], returned[lookup].astype(jnp.float32), 0.0)
    token_grad = jnp.sum(picked.reshape(tok_dev, top_count, width), axis=1).astype(jnp.bfloat16)
    return (token_grad, down_local[None])


def solution(mesh):
    return jax.shard_map(
        body,
        mesh=mesh,
        in_specs=(
            P(("node", "local"), None),
            P(("node", "local"), None),
            P(("node", "local"), None),
            P(("node", "local"), None),
            P(("node", "local"), None),
            P(("node", "local"), None, None),
            P(("node", "local"), None, None),
            P(("node", "local"), None, None),
        ),
        out_specs=(P(("node", "local"), None), P(("node", "local"), None, None)),
        check_vma=False,
    )
```

profile of v0, /device:TPU:0, one launch (start us, length us, event | category | flops | bytes accessed | tf_op | source)
XLA Modules:
  0.0 193.2 jit_solution(3152423783415407385)
XLA Ops:
  0.7 0.8 copy.10
  1.5 0.1 reshape.191
  1.6 2.4 %gather_fusion.4 = s32[256]{0:T(256)S(1)} fusion(s32[32,4]{0,1:T(4,128)S(1)} %copy-done.1, s32[256]{0:T(256)S(1)} %reshape.191), kind=kCustom, calls=%fused_computation.4 | custom fusion | bytes 4096 | tf_op jit(solution)/shard_map/jit(take_along_axis)/gather | solution.py:38
  4.1 0.1 eq.27
  4.2 0.1 eq.31
  4.3 0.6 reduce-window.6
  4.9 0.2 slice_reduce_fusion
  5.1 0.1 fusion.31
  5.3 0.1 mul.73
  5.4 1.4 scatter_custom_fusion
  6.8 0.1 broadcast_in_dim.60
  6.9 1.8 gather_fusion.2
  8.8 1.5 bitcast_select_fusion
  10.3 7.4 %all-to-all-start.1 = ((bf16[32,8,4096]{2,1,0:T(8,128)(2,1)}), bf16[32,8,4096]{2,1,0:T(8,128)(2,1)}, u32[]{:S(2)}, u32[]{:S(2)}) async-start(bf16[32,8,4096]{2,1,0:T(8,128)(2,1)} %bitcast_select_fusion), calls=%async_computation.1 | async-start | bytes 4194304 | tf_op jit(solution)/shard_map/all_to_all | solution.py:63
  17.8 1.8 gather_fusion.1
  19.7 0.1 reshape.152
  19.8 1.9 %gather_fusion = s32[256]{0:T(256)S(1)} fusion(s32[256]{0:T(256)S(1)} %reshape.152, s32[1024]{0:T(1024)S(1)} %get-tuple-element.9), kind=kCustom, calls=%fused_computation | custom fusion | bytes 3072 | tf_op jit(solution)/shard_map/gather | solution.py:59
  21.8 2.1 %fusion.22 = bf16[32,8,4096]{2,1,0:T(8,128)(2,1)} fusion(bf16[256,4096]{1,0:T(8,128)(2,1)S(1)} %gather_fusion.1, f32[32,8]{1,0:T(8,128)S(1)} %mul.76, pred[32,8]{1,0:T(8,128)(4,1)S(1)} %broadcast_in_dim.60), kind=kLoop, calls=%fused_computation.25 | loop fusion | flops 4194304 | bytes 4195584 | tf_op jit(solution)/shard_map/convert_element_type | solution.py:61
  24.0 42.6 %all-to-all-done.1 = bf16[32,8,4096]{2,1,0:T(8,128)(2,1)} async-done(((bf16[32,8,4096]{2,1,0:T(8,128)(2,1)}), bf16[32,8,4096]{2,1,0:T(8,128)(2,1)}, u32[]{:S(2)}, u32[]{:S(2)}) %all-to-all-start.1) | async-done | bytes 2097184 | tf_op jit(solution)/shard_map/all_to_all | solution.py:63
  66.6 4.2 %all-to-all-start = ((bf16[32,8,4096]{2,1,0:T(8,128)(2,1)}), bf16[32,8,4096]{2,1,0:T(8,128)(2,1)S(1)}, u32[]{:S(2)}, u32[]{:S(2)}) async-start(bf16[32,8,4096]{2,1,0:T(8,128)(2,1)} %fusion.22), calls=%async_computation | async-start | bytes 4194304 | tf_op jit(solution)/shard_map/all_to_all | solution.py:64
  70.8 5.2 %fusion.2 = f32[256,768]{1,0:T(8,128)S(1)} fusion(bf16[1,4096,768]{2,1,0:T(8,128)(2,1)} %param.13, bf16[32,8,4096]{2,1,0:T(8,128)(2,1)} %all-to-all-done.1), kind=kOutput, calls=%fused_computation.9 | convolution fusion | flops 1610612736 | bytes 9175040 | tf_op jit(solution)/shard_map/dot_general | solution.py:8
  76.0 6.1 %fusion.6 = f32[256,768]{1,0:T(8,128)} fusion(bf16[1,4096,768]{2,1,0:T(8,128)(2,1)} %param.14, bf16[32,8,4096]{2,1,0:T(8,128)(2,1)} %all-to-all-done.1), kind=kOutput, calls=%fused_computation.13 | convolution fusion | flops 1610612736 | bytes 9175040 | tf_op jit(solution)/shard_map/dot_general | solution.py:9
  82.1 37.5 %all-to-all-done = bf16[32,8,4096]{2,1,0:T(8,128)(2,1)S(1)} async-done(((bf16[32,8,4096]{2,1,0:T(8,128)(2,1)}), bf16[32,8,4096]{2,1,0:T(8,128)(2,1)S(1)}, u32[]{:S(2)}, u32[]{:S(2)}) %all-to-all-start) | async-done | bytes 2097184 | tf_op jit(solution)/shard_map/all_to_all | solution.py:64
  119.6 5.4 %fusion.8 = f32[256,768]{1,0:T(8,128)S(1)} fusion(bf16[1,768,4096]{2,1,0:T(8,128)(2,1)} %param.15, bf16[32,8,4096]{2,1,0:T(8,128)(2,1)S(1)} %all-to-all-done), kind=kOutput, calls=%fused_computation.15 | convolution fusion | flops 1610612736 | bytes 9175040 | tf_op jit(solution)/shard_map/dot_general | solution.py:17
  125.0 4.9 %fusion = f32[256,4096]{1,0:T(8,128)S(1)} fusion(bf16[1,4096,768]{2,1,0:T(8,128)(2,1)} %param.13, f32[256,768]{1,0:T(8,128)S(1)} %fusion.2, f32[256,768]{1,0:T(8,128)S(1)} %fusion.8, f32[256,768]{1,0:T(8,128)S(1)} %copy-done.4), kind=kOutput, calls=%fused_computation.7 | convolution fusion | flops 1612578816 | bytes 12845056 | tf_op jit(solution)/shard_map/dot_general | solution.py:23
  129.9 3.2 %fusion.17 = bf16[32,8,4096]{2,1,0:T(8,128)(2,1)} fusion(f32[256,4096]{1,0:T(8,128)S(1)} %fusion, bf16[1,4096,768]{2,1,0:T(8,128)(2,1)S(1)} %bitcast.66, f32[256,768]{1,0:T(8,128)S(1)} %fusion.8, f32[256,768]{1,0:T(8,128)S(1)} %fusion.2), kind=kOutput, calls=%fused_computation.20 | convolution fusion | flops 1613889536 | bytes 14155776 | tf_op jit(solution)/shard_map/dot_general | solution.py:24
  133.1 4.2 %all-to-all-start.2 = ((bf16[32,8,4096]{2,1,0:T(8,128)(2,1)}), bf16[32,8,4096]{2,1,0:T(8,128)(2,1)S(1)}, u32[]{:S(2)}, u32[]{:S(2)}) async-start(bf16[32,8,4096]{2,1,0:T(8,128)(2,1)} %fusion.17), calls=%async_computation.2 | async-start | bytes 4194304 | tf_op jit(solution)/shard_map/all_to_all | solution.py:69
  137.3 0.1 lt.62
  137.4 6.4 %fusion.10 = bf16[1,768,4096]{2,1,0:T(8,128)(2,1)} fusion(bf16[32,8,4096]{2,1,0:T(8,128)(2,1)} %copy-done.3, f32[256,768]{1,0:T(8,128)} %fusion.6, f32[256,768]{1,0:T(8,128)S(1)} %fusion.2), kind=kOutput, calls=%fused_computation.17 | convolution fusion | flops 1614938112 | bytes 9961472 | tf_op jit(solution)/shard_map/dot_general | solution.py:14
  143.8 42.2 %all-to-all-done.2 = bf16[32,8,4096]{2,1,0:T(8,128)(2,1)S(1)} async-done(((bf16[32,8,4096]{2,1,0:T(8,128)(2,1)}), bf16[32,8,4096]{2,1,0:T(8,128)(2,1)S(1)}, u32[]{:S(2)}, u32[]{:S(2)}) %all-to-all-start.2) | async-done | bytes 2097184 | tf_op jit(solution)/shard_map/all_to_all | solution.py:69
  186.1 3.2 %gather_fusion.3 = bf16[256,4096]{1,0:T(8,128)(2,1)} fusion(bf16[256,4096]{1,0:T(8,128)(2,1)S(1)} %bitcast.64, s32[1024]{0:T(1024)S(1)} %pad_clamp_fusion), kind=kCustom, calls=%fused_computation.3 | custom fusion | bytes 4195328 | tf_op jit(solution)/shard_map/gather | solution.py:78
  189.2 3.9 %fusion.20 = bf16[32,4096]{1,0:T(8,128)(2,1)} fusion(bf16[256,4096]{1,0:T(8,128)(2,1)} %gather_fusion.3, pred[32,8]{1,0:T(8,128)(4,1)S(1)} %lt.62), kind=kLoop, calls=%fused_computation.22 | loop fusion | flops 3014656 | bytes 2359552 | tf_op jit(solution)/shard_map/reduce_sum | solution.py:79
  (34 shorter events, 0.4 us)
Async XLA Ops:
  0.6 6.3 %copy-start = (bf16[32,4096]{1,0:T(8,128)(2,1)S(1)}, bf16[32,4096]{1,0:T(8,128)(2,1)}, u32[]{:S(2)}) copy-start(bf16[32,4096]{1,0:T(8,128)(2,1)} %param.8) | copy-start | bytes 786436
  0.6 0.9 copy-start.1
  10.3 7.4 %copy-start.2 = (bf16[32,4096]{1,0:T(8,128)(2,1)S(1)}, bf16[32,4096]{1,0:T(8,128)(2,1)}, u32[]{:S(2)}) copy-start(bf16[32,4096]{1,0:T(8,128)(2,1)} %param.9) | copy-start | bytes 786436
  10.3 56.3 %all-to-all-start.1 = ((bf16[32,8,4096]{2,1,0:T(8,128)(2,1)}), bf16[32,8,4096]{2,1,0:T(8,128)(2,1)}, u32[]{:S(2)}, u32[]{:S(2)}) async-start(bf16[32,8,4096]{2,1,0:T(8,128)(2,1)} %bitcast_select_fusion), calls=%async_computation.1 | async-start | bytes 4194304 | tf_op jit(solution)/shard_map/all_to_all | solution.py:63
  17.7 1.9 copy-start.5
  66.6 53.0 %all-to-all-start = ((bf16[32,8,4096]{2,1,0:T(8,128)(2,1)}), bf16[32,8,4096]{2,1,0:T(8,128)(2,1)S(1)}, u32[]{:S(2)}, u32[]{:S(2)}) async-start(bf16[32,8,4096]{2,1,0:T(8,128)(2,1)} %fusion.22), calls=%async_computation | async-start | bytes 4194304 | tf_op jit(solution)/shard_map/all_to_all | solution.py:64
  119.6 5.4 %copy-start.3 = (bf16[32,8,4096]{2,1,0:T(8,128)(2,1)}, bf16[32,8,4096]{2,1,0:T(8,128)(2,1)S(1)}, u32[]{:S(2)}) copy-start(bf16[32,8,4096]{2,1,0:T(8,128)(2,1)S(1)} %all-to-all-done) | copy-start | bytes 6291460
  119.6 5.4 %copy-start.4 = (f32[256,768]{1,0:T(8,128)S(1)}, f32[256,768]{1,0:T(8,128)}, u32[]{:S(2)}) copy-start(f32[256,768]{1,0:T(8,128)} %fusion.6) | copy-start | bytes 2359300
  119.6 10.3 %slice-start = ((s8[6291456]{0:T(1024)(128)(4,1)}), s8[4194304]{0:T(1024)(128)(4,1)S(1)}, s32[]{:S(2)}) async-start(s8[6291456]{0:T(1024)(128)(4,1)} %bitcast.65), calls=%async_computation.3 | async-start | bytes 8388608
  125.0 4.9 %slice-start.1 = ((s8[6291456]{0:T(1024)(128)(4,1)}), s8[2097152]{0:T(1024)(128)(4,1)S(1)}, s32[]{:S(2)}) async-start(s8[6291456]{0:T(1024)(128)(4,1)} %bitcast.65), calls=%async_computation.4 | async-start | bytes 4194304
  133.1 52.9 %all-to-all-start.2 = ((bf16[32,8,4096]{2,1,0:T(8,128)(2,1)}), bf16[32,8,4096]{2,1,0:T(8,128)(2,1)S(1)}, u32[]{:S(2)}, u32[]{:S(2)}) async-start(bf16[32,8,4096]{2,1,0:T(8,128)(2,1)} %fusion.17), calls=%async_computation.2 | async-start | bytes 4194304 | tf_op jit(solution)/shard_map/all_to_all | solution.py:69
where the time goes:
time: 194 us; the launch traced here: 193 us
  waiting for transfers between devices  122 us (63%)
  matrix products  31.2 us (16%)
  starting transfers between devices  15.8 us (8%)
  local copies, waits for them, and re-layouts  14.5 us (7%)
  other arithmetic  8.43 us (4%)
    all_to_all x1, waiting for transfers between devices, body(): lax.all_to_all(send_x, ('node', 'local'), split_axis=0, concat_axis=0, ti...  42.6 us
    all_to_all x1, waiting for transfers between devices, body(): lax.all_to_all(row_grad.reshape(experts, capacity, width), ('node', 'loca...  42.2 us
    all_to_all x1, waiting for transfers between devices, body(): lax.all_to_all(send_dy, ('node', 'local'), split_axis=0, concat_axis=0, t...  37.5 us
    all_to_all x1, starting transfers between devices, body(): lax.all_to_all(send_x, ('node', 'local'), split_axis=0, concat_axis=0, ti...  7.43 us
    dot_general x1, matrix products, expert_math(): lax.dot_general(hidden, dy_rows, contract_rows, preferred_element_type=jn...  6.42 us
    dot_general x1, matrix products, expert_math(): up_act = jnp.dot(x_rows, w_up_e, preferred_element_type=jnp.float32)  6.09 us
    dot_general x1, matrix products, expert_math(): lax.dot_general(dy_rows, w_down_e, contract_last, preferred_element_type=...  5.42 us
    dot_general x1, matrix products, expert_math(): gate_act = jnp.dot(x_rows, w_gate_e, preferred_element_type=jnp.float32)  5.2 us
  transfers between devices with their start and end apart: 3, of which 3 were waited for; matrix products, arithmetic and copies ran while one was open for 12% of the time, Pallas kernels for 0%

commit v1 on v0

v1 whole, which is shorter than its diff:
```python
import jax
import jax.numpy as jnp
from jax import lax
from jax.sharding import PartitionSpec as P

AXES = ("node", "local")
BF16 = jnp.bfloat16
F32 = jnp.float32


def device_perms(nodes, per_node):
    depth = nodes // 2
    order = [z for z in range(depth) if z == 0 or z % 2 == 1]
    order += [z for z in reversed(range(depth)) if z not in order]
    follow = {order[i]: order[(i + 1) % depth] for i in range(depth)}

    def flat(z, y, place):
        return (z * 2 + y) * per_node + place

    cells = [(z, y, p) for z in range(depth) for y in range(2) for p in range(per_node)]
    ring = [(flat(z, y, p), flat(follow[z], y, p)) for z, y, p in cells]
    back = [(b, a) for a, b in ring]
    flip_x = [(flat(z, y, p), flat(z, y, p ^ 2)) for z, y, p in cells]
    flip_y = [(flat(z, y, p), flat(z, 1 - y, p)) for z, y, p in cells]
    flip_xy = [(flat(z, y, p), flat(z, 1 - y, p ^ 2)) for z, y, p in cells]
    flip_core = [(flat(z, y, p), flat(z, y, p ^ 1)) for z, y, p in cells]
    return depth, ring, back, (flip_x, flip_y, flip_xy), flip_core


def route(node_lists, expert_local, gate_fixed, experts, per_node, capacity):
    tok_dev = expert_local.shape[0]
    place = expert_local // per_node
    group = jnp.zeros_like(expert_local)
    for j in range(node_lists.shape[1]):
        group = jnp.where(place == j, node_lists[:, j : j + 1], group)
    expert = group * per_node + expert_local % per_node
    ids = jnp.arange(experts, dtype=jnp.int32)
    member = jnp.any(expert[:, :, None] == ids[None, None, :], axis=1)
    earlier = jnp.tril(jnp.ones((tok_dev, tok_dev), BF16), -1)
    before = jnp.dot(earlier, member.astype(BF16), preferred_element_type=F32).astype(jnp.int32)
    slot = jnp.sum(jnp.where(expert[:, :, None] == ids[None, None, :], before[:, None, :], 0), axis=2)
    code = jnp.where(slot < capacity, expert * capacity + slot, -1)
    meta = jnp.concatenate([code, gate_fixed // 256, gate_fixed % 256], axis=1).astype(BF16)
    return jnp.pad(meta, ((0, 0), (0, -meta.shape[1] % 128)))


def selection(meta, top, codes):
    meta = meta.astype(F32)
    code = meta[:, :top].astype(jnp.int32)
    gate = meta[:, top : 2 * top] * 256.0 + meta[:, 2 * top : 3 * top]
    hit = code[:, :, None] == codes[None, None, :]
    pick = jnp.any(hit, axis=1)
    gate = jnp.sum(jnp.where(hit, gate[:, :, None], 0.0), axis=(0, 1))
    return pick.astype(BF16), gate


def expert_math(x_rows, dy_rows, w_gate_e, w_up_e, w_down_e):
    gate_act = jnp.dot(x_rows, w_gate_e, preferred_element_type=F32)
    up_act = jnp.dot(x_rows, w_up_e, preferred_element_type=F32)
    sig = jax.nn.sigmoid(gate_act)
    hidden = (gate_act * sig * up_act).astype(BF16)
    rows = (((0,), (0,)), ((), ()))
    last = (((1,), (1,)), ((), ()))
    down_local = lax.dot_general(hidden, dy_rows, rows, preferred_element_type=F32).astype(BF16)
    hidden_grad = lax.dot_general(dy_rows, w_down_e, last, preferred_element_type=F32)
    gate_grad = (hidden_grad * up_act * sig * (1.0 + gate_act * (1.0 - sig))).astype(BF16)
    up_grad = (hidden_grad * gate_act * sig).astype(BF16)
    row_grad = (
        lax.dot_general(gate_grad, w_gate_e, last, preferred_element_type=F32)
        + lax.dot_general(up_grad, w_up_e, last, preferred_element_type=F32)
    ).astype(BF16)
    return down_local, row_grad


def body(
    tokens, out_grad, node_lists, expert_local, gate_fixed, gate_weight, up_weight, down_weight
):
    nodes, per_node = lax.axis_size("node"), lax.axis_size("local")
    experts = nodes * per_node
    tok_dev, top = expert_local.shape
    width = tokens.shape[1]
    capacity = tok_dev * top // experts
    depth, ring, back, flips, flip_core = device_perms(nodes, per_node)
    places = per_node // 2

    node, place = lax.axis_index("node"), lax.axis_index("local")
    plane = node // 2 * 2 * per_node
    here = (node % 2) * per_node + place
    chips = (0, 2, per_node, per_node + 2)
    reach = jnp.array([a ^ b for a in chips for b in (0, 1)], jnp.int32)
    slots = jnp.arange(capacity, dtype=jnp.int32)
    codes = ((plane + (here ^ reach))[:, None] * capacity + slots[None, :]).reshape(-1)
    pair = 2 * capacity

    meta = route(node_lists, expert_local, gate_fixed, experts, per_node, capacity)
    held = jnp.concatenate([tokens, out_grad, meta], axis=1)
    first = jnp.arange(2 * width)[None, :] < width
    picks, mine, other = [], [], []
    for step in range(depth):
        coming = lax.ppermute(held, AXES, ring) if step < depth - 1 else None
        pick, gate = selection(held[:, 2 * width :], top, codes)
        picks.append(pick)
        chosen = lax.dot_general(
            pick, held[:, : 2 * width], (((0,), (0,)), ((), ())), preferred_element_type=F32
        )
        scale = jnp.where(first, 1.0, (gate * (1.0 / 65536.0))[:, None])
        chosen = (chosen * scale).astype(BF16)
        got = [chosen[:pair]]
        for i, flip in enumerate(flips):
            got.append(lax.ppermute(chosen[(i + 1) * pair : (i + 2) * pair], AXES, flip))
        mine += [g[:capacity] for g in got]
        other += [g[capacity:] for g in got]
        held = coming
    cut = 4 * (depth - 1)
    crossed = [lax.ppermute(jnp.concatenate(part, axis=0), AXES, flip_core) for part in (other[:cut], other[cut:])]
    rows = jnp.concatenate(mine + crossed, axis=0)

    down_local, row_grad = expert_math(
        rows[:, :width], rows[:, width:], gate_weight[0], up_weight[0], down_weight[0]
    )

    half = depth * 4 * capacity
    own = row_grad[:half].reshape(depth, 4, capacity, width)
    theirs = row_grad[half:].reshape(depth, 4, capacity, width)
    last = lax.ppermute(theirs[depth - 1 :], AXES, flip_core)
    rest = lax.ppermute(theirs[: depth - 1], AXES, flip_core)
    total = None
    for step in reversed(range(depth)):
        swapped = last[0] if step == depth - 1 else rest[step]
        both = jnp.concatenate([own[step], swapped], axis=1)
        got = [both[0]] + [lax.ppermute(both[i + 1], AXES, flip) for i, flip in enumerate(flips)]
        partial = jnp.dot(picks[step], jnp.concatenate(got, axis=0), preferred_element_type=F32)
        if total is not None:
            partial = partial + total.astype(F32)
        total = partial.astype(BF16)
        if step:
            total = lax.ppermute(total, AXES, back)
    return total, down_local[None]


def solution(mesh):
    split = P(AXES)
    return jax.shard_map(
        body, mesh=mesh, in_specs=(split,) * 8, out_specs=(split, split), check_vma=False
    )
```

time: 194 us -> 149 us (0.77)
  waiting for transfers between devices: 122 us -> 76.9 us
  starting transfers between devices: 15.8 us -> 42.9 us
  matrix products: 31.2 us -> 19.5 us
  local copies, waits for them, and re-layouts: 14.5 us -> 4.55 us
  other arithmetic: 8.43 us -> 3.36 us
    all_to_all x3 -> x0, waiting for transfers between devices: 122 us -> none  [the longest x1 42.6 us: body(): lax.all_to_all(send_x, ('node', 'local'), split_axis=0, concat_axis=0, ti...]
    ppermute x0 -> x34, waiting for transfers between devices: none -> 76.9 us  [the longest x3 38.8 us: body(): coming = lax.ppermute(held, AXES, ring) if step < depth - 1 else None]
    ppermute x0 -> x34, starting transfers between devices: none -> 42.9 us  [the longest x12 17.4 us: body(): got.append(lax.ppermute(chosen[(i + 1) * pair:(i + 2) * pair], AXES, flip))]
    all_to_all x3 -> x0, starting transfers between devices: 15.8 us -> none  [the longest x1 7.43 us: body(): lax.all_to_all(send_x, ('node', 'local'), split_axis=0, concat_axis=0, ti...]
    dot_general x6 -> x15, matrix products: 31.2 us -> 19.5 us  [the longest x1 4.58 us: expert_math(): lax.dot_general(hidden, dy_rows, rows, preferred_element_type=F32)]
    gather x7 -> x0, local copies, waits for them, and re-layouts: 11.4 us -> none  [the longest x1 3.18 us: body(): picked = jnp.where(kept[:, None], returned[lookup].astype(jnp.float32), 0.0)]
    reduce_sum x2, other arithmetic: 4.02 us -> 1.04 us  [the longest x1 0.69 us: route(): jnp.sum(jnp.where(expert[:, :, None] == ids[None, None, :], before[:, Non...]
    unnamed x18 -> x28, local copies, waits for them, and re-layouts: 0.93 us -> 3.08 us
  transfers between devices with their start and end apart: 3 -> 34, of which waited for: 3 -> 23; matrix products, arithmetic and copies ran while one was open for 12% -> 6% of each run, Pallas kernels for 0% -> 0%
where the time goes in v1:
time: 149 us; the launch traced here: 148 us
  waiting for transfers between devices  76.9 us (52%)
  starting transfers between devices  42.9 us (29%)
  matrix products  19.5 us (13%)
  local copies, waits for them, and re-layouts  4.55 us (3%)
  other arithmetic  3.36 us (2%)
    ppermute x3, waiting for transfers between devices, body(): coming = lax.ppermute(held, AXES, ring) if step < depth - 1 else None  38.8 us
    ppermute x12, waiting for transfers between devices, body(): got.append(lax.ppermute(chosen[(i + 1) * pair:(i + 2) * pair], AXES, flip))  24.9 us
    ppermute x12, starting transfers between devices, body(): got.append(lax.ppermute(chosen[(i + 1) * pair:(i + 2) * pair], AXES, flip))  17.4 us
    ppermute x12, starting transfers between devices, body(): lax.ppermute(both[i + 1], AXES, flip)  13.3 us
    ppermute x12, waiting for transfers between devices, body(): lax.ppermute(both[i + 1], AXES, flip)  8.19 us
    ppermute x3, starting transfers between devices, body(): total = lax.ppermute(total, AXES, back)  6.87 us
    dot_general x1, matrix products, expert_math(): lax.dot_general(hidden, dy_rows, rows, preferred_element_type=F32)  4.58 us
    ppermute x3, starting transfers between devices, body(): coming = lax.ppermute(held, AXES, ring) if step < depth - 1 else None  4.43 us
  transfers between devices with their start and end apart: 34, of which 23 were waited for; matrix products, arithmetic and copies ran while one was open for 6% of the time, Pallas kernels for 0%

profile of v1, /device:TPU:0, one launch (start us, length us, event | category | flops | bytes accessed | tf_op | source)
XLA Modules:
  0.0 148.2 jit_solution(10422286517423560962)
XLA Ops:
  5.4 3.1 %collective-permute-start.3 = (bf16[32,8320]{1,0:T(8,128)(2,1)S(1)}, bf16[32,8320]{1,0:T(8,128)(2,1)S(1)}, u32[]{:S(2)}, u32[]{:S(2)}) collective-permute-start(bf16[32,8320]{1,0:T(8,128)(2,1)S(1)} %pad_maximum_fusion), channel_id=1, source_target_pairs={{0,8},{1,9},{2,10},{3,11},{4,12},{5,13},{6,14},{7,15},{8,24},{9,25... | collective-permute-start | bytes 1597448 | tf_op jit(solution)/shard_map/ppermute | solution.py:100
  8.6 12.9 %collective-permute-done.3 = bf16[32,8320]{1,0:T(8,128)(2,1)S(1)} collective-permute-done((bf16[32,8320]{1,0:T(8,128)(2,1)S(1)}, bf16[32,8320]{1,0:T(8,128)(2,1)S(1)}, u32[]{:S(2)}, u32[]{:S(2)}) %collective-permute-start.3) | collective-permute-done | bytes 532512 | tf_op jit(solution)/shard_map/ppermute | solution.py:100
  22.5 13.3 %collective-permute-done.7 = bf16[32,8320]{1,0:T(8,128)(2,1)S(1)} collective-permute-done((bf16[32,8320]{1,0:T(8,128)(2,1)S(1)}, bf16[32,8320]{1,0:T(8,128)(2,1)S(1)}, u32[]{:S(2)}, u32[]{:S(2)}) %collective-permute-start.7) | collective-permute-done | bytes 532512 | tf_op jit(solution)/shard_map/ppermute | solution.py:100
  36.4 12.6 %collective-permute-done.11 = bf16[32,8320]{1,0:T(8,128)(2,1)S(1)} collective-permute-done((bf16[32,8320]{1,0:T(8,128)(2,1)S(1)}, bf16[32,8320]{1,0:T(8,128)(2,1)S(1)}, u32[]{:S(2)}, u32[]{:S(2)}) %collective-permute-start.11) | collective-permute-done | bytes 532512 | tf_op jit(solution)/shard_map/ppermute | solution.py:100
  60.6 1.9 %collective-permute-start.6 = (bf16[16,8192]{1,0:T(8,128)(2,1)S(1)}, bf16[16,8192]{1,0:T(8,128)(2,1)S(1)}, u32[]{:S(2)}, u32[]{:S(2)}) collective-permute-start(bf16[16,8192]{1,0:T(8,128)(2,1)S(1)} %get-tuple-element.31), channel_id=1, source_target_pairs={{0,6},{1,7},{2,4},{3,5},{4,2},{5,3},{6,0},{7,1},{8,14},{9,15},{10,... | collective-permute-start | bytes 786440 | tf_op jit(solution)/shard_map/ppermute | solution.py:110
  62.5 4.4 %collective-permute-done.1 = bf16[16,8192]{1,0:T(8,128)(2,1)S(1)} collective-permute-done((bf16[16,8192]{1,0:T(8,128)(2,1)S(1)}, bf16[16,8192]{1,0:T(8,128)(2,1)S(1)}, u32[]{:S(2)}, u32[]{:S(2)}) %collective-permute-start.1) | collective-permute-done | bytes 262176 | tf_op jit(solution)/shard_map/ppermute | solution.py:110
  66.9 2.1 %collective-permute-start.9 = (bf16[16,8192]{1,0:T(8,128)(2,1)S(1)}, bf16[16,8192]{1,0:T(8,128)(2,1)S(1)}, u32[]{:S(2)}, u32[]{:S(2)}) collective-permute-start(bf16[16,8192]{1,0:T(8,128)(2,1)S(1)} %get-tuple-element.29), channel_id=1, source_target_pairs={{0,4},{1,5},{2,6},{3,7},{4,0},{5,1},{6,2},{7,3},{8,12},{9,13},{10,... | collective-permute-start | bytes 786440 | tf_op jit(solution)/shard_map/ppermute | solution.py:110
  69.1 2.8 %collective-permute-done.4 = bf16[16,8192]{1,0:T(8,128)(2,1)S(1)} collective-permute-done((bf16[16,8192]{1,0:T(8,128)(2,1)S(1)}, bf16[16,8192]{1,0:T(8,128)(2,1)S(1)}, u32[]{:S(2)}, u32[]{:S(2)}) %collective-permute-start.4) | collective-permute-done | bytes 262176 | tf_op jit(solution)/shard_map/ppermute | solution.py:110
  71.9 1.9 %collective-permute-start.10 = (bf16[16,8192]{1,0:T(8,128)(2,1)S(1)}, bf16[16,8192]{1,0:T(8,128)(2,1)S(1)}, u32[]{:S(2)}, u32[]{:S(2)}) collective-permute-start(bf16[16,8192]{1,0:T(8,128)(2,1)S(1)} %get-tuple-element.28), channel_id=1, source_target_pairs={{0,6},{1,7},{2,4},{3,5},{4,2},{5,3},{6,0},{7,1},{8,14},{9,15},{10,... | collective-permute-start | bytes 786440 | tf_op jit(solution)/shard_map/ppermute | solution.py:110
  73.8 2.1 %collective-permute-done.5 = bf16[16,8192]{1,0:T(8,128)(2,1)S(1)} collective-permute-done((bf16[16,8192]{1,0:T(8,128)(2,1)S(1)}, bf16[16,8192]{1,0:T(8,128)(2,1)S(1)}, u32[]{:S(2)}, u32[]{:S(2)}) %collective-permute-start.5) | collective-permute-done | bytes 262176 | tf_op jit(solution)/shard_map/ppermute | solution.py:110
  78.0 2.2 %collective-permute-start.13 = (bf16[16,8192]{1,0:T(8,128)(2,1)S(1)}, bf16[16,8192]{1,0:T(8,128)(2,1)S(1)}, u32[]{:S(2)}, u32[]{:S(2)}) collective-permute-start(bf16[16,8192]{1,0:T(8,128)(2,1)S(1)} %get-tuple-element.26), channel_id=1, source_target_pairs={{0,4},{1,5},{2,6},{3,7},{4,0},{5,1},{6,2},{7,3},{8,12},{9,13},{10,... | collective-permute-start | bytes 786440 | tf_op jit(solution)/shard_map/ppermute | solution.py:110
  80.3 2.9 %collective-permute-done.8 = bf16[16,8192]{1,0:T(8,128)(2,1)S(1)} collective-permute-done((bf16[16,8192]{1,0:T(8,128)(2,1)S(1)}, bf16[16,8192]{1,0:T(8,128)(2,1)S(1)}, u32[]{:S(2)}, u32[]{:S(2)}) %collective-permute-start.8) | collective-permute-done | bytes 262176 | tf_op jit(solution)/shard_map/ppermute | solution.py:110
  83.2 1.9 %collective-permute-start.14 = (bf16[16,8192]{1,0:T(8,128)(2,1)S(1)}, bf16[16,8192]{1,0:T(8,128)(2,1)S(1)}, u32[]{:S(2)}, u32[]{:S(2)}) collective-permute-start(bf16[16,8192]{1,0:T(8,128)(2,1)S(1)} %get-tuple-element.25), channel_id=1, source_target_pairs={{0,6},{1,7},{2,4},{3,5},{4,2},{5,3},{6,0},{7,1},{8,14},{9,15},{10,... | collective-permute-start | bytes 786440 | tf_op jit(solution)/shard_map/ppermute | solution.py:110
  85.1 2.1 %collective-permute-done.9 = bf16[16,8192]{1,0:T(8,128)(2,1)S(1)} collective-permute-done((bf16[16,8192]{1,0:T(8,128)(2,1)S(1)}, bf16[16,8192]{1,0:T(8,128)(2,1)S(1)}, u32[]{:S(2)}, u32[]{:S(2)}) %collective-permute-start.9) | collective-permute-done | bytes 262176 | tf_op jit(solution)/shard_map/ppermute | solution.py:110
  87.2 2.1 %collective-permute-done.10 = bf16[16,8192]{1,0:T(8,128)(2,1)S(1)} collective-permute-done((bf16[16,8192]{1,0:T(8,128)(2,1)S(1)}, bf16[16,8192]{1,0:T(8,128)(2,1)S(1)}, u32[]{:S(2)}, u32[]{:S(2)}) %collective-permute-start.10) | collective-permute-done | bytes 262176 | tf_op jit(solution)/shard_map/ppermute | solution.py:110
  89.4 4.3 %collective-permute-done.12 = bf16[16,8192]{1,0:T(8,128)(2,1)S(1)} collective-permute-done((bf16[16,8192]{1,0:T(8,128)(2,1)S(1)}, bf16[16,8192]{1,0:T(8,128)(2,1)S(1)}, u32[]{:S(2)}, u32[]{:S(2)}) %collective-permute-start.12) | collective-permute-done | bytes 262176 | tf_op jit(solution)/shard_map/ppermute | solution.py:110
  93.7 2.1 %collective-permute-done.13 = bf16[16,8192]{1,0:T(8,128)(2,1)S(1)} collective-permute-done((bf16[16,8192]{1,0:T(8,128)(2,1)S(1)}, bf16[16,8192]{1,0:T(8,128)(2,1)S(1)}, u32[]{:S(2)}, u32[]{:S(2)}) %collective-permute-start.13) | collective-permute-done | bytes 262176 | tf_op jit(solution)/shard_map/ppermute | solution.py:110
  97.0 1.8 %collective-permute-done.16 = bf16[32,8192]{1,0:T(8,128)(2,1)S(1)} collective-permute-done((bf16[32,8192]{1,0:T(8,128)(2,1)S(1)}, bf16[32,8192]{1,0:T(8,128)(2,1)S(1)}, u32[]{:S(2)}, u32[]{:S(2)}) %collective-permute-start.16) | collective-permute-done | bytes 524320 | tf_op jit(solution)/shard_map/ppermute | solution.py:115
  98.8 1.8 %fusion.10 = f32[256,768]{1,0:T(8,128)S(1)} fusion(bf16[1,4096,768]{2,1,0:T(8,128)(2,1)S(1)} %bitcast.87, bf16[256,8192]{1,0:T(8,128)(2,1)S(1)} %constant_dynamic-update-slice_fusion), kind=kOutput, calls=%fused_computation.15 | convolution fusion | flops 1610612736 | bytes 9175040 | tf_op jit(solution)/shard_map/dot_general | solution.py:59
  101.6 1.8 %fusion.6 = f32[256,768]{1,0:T(8,128)S(1)} fusion(bf16[1,4096,768]{2,1,0:T(8,128)(2,1)S(1)} %bitcast.89, bf16[256,8192]{1,0:T(8,128)(2,1)S(1)} %constant_dynamic-update-slice_fusion), kind=kOutput, calls=%fused_computation.11 | convolution fusion | flops 1610612736 | bytes 9175040 | tf_op jit(solution)/shard_map/dot_general | solution.py:58
  103.6 1.8 %fusion.12 = f32[256,768]{1,0:T(8,128)S(1)} fusion(bf16[1,768,4096]{2,1,0:T(8,128)(2,1)S(1)} %bitcast.93, bf16[256,8192]{1,0:T(8,128)(2,1)S(1)} %constant_dynamic-update-slice_fusion), kind=kOutput, calls=%fused_computation.17 | convolution fusion | flops 1610612736 | bytes 9175040 | tf_op jit(solution)/shard_map/dot_general | solution.py:65
  105.5 1.9 %fusion.4 = f32[256,4096]{1,0:T(8,128)S(1)} fusion(bf16[1,4096,768]{2,1,0:T(8,128)(2,1)S(1)} %bitcast.89, f32[256,768]{1,0:T(8,128)S(1)} %fusion.6, f32[256,768]{1,0:T(8,128)S(1)} %fusion.12, f32[256,768]{1,0:T(8,128)S(1)} %fusion.10), kind=kOutput, calls=%fused_computation.9 | convolution fusion | flops 1612578816 | bytes 12845056 | tf_op jit(solution)/shard_map/dot_general | solution.py:69
  107.4 1.8 %fusion.18 = bf16[256,4096]{1,0:T(8,128)(2,1)S(1)} fusion(f32[256,4096]{1,0:T(8,128)S(1)} %fusion.4, bf16[1,4096,768]{2,1,0:T(8,128)(2,1)S(1)} %bitcast.87, f32[256,768]{1,0:T(8,128)S(1)} %fusion.12, f32[256,768]{1,0:T(8,128)S(1)} %fusion.6), kind=kOutput, calls=%fused_computation.21 | convolution fusion | flops 1613889536 | bytes 14155776 | tf_op jit(solution)/shard_map/dot_general | solution.py:70
  114.6 2.5 %collective-permute-done.28 = bf16[16,4096]{1,0:T(8,128)(2,1)S(1)} collective-permute-done((bf16[16,4096]{1,0:T(8,128)(2,1)S(1)}, bf16[16,4096]{1,0:T(8,128)(2,1)S(1)}, u32[]{:S(2)}, u32[]{:S(2)}) %collective-permute-start.28) | collective-permute-done | bytes 131104 | tf_op jit(solution)/shard_map/ppermute | solution.py:131
  117.0 1.7 %collective-permute-done.29 = bf16[16,4096]{1,0:T(8,128)(2,1)S(1)} collective-permute-done((bf16[16,4096]{1,0:T(8,128)(2,1)S(1)}, bf16[16,4096]{1,0:T(8,128)(2,1)S(1)}, u32[]{:S(2)}, u32[]{:S(2)}) %collective-permute-start.29) | collective-permute-done | bytes 131104 | tf_op jit(solution)/shard_map/ppermute | solution.py:131
  118.8 1.8 %collective-permute-done.30 = bf16[16,4096]{1,0:T(8,128)(2,1)S(1)} collective-permute-done((bf16[16,4096]{1,0:T(8,128)(2,1)S(1)}, bf16[16,4096]{1,0:T(8,128)(2,1)S(1)}, u32[]{:S(2)}, u32[]{:S(2)}) %collective-permute-start.30) | collective-permute-done | bytes 131104 | tf_op jit(solution)/shard_map/ppermute | solution.py:131
  120.8 1.8 %collective-permute-start.31 = (bf16[32,4096]{1,0:T(8,128)(2,1)S(1)}, bf16[32,4096]{1,0:T(8,128)(2,1)S(1)}, u32[]{:S(2)}, u32[]{:S(2)}) collective-permute-start(bf16[32,4096]{1,0:T(8,128)(2,1)S(1)} %convolution_convert_fusion.1), channel_id=1, source_target_pairs={{8,0},{9,1},{10,2},{11,3},{12,4},{13,5},{14,6},{15,7},{24,8},{25,9... | collective-permute-start | bytes 786440 | tf_op jit(solution)/shard_map/ppermute | solution.py:137
  130.7 1.6 %collective-permute-done.26 = bf16[16,4096]{1,0:T(8,128)(2,1)S(1)} collective-permute-done((bf16[16,4096]{1,0:T(8,128)(2,1)S(1)}, bf16[16,4096]{1,0:T(8,128)(2,1)S(1)}, u32[]{:S(2)}, u32[]{:S(2)}) %collective-permute-start.26) | collective-permute-done | bytes 131104 | tf_op jit(solution)/shard_map/ppermute | solution.py:131
  132.5 2.4 %collective-permute-start.32 = (bf16[32,4096]{1,0:T(8,128)(2,1)S(1)}, bf16[32,4096]{1,0:T(8,128)(2,1)S(1)}, u32[]{:S(2)}, u32[]{:S(2)}) collective-permute-start(bf16[32,4096]{1,0:T(8,128)(2,1)S(1)} %fusion.23), channel_id=1, source_target_pairs={{8,0},{9,1},{10,2},{11,3},{12,4},{13,5},{14,6},{15,7},{24,8},{25,9... | collective-permute-start | bytes 786440 | tf_op jit(solution)/shard_map/ppermute | solution.py:137
  136.9 1.7 %collective-permute-start.20 = (bf16[16,4096]{1,0:T(8,128)(2,1)S(1)}, bf16[16,4096]{1,0:T(8,128)(2,1)S(1)}, u32[]{:S(2)}, u32[]{:S(2)}) collective-permute-start(bf16[16,4096]{1,0:T(8,128)(2,1)S(1)} %get-tuple-element.54), channel_id=1, source_target_pairs={{0,6},{1,7},{2,4},{3,5},{4,2},{5,3},{6,0},{7,1},{8,14},{9,15},{10,... | collective-permute-start | bytes 393224 | tf_op jit(solution)/shard_map/ppermute | solution.py:131
  140.0 2.7 %collective-permute-start.33 = (bf16[32,4096]{1,0:T(8,128)(2,1)S(1)}, bf16[32,4096]{1,0:T(8,128)(2,1)S(1)}, u32[]{:S(2)}, u32[]{:S(2)}) collective-permute-start(bf16[32,4096]{1,0:T(8,128)(2,1)S(1)} %fusion.22), channel_id=1, source_target_pairs={{8,0},{9,1},{10,2},{11,3},{12,4},{13,5},{14,6},{15,7},{24,8},{25,9... | collective-permute-start | bytes 786440 | tf_op jit(solution)/shard_map/ppermute | solution.py:137
  142.7 4.6 %fusion.14 = bf16[1,768,4096]{2,1,0:T(8,128)(2,1)} fusion(bf16[256,8192]{1,0:T(8,128)(2,1)S(1)} %constant_dynamic-update-slice_fusion, f32[256,768]{1,0:T(8,128)S(1)} %fusion.10, f32[256,768]{1,0:T(8,128)S(1)} %fusion.6), kind=kOutput, calls=%fused_computation.19 | convolution fusion | flops 1614938112 | bytes 9961472 | tf_op jit(solution)/shard_map/dot_general | solution.py:64
  (125 shorter events, 40.9 us)
Async XLA Ops:
  5.4 16.2 %collective-permute-start.3 = (bf16[32,8320]{1,0:T(8,128)(2,1)S(1)}, bf16[32,8320]{1,0:T(8,128)(2,1)S(1)}, u32[]{:S(2)}, u32[]{:S(2)}) collective-permute-start(bf16[32,8320]{1,0:T(8,128)(2,1)S(1)} %pad_maximum_fusion), channel_id=1, source_target_pairs={{0,8},{1,9},{2,10},{3,11},{4,12},{5,13},{6,14},{7,15},{8,24},{9,25... | collective-permute-start | bytes 1597448 | tf_op jit(solution)/shard_map/ppermute | solution.py:100
  21.5 14.2 %collective-permute-start.7 = (bf16[32,8320]{1,0:T(8,128)(2,1)S(1)}, bf16[32,8320]{1,0:T(8,128)(2,1)S(1)}, u32[]{:S(2)}, u32[]{:S(2)}) collective-permute-start(bf16[32,8320]{1,0:T(8,128)(2,1)S(1)} %collective-permute-done.3), channel_id=1, source_target_pairs={{0,8},{1,9},{2,10},{3,11},{4,12},{5,13},{6,14},{7,15},{8,24},{9,25... | collective-permute-start | bytes 1597448 | tf_op jit(solution)/shard_map/ppermute | solution.py:100
  35.7 13.3 %collective-permute-start.11 = (bf16[32,8320]{1,0:T(8,128)(2,1)S(1)}, bf16[32,8320]{1,0:T(8,128)(2,1)S(1)}, u32[]{:S(2)}, u32[]{:S(2)}) collective-permute-start(bf16[32,8320]{1,0:T(8,128)(2,1)S(1)} %collective-permute-done.7), channel_id=1, source_target_pairs={{0,8},{1,9},{2,10},{3,11},{4,12},{5,13},{6,14},{7,15},{8,24},{9,25... | collective-permute-start | bytes 1597448 | tf_op jit(solution)/shard_map/ppermute | solution.py:100
  51.3 9.3 %collective-permute-start = (bf16[16,8192]{1,0:T(8,128)(2,1)S(1)}, bf16[16,8192]{1,0:T(8,128)(2,1)S(1)}, u32[]{:S(2)}, u32[]{:S(2)}) collective-permute-start(bf16[16,8192]{1,0:T(8,128)(2,1)S(1)} %get-tuple-element.36), channel_id=1, source_target_pairs={{0,2},{1,3},{2,0},{3,1},{4,6},{5,7},{6,4},{7,5},{8,10},{9,11},{10,... | collective-permute-start | bytes 786440 | tf_op jit(solution)/shard_map/ppermute | solution.py:110
  52.3 14.6 %collective-permute-start.1 = (bf16[16,8192]{1,0:T(8,128)(2,1)S(1)}, bf16[16,8192]{1,0:T(8,128)(2,1)S(1)}, u32[]{:S(2)}, u32[]{:S(2)}) collective-permute-start(bf16[16,8192]{1,0:T(8,128)(2,1)S(1)} %get-tuple-element.35), channel_id=1, source_target_pairs={{0,4},{1,5},{2,6},{3,7},{4,0},{5,1},{6,2},{7,3},{8,12},{9,13},{10,... | collective-permute-start | bytes 786440 | tf_op jit(solution)/shard_map/ppermute | solution.py:110
  53.8 13.1 %collective-permute-start.2 = (bf16[16,8192]{1,0:T(8,128)(2,1)S(1)}, bf16[16,8192]{1,0:T(8,128)(2,1)S(1)}, u32[]{:S(2)}, u32[]{:S(2)}) collective-permute-start(bf16[16,8192]{1,0:T(8,128)(2,1)S(1)} %get-tuple-element.34), channel_id=1, source_target_pairs={{0,6},{1,7},{2,4},{3,5},{4,2},{5,3},{6,0},{7,1},{8,14},{9,15},{10,... | collective-permute-start | bytes 786440 | tf_op jit(solution)/shard_map/ppermute | solution.py:110
  56.5 15.4 %collective-permute-start.4 = (bf16[16,8192]{1,0:T(8,128)(2,1)S(1)}, bf16[16,8192]{1,0:T(8,128)(2,1)S(1)}, u32[]{:S(2)}, u32[]{:S(2)}) collective-permute-start(bf16[16,8192]{1,0:T(8,128)(2,1)S(1)} %get-tuple-element.33), channel_id=1, source_target_pairs={{0,2},{1,3},{2,0},{3,1},{4,6},{5,7},{6,4},{7,5},{8,10},{9,11},{10,... | collective-permute-start | bytes 786440 | tf_op jit(solution)/shard_map/ppermute | solution.py:110
  57.4 18.5 %collective-permute-start.5 = (bf16[16,8192]{1,0:T(8,128)(2,1)S(1)}, bf16[16,8192]{1,0:T(8,128)(2,1)S(1)}, u32[]{:S(2)}, u32[]{:S(2)}) collective-permute-start(bf16[16,8192]{1,0:T(8,128)(2,1)S(1)} %get-tuple-element.32), channel_id=1, source_target_pairs={{0,4},{1,5},{2,6},{3,7},{4,0},{5,1},{6,2},{7,3},{8,12},{9,13},{10,... | collective-permute-start | bytes 786440 | tf_op jit(solution)/shard_map/ppermute | solution.py:110
  60.6 17.4 %collective-permute-start.6 = (bf16[16,8192]{1,0:T(8,128)(2,1)S(1)}, bf16[16,8192]{1,0:T(8,128)(2,1)S(1)}, u32[]{:S(2)}, u32[]{:S(2)}) collective-permute-start(bf16[16,8192]{1,0:T(8,128)(2,1)S(1)} %get-tuple-element.31), channel_id=1, source_target_pairs={{0,6},{1,7},{2,4},{3,5},{4,2},{5,3},{6,0},{7,1},{8,14},{9,15},{10,... | collective-permute-start | bytes 786440 | tf_op jit(solution)/shard_map/ppermute | solution.py:110
  66.9 16.3 %collective-permute-start.8 = (bf16[16,8192]{1,0:T(8,128)(2,1)S(1)}, bf16[16,8192]{1,0:T(8,128)(2,1)S(1)}, u32[]{:S(2)}, u32[]{:S(2)}) collective-permute-start(bf16[16,8192]{1,0:T(8,128)(2,1)S(1)} %get-tuple-element.30), channel_id=1, source_target_pairs={{0,2},{1,3},{2,0},{3,1},{4,6},{5,7},{6,4},{7,5},{8,10},{9,11},{10,... | collective-permute-start | bytes 786440 | tf_op jit(solution)/shard_map/ppermute | solution.py:110
  66.9 20.2 %collective-permute-start.9 = (bf16[16,8192]{1,0:T(8,128)(2,1)S(1)}, bf16[16,8192]{1,0:T(8,128)(2,1)S(1)}, u32[]{:S(2)}, u32[]{:S(2)}) collective-permute-start(bf16[16,8192]{1,0:T(8,128)(2,1)S(1)} %get-tuple-element.29), channel_id=1, source_target_pairs={{0,4},{1,5},{2,6},{3,7},{4,0},{5,1},{6,2},{7,3},{8,12},{9,13},{10,... | collective-permute-start | bytes 786440 | tf_op jit(solution)/shard_map/ppermute | solution.py:110
  71.9 17.4 %collective-permute-start.10 = (bf16[16,8192]{1,0:T(8,128)(2,1)S(1)}, bf16[16,8192]{1,0:T(8,128)(2,1)S(1)}, u32[]{:S(2)}, u32[]{:S(2)}) collective-permute-start(bf16[16,8192]{1,0:T(8,128)(2,1)S(1)} %get-tuple-element.28), channel_id=1, source_target_pairs={{0,6},{1,7},{2,4},{3,5},{4,2},{5,3},{6,0},{7,1},{8,14},{9,15},{10,... | collective-permute-start | bytes 786440 | tf_op jit(solution)/shard_map/ppermute | solution.py:110
  75.9 17.8 %collective-permute-start.12 = (bf16[16,8192]{1,0:T(8,128)(2,1)S(1)}, bf16[16,8192]{1,0:T(8,128)(2,1)S(1)}, u32[]{:S(2)}, u32[]{:S(2)}) collective-permute-start(bf16[16,8192]{1,0:T(8,128)(2,1)S(1)} %get-tuple-element.27), channel_id=1, source_target_pairs={{0,2},{1,3},{2,0},{3,1},{4,6},{5,7},{6,4},{7,5},{8,10},{9,11},{10,... | collective-permute-start | bytes 786440 | tf_op jit(solution)/shard_map/ppermute | solution.py:110
  78.0 17.8 %collective-permute-start.13 = (bf16[16,8192]{1,0:T(8,128)(2,1)S(1)}, bf16[16,8192]{1,0:T(8,128)(2,1)S(1)}, u32[]{:S(2)}, u32[]{:S(2)}) collective-permute-start(bf16[16,8192]{1,0:T(8,128)(2,1)S(1)} %get-tuple-element.26), channel_id=1, source_target_pairs={{0,4},{1,5},{2,6},{3,7},{4,0},{5,1},{6,2},{7,3},{8,12},{9,13},{10,... | collective-permute-start | bytes 786440 | tf_op jit(solution)/shard_map/ppermute | solution.py:110
  83.2 13.5 %collective-permute-start.14 = (bf16[16,8192]{1,0:T(8,128)(2,1)S(1)}, bf16[16,8192]{1,0:T(8,128)(2,1)S(1)}, u32[]{:S(2)}, u32[]{:S(2)}) collective-permute-start(bf16[16,8192]{1,0:T(8,128)(2,1)S(1)} %get-tuple-element.25), channel_id=1, source_target_pairs={{0,6},{1,7},{2,4},{3,5},{4,2},{5,3},{6,0},{7,1},{8,14},{9,15},{10,... | collective-permute-start | bytes 786440 | tf_op jit(solution)/shard_map/ppermute | solution.py:110
  89.3 7.5 %collective-permute-start.15 = (bf16[96,8192]{1,0:T(8,128)(2,1)S(1)}, bf16[96,8192]{1,0:T(8,128)(2,1)S(1)}, u32[]{:S(2)}, u32[]{:S(2)}) collective-permute-start(bf16[96,8192]{1,0:T(8,128)(2,1)S(1)} %get-tuple-element.62), channel_id=1, source_target_pairs={{0,1},{1,0},{2,3},{3,2},{4,5},{5,4},{6,7},{7,6},{8,9},{9,8},{10,11... | collective-permute-start | bytes 4718600 | tf_op jit(solution)/shard_map/ppermute | solution.py:115
  109.6 12.9 %collective-permute-start.17 = (bf16[3,4,8,4096]{3,2,1,0:T(8,128)(2,1)S(1)}, bf16[3,4,8,4096]{3,2,1,0:T(8,128)(2,1)S(1)}, u32[]{:S(2)}, u32[]{:S(2)}) collective-permute-start(bf16[3,4,8,4096]{3,2,1,0:T(8,128)(2,1)S(1)} %bitcast.90), channel_id=1, source_target_pairs={{0,1},{1,0},{2,3},{3,2},{4,5},{5,4},{6,7},{7,6},{8,9},{9,8},{10,11... | collective-permute-start | bytes 2359304 | tf_op jit(solution)/shard_map/ppermute | solution.py:126
  111.0 6.0 %collective-permute-start.28 = (bf16[16,4096]{1,0:T(8,128)(2,1)S(1)}, bf16[16,4096]{1,0:T(8,128)(2,1)S(1)}, u32[]{:S(2)}, u32[]{:S(2)}) collective-permute-start(bf16[16,4096]{1,0:T(8,128)(2,1)S(1)} %get-tuple-element.41), channel_id=1, source_target_pairs={{0,2},{1,3},{2,0},{3,1},{4,6},{5,7},{6,4},{7,5},{8,10},{9,11},{10,... | collective-permute-start | bytes 393224 | tf_op jit(solution)/shard_map/ppermute | solution.py:131
  112.5 6.3 %collective-permute-start.29 = (bf16[16,4096]{1,0:T(8,128)(2,1)S(1)}, bf16[16,4096]{1,0:T(8,128)(2,1)S(1)}, u32[]{:S(2)}, u32[]{:S(2)}) collective-permute-start(bf16[16,4096]{1,0:T(8,128)(2,1)S(1)} %get-tuple-element.43), channel_id=1, source_target_pairs={{0,4},{1,5},{2,6},{3,7},{4,0},{5,1},{6,2},{7,3},{8,12},{9,13},{10,... | collective-permute-start | bytes 393224 | tf_op jit(solution)/shard_map/ppermute | solution.py:131
  113.1 7.4 %collective-permute-start.30 = (bf16[16,4096]{1,0:T(8,128)(2,1)S(1)}, bf16[16,4096]{1,0:T(8,128)(2,1)S(1)}, u32[]{:S(2)}, u32[]{:S(2)}) collective-permute-start(bf16[16,4096]{1,0:T(8,128)(2,1)S(1)} %get-tuple-element.42), channel_id=1, source_target_pairs={{0,6},{1,7},{2,4},{3,5},{4,2},{5,3},{6,0},{7,1},{8,14},{9,15},{10,... | collective-permute-start | bytes 393224 | tf_op jit(solution)/shard_map/ppermute | solution.py:131
  120.8 7.5 %collective-permute-start.31 = (bf16[32,4096]{1,0:T(8,128)(2,1)S(1)}, bf16[32,4096]{1,0:T(8,128)(2,1)S(1)}, u32[]{:S(2)}, u32[]{:S(2)}) collective-permute-start(bf16[32,4096]{1,0:T(8,128)(2,1)S(1)} %convolution_convert_fusion.1), channel_id=1, source_target_pairs={{8,0},{9,1},{10,2},{11,3},{12,4},{13,5},{14,6},{15,7},{24,8},{25,9... | collective-permute-start | bytes 786440 | tf_op jit(solution)/shard_map/ppermute | solution.py:137
  122.7 6.5 %collective-permute-start.24 = (bf16[16,4096]{1,0:T(8,128)(2,1)S(1)}, bf16[16,4096]{1,0:T(8,128)(2,1)S(1)}, u32[]{:S(2)}, u32[]{:S(2)}) collective-permute-start(bf16[16,4096]{1,0:T(8,128)(2,1)S(1)} %get-tuple-element.45), channel_id=1, source_target_pairs={{0,2},{1,3},{2,0},{3,1},{4,6},{5,7},{6,4},{7,5},{8,10},{9,11},{10,... | collective-permute-start | bytes 393224 | tf_op jit(solution)/shard_map/ppermute | solution.py:131
  123.4 7.3 %collective-permute-start.25 = (bf16[16,4096]{1,0:T(8,128)(2,1)S(1)}, bf16[16,4096]{1,0:T(8,128)(2,1)S(1)}, u32[]{:S(2)}, u32[]{:S(2)}) collective-permute-start(bf16[16,4096]{1,0:T(8,128)(2,1)S(1)} %get-tuple-element.47), channel_id=1, source_target_pairs={{0,4},{1,5},{2,6},{3,7},{4,0},{5,1},{6,2},{7,3},{8,12},{9,13},{10,... | collective-permute-start | bytes 393224 | tf_op jit(solution)/shard_map/ppermute | solution.py:131
  124.9 7.4 %collective-permute-start.26 = (bf16[16,4096]{1,0:T(8,128)(2,1)S(1)}, bf16[16,4096]{1,0:T(8,128)(2,1)S(1)}, u32[]{:S(2)}, u32[]{:S(2)}) collective-permute-start(bf16[16,4096]{1,0:T(8,128)(2,1)S(1)} %get-tuple-element.46), channel_id=1, source_target_pairs={{0,6},{1,7},{2,4},{3,5},{4,2},{5,3},{6,0},{7,1},{8,14},{9,15},{10,... | collective-permute-start | bytes 393224 | tf_op jit(solution)/shard_map/ppermute | solution.py:131
  126.2 10.1 %collective-permute-start.21 = (bf16[16,4096]{1,0:T(8,128)(2,1)S(1)}, bf16[16,4096]{1,0:T(8,128)(2,1)S(1)}, u32[]{:S(2)}, u32[]{:S(2)}) collective-permute-start(bf16[16,4096]{1,0:T(8,128)(2,1)S(1)} %get-tuple-element.49), channel_id=1, source_target_pairs={{0,2},{1,3},{2,0},{3,1},{4,6},{5,7},{6,4},{7,5},{8,10},{9,11},{10,... | collective-permute-start | bytes 393224 | tf_op jit(solution)/shard_map/ppermute | solution.py:131
  128.3 8.6 %collective-permute-start.22 = (bf16[16,4096]{1,0:T(8,128)(2,1)S(1)}, bf16[16,4096]{1,0:T(8,128)(2,1)S(1)}, u32[]{:S(2)}, u32[]{:S(2)}) collective-permute-start(bf16[16,4096]{1,0:T(8,128)(2,1)S(1)} %get-tuple-element.51), channel_id=1, source_target_pairs={{0,4},{1,5},{2,6},{3,7},{4,0},{5,1},{6,2},{7,3},{8,12},{9,13},{10,... | collective-permute-start | bytes 393224 | tf_op jit(solution)/shard_map/ppermute | solution.py:131
  129.2 9.4 %collective-permute-start.23 = (bf16[16,4096]{1,0:T(8,128)(2,1)S(1)}, bf16[16,4096]{1,0:T(8,128)(2,1)S(1)}, u32[]{:S(2)}, u32[]{:S(2)}) collective-permute-start(bf16[16,4096]{1,0:T(8,128)(2,1)S(1)} %get-tuple-element.50), channel_id=1, source_target_pairs={{0,6},{1,7},{2,4},{3,5},{4,2},{5,3},{6,0},{7,1},{8,14},{9,15},{10,... | collective-permute-start | bytes 393224 | tf_op jit(solution)/shard_map/ppermute | solution.py:131
  132.5 7.2 %collective-permute-start.32 = (bf16[32,4096]{1,0:T(8,128)(2,1)S(1)}, bf16[32,4096]{1,0:T(8,128)(2,1)S(1)}, u32[]{:S(2)}, u32[]{:S(2)}) collective-permute-start(bf16[32,4096]{1,0:T(8,128)(2,1)S(1)} %fusion.23), channel_id=1, source_target_pairs={{8,0},{9,1},{10,2},{11,3},{12,4},{13,5},{14,6},{15,7},{24,8},{25,9... | collective-permute-start | bytes 786440 | tf_op jit(solution)/shard_map/ppermute | solution.py:137
  135.0 12.3 %collective-permute-start.18 = (bf16[16,4096]{1,0:T(8,128)(2,1)S(1)}, bf16[16,4096]{1,0:T(8,128)(2,1)S(1)}, u32[]{:S(2)}, u32[]{:S(2)}) collective-permute-start(bf16[16,4096]{1,0:T(8,128)(2,1)S(1)} %get-tuple-element.53), channel_id=1, source_target_pairs={{0,2},{1,3},{2,0},{3,1},{4,6},{5,7},{6,4},{7,5},{8,10},{9,11},{10,... | collective-permute-start | bytes 393224 | tf_op jit(solution)/shard_map/ppermute | solution.py:131
  136.4 10.9 %collective-permute-start.19 = (bf16[16,4096]{1,0:T(8,128)(2,1)S(1)}, bf16[16,4096]{1,0:T(8,128)(2,1)S(1)}, u32[]{:S(2)}, u32[]{:S(2)}) collective-permute-start(bf16[16,4096]{1,0:T(8,128)(2,1)S(1)} %get-tuple-element.55), channel_id=1, source_target_pairs={{0,4},{1,5},{2,6},{3,7},{4,0},{5,1},{6,2},{7,3},{8,12},{9,13},{10,... | collective-permute-start | bytes 393224 | tf_op jit(solution)/shard_map/ppermute | solution.py:131
  136.9 10.4 %collective-permute-start.20 = (bf16[16,4096]{1,0:T(8,128)(2,1)S(1)}, bf16[16,4096]{1,0:T(8,128)(2,1)S(1)}, u32[]{:S(2)}, u32[]{:S(2)}) collective-permute-start(bf16[16,4096]{1,0:T(8,128)(2,1)S(1)} %get-tuple-element.54), channel_id=1, source_target_pairs={{0,6},{1,7},{2,4},{3,5},{4,2},{5,3},{6,0},{7,1},{8,14},{9,15},{10,... | collective-permute-start | bytes 393224 | tf_op jit(solution)/shard_map/ppermute | solution.py:131
  140.0 7.3 %collective-permute-start.33 = (bf16[32,4096]{1,0:T(8,128)(2,1)S(1)}, bf16[32,4096]{1,0:T(8,128)(2,1)S(1)}, u32[]{:S(2)}, u32[]{:S(2)}) collective-permute-start(bf16[32,4096]{1,0:T(8,128)(2,1)S(1)} %fusion.22), channel_id=1, source_target_pairs={{8,0},{9,1},{10,2},{11,3},{12,4},{13,5},{14,6},{15,7},{24,8},{25,9... | collective-permute-start | bytes 786440 | tf_op jit(solution)/shard_map/ppermute | solution.py:137
  (9 other events, 91.6 us)

commit v2 on v1

v2 whole, which is shorter than its diff:
```python
import functools

import jax
import jax.numpy as jnp
from jax import lax
from jax.experimental import pallas as pl
from jax.experimental.pallas import tpu as pltpu
from jax.sharding import PartitionSpec as P

AXES = ("node", "local")
BF16 = jnp.bfloat16
F32 = jnp.float32
COLUMNS = 1024
META = 128
NEAR = 2


def device_perms(nodes, per_node):
    depth = nodes // 2
    order = [z for z in range(depth) if z == 0 or z % 2 == 1]
    order += [z for z in reversed(range(depth)) if z not in order]
    follow = {order[i]: order[(i + 1) % depth] for i in range(depth)}

    def flat(z, y, place):
        return (z * 2 + y) * per_node + place

    cells = [(z, y, p) for z in range(depth) for y in range(2) for p in range(per_node)]
    ring = [(flat(z, y, p), flat(follow[z], y, p)) for z, y, p in cells]
    back = [(b, a) for a, b in ring]
    flip_x = [(flat(z, y, p), flat(z, y, p ^ 2)) for z, y, p in cells]
    flip_y = [(flat(z, y, p), flat(z, 1 - y, p)) for z, y, p in cells]
    flip_xy = [(flat(z, y, p), flat(z, 1 - y, p ^ 2)) for z, y, p in cells]
    flip_core = [(flat(z, y, p), flat(z, y, p ^ 1)) for z, y, p in cells]
    return depth, ring, back, (flip_x, flip_y, flip_xy), flip_core


def slot_codes(spot, per_node, capacity):
    rank = lax.broadcasted_iota(jnp.int32, (8 * capacity, 1), 0)
    flip, slot = rank // capacity, rank % capacity
    reach = flip // 4 * per_node + flip % 4
    return ((spot[0] + (spot[1] ^ reach)) * capacity + slot).astype(F32)


def pick_rows(meta, codes, tok, grad, top, outs, pick_ref):
    tok_dev, width = tok.shape
    hit = None
    gate = jnp.zeros(codes.shape, F32)
    for k in range(top):
        same = meta[k : k + 1, :tok_dev] == codes
        value = meta[top + k : top + k + 1, :tok_dev] * 256.0 + meta[2 * top + k : 2 * top + k + 1, :tok_dev]
        gate = gate + jnp.sum(jnp.where(same, value, 0.0), axis=1, keepdims=True)
        hit = same if hit is None else hit | same
    pick = jnp.where(hit, 1.0, 0.0).astype(BF16)
    pick_ref[...] = pick
    scale = gate * (1.0 / 65536.0)
    pair = codes.shape[0] // 4
    for c in range(0, width, COLUMNS):
        cols = slice(c, min(c + COLUMNS, width))
        x = jnp.dot(pick, tok[:, cols], preferred_element_type=F32).astype(BF16)
        dy = (jnp.dot(pick, grad[:, cols], preferred_element_type=F32) * scale).astype(BF16)
        for i, (out_x, out_dy) in enumerate(outs):
            out_x[:, cols] = x[i * pair : (i + 1) * pair]
            out_dy[:, cols] = dy[i * pair : (i + 1) * pair]


def first_kernel(per_node, capacity, experts, spot, *refs):
    far, (*outs, pick_ref, held, codes_ref) = refs[:5], refs[5:12]
    (lists, local, gate, tok, grad), meta, sems = refs[12:17], refs[17], refs[18]
    copies = [pltpu.make_async_copy(a, b, sems.at[i]) for i, (a, b) in enumerate(zip(far, refs[12:17]))]
    for copy in copies:
        copy.start()
    for copy in copies[:3]:
        copy.wait()
    top, tok_dev = local.shape
    width = tok.shape[1]
    place = local[...] // per_node
    group = jnp.zeros_like(place)
    for j in range(lists.shape[0]):
        group = jnp.where(place == j, lists[j : j + 1, :], group)
    expert = group * per_node + local[...] % per_node
    ids = lax.broadcasted_iota(jnp.int32, (experts, tok_dev), 0)
    member = None
    for k in range(top):
        same = ids == expert[k : k + 1, :]
        member = same if member is None else member | same
    rows = lax.broadcasted_iota(jnp.int32, (tok_dev, tok_dev), 0)
    cols = lax.broadcasted_iota(jnp.int32, (tok_dev, tok_dev), 1)
    earlier = jnp.where(rows < cols, 1.0, 0.0).astype(BF16)
    before = jnp.dot(jnp.where(member, 1.0, 0.0).astype(BF16), earlier, preferred_element_type=F32)
    meta[...] = jnp.zeros(meta.shape, F32)
    for k in range(top):
        slot = jnp.sum(jnp.where(ids == expert[k : k + 1, :], before, 0.0), axis=0, keepdims=True)
        code = expert[k : k + 1, :].astype(F32) * capacity + slot
        meta[k : k + 1, :tok_dev] = jnp.where(slot < capacity, code, -1.0)
    meta[top : 2 * top, :tok_dev] = (gate[...] // 256).astype(F32)
    meta[2 * top : 3 * top, :tok_dev] = (gate[...] % 256).astype(F32)
    for copy in copies[3:]:
        copy.wait()
    held[:, :width] = tok[...]
    held[:, width : 2 * width] = grad[...]
    held[:, 2 * width :] = meta[...].astype(BF16)
    codes = slot_codes(spot, per_node, capacity)
    codes_ref[...] = codes
    pick_rows(meta, codes, tok, grad, top, [(out.at[0], out.at[1]) for out in outs], pick_ref)


def next_kernel(top, codes, held, *refs):
    *outs, pick_ref = refs
    width = outs[0].shape[-1]
    meta = held[:, 2 * width :].astype(F32)
    tok, grad = held.at[:, :width], held.at[:, width : 2 * width]
    pairs = list(zip(outs[:4], outs[4:])) if len(outs) == 8 else [(out.at[0], out.at[1]) for out in outs]
    pick_rows(meta, codes[...], tok, grad, top, pairs, pick_ref)


def whole(n):
    return [pl.BlockSpec(memory_space=pltpu.VMEM)] * n


def row_shapes(capacity, tok_dev, width, apart=False):
    shape = (2 * capacity, width)
    rows = [jax.ShapeDtypeStruct(shape, BF16)] * 8 if apart else [jax.ShapeDtypeStruct((2,) + shape, BF16)] * 4
    return rows + [jax.ShapeDtypeStruct((8 * capacity, tok_dev), BF16)]


PARAMS = pltpu.CompilerParams(vmem_limit_bytes=12 * 1024 * 1024)


def first_rows(per_node, capacity, experts, spot, lists, local, gate, tok, grad):
    shape = (tok.shape[0], 2 * tok.shape[1] + META)
    operands = [pltpu.with_memory_space_constraint(a, pltpu.HBM) for a in (lists, local, gate, tok, grad)]
    extra = [jax.ShapeDtypeStruct(shape, BF16), jax.ShapeDtypeStruct((8 * capacity, 1), F32)]
    return pl.pallas_call(
        functools.partial(first_kernel, per_node, capacity, experts),
        in_specs=[pl.BlockSpec(memory_space=pltpu.SMEM)] + [pl.BlockSpec(memory_space=pltpu.HBM)] * 5,
        out_specs=whole(7),
        out_shape=row_shapes(capacity, *tok.shape) + extra,
        scratch_shapes=[pltpu.VMEM(a.shape, a.dtype) for a in (lists, local, gate, tok, grad)]
        + [pltpu.VMEM((tok.shape[0], META), F32), pltpu.SemaphoreType.DMA((5,))],
        compiler_params=PARAMS,
        name="first_rows",
    )(spot, *operands)


def next_rows(top, codes, held, apart):
    shapes = row_shapes(codes.shape[0] // 8, held.shape[0], (held.shape[1] - META) // 2, apart)
    return pl.pallas_call(
        functools.partial(next_kernel, top),
        in_specs=whole(2),
        out_specs=whole(len(shapes)),
        out_shape=shapes,
        compiler_params=PARAMS,
        name="next_rows",
    )(codes, held)


def products(x_rows, w_gate_e, w_up_e):
    gate_act = jnp.dot(x_rows, w_gate_e, preferred_element_type=F32)
    up_act = jnp.dot(x_rows, w_up_e, preferred_element_type=F32)
    return gate_act, up_act


def gradients(gate_act, up_act, dy_rows, w_gate_e, w_up_e, w_down_e):
    last = (((1,), (1,)), ((), ()))
    sig = jax.nn.sigmoid(gate_act)
    hidden = (gate_act * sig * up_act).astype(BF16)
    hidden_grad = lax.dot_general(dy_rows, w_down_e, last, preferred_element_type=F32)
    gate_grad = (hidden_grad * up_act * sig * (1.0 + gate_act * (1.0 - sig))).astype(BF16)
    up_grad = (hidden_grad * gate_act * sig).astype(BF16)
    row_grad = (
        lax.dot_general(gate_grad, w_gate_e, last, preferred_element_type=F32)
        + lax.dot_general(up_grad, w_up_e, last, preferred_element_type=F32)
    ).astype(BF16)
    return hidden, row_grad


def ordered(held, got, w):
    near, far = got[w - 1][1:NEAR], got[w - 2][NEAR:] if w > 1 else []
    held, near, far = lax.optimization_barrier((held, near, far))
    got[w - 1][1:NEAR] = near
    if far:
        got[w - 2][NEAR:] = far
    return held


def body(
    tokens, out_grad, node_lists, expert_local, gate_fixed, gate_weight, up_weight, down_weight
):
    nodes, per_node = lax.axis_size("node"), lax.axis_size("local")
    experts = nodes * per_node
    tok_dev, top = expert_local.shape
    width = tokens.shape[1]
    capacity = tok_dev * top // experts
    depth, ring, back, flips, flip_core = device_perms(nodes, per_node)

    node, place = lax.axis_index("node"), lax.axis_index("local")
    spot = jnp.stack([node // 2 * 2 * per_node, (node % 2) * per_node + place])

    picks, got = [], []
    for w in range(depth - 1):
        if w == 0:
            *chosen, pick, held, codes = first_rows(
                per_node, capacity, experts, spot, node_lists.T, expert_local.T, gate_fixed.T, tokens, out_grad
            )
        else:
            ready = ordered(held, got, w)
            held = ready
            *chosen, pick = next_rows(top, codes, ready, False)
        picks.append(pick)
        got.append([chosen[0]] + [lax.ppermute(c, AXES, flip) for c, flip in zip(chosen[1:], flips)])
        held = lax.ppermute(held, AXES, ring)
    *chosen, pick = next_rows(top, codes, ordered(held, got, depth - 1), True)
    picks.append(pick)
    ends = []
    for part in (chosen[:4], chosen[4:]):
        ends.append([part[0]] + [lax.ppermute(c, AXES, flip) for c, flip in zip(part[1:], flips)])
    most = lax.ppermute(jnp.concatenate([g[:, capacity:] for window in got for g in window], axis=1), AXES, flip_core)

    def gather(i, end):
        rest = lax.ppermute(jnp.concatenate([g[capacity:] for g in end], axis=0), AXES, flip_core)
        own = [g[i, :capacity] for window in got for g in window] + [g[:capacity] for g in end]
        return jnp.concatenate(own + [most[i], rest], axis=0)

    x_rows = gather(0, ends[0])
    gate_act, up_act = products(x_rows, gate_weight[0], up_weight[0])
    gate_act, up_act, ends[1] = lax.optimization_barrier((gate_act, up_act, ends[1]))
    dy_rows = gather(1, ends[1])
    hidden, row_grad = gradients(gate_act, up_act, dy_rows, gate_weight[0], up_weight[0], down_weight[0])

    half = depth * 4 * capacity
    own = row_grad[:half].reshape(depth, 4, capacity, width)
    theirs = row_grad[half:].reshape(depth, 4, capacity, width)
    last = lax.ppermute(theirs[depth - 1], AXES, flip_core)
    rest = lax.ppermute(theirs[: depth - 1], AXES, flip_core)
    came = {}
    for w in reversed(range(depth)):
        both = jnp.concatenate([own[w], last if w == depth - 1 else rest[w]], axis=1)
        came[w] = [both[0]] + [lax.ppermute(both[i + 1], AXES, flip) for i, flip in enumerate(flips)]
    down_local = None
    total = None
    for w in reversed(range(depth)):
        partial = lax.dot_general(
            picks[w], jnp.concatenate(came[w], axis=0), (((0,), (0,)), ((), ())), preferred_element_type=F32
        )
        if total is not None:
            partial = partial + total.astype(F32)
        total = partial.astype(BF16)
        if w == 2:
            total, hidden = lax.optimization_barrier((total, hidden))
            down_local = lax.dot_general(
                hidden, dy_rows, (((0,), (0,)), ((), ())), preferred_element_type=F32
            ).astype(BF16)
        if w:
            if w == 1:
                total, down_local = lax.optimization_barrier((total, down_local))
            if w == 1:
                total, came[w - 1][1:2] = lax.optimization_barrier((total, came[w - 1][1:2]))
            total = lax.ppermute(total, AXES, back)
    return total, down_local[None]


def solution(mesh):
    split = P(AXES)
    return jax.shard_map(
        body, mesh=mesh, in_specs=(split,) * 8, out_specs=(split, split), check_vma=False
    )
```

time: 149 us -> 112 us (0.75)
  waiting for transfers between devices: 76.9 us -> 43.8 us
  matrix products: 19.5 us -> 15.8 us
  Pallas kernels: 0 us -> 3.63 us
  other arithmetic: 3.36 us -> 0.48 us
  local copies, waits for them, and re-layouts: 4.55 us -> 1.75 us
  starting transfers between devices: 42.9 us -> 45.3 us
    ppermute x18 -> x22, waiting for transfers between devices: 66.2 us -> 33.5 us  [the longest x15 18.6 us: body(): lax.ppermute(c, AXES, flip)]
    dot_general x15 -> x10, matrix products: 19.5 us -> 15.8 us  [the longest x1 4.54 us: body(): lax.dot_general(hidden, dy_rows, (((0,), (0,)), ((), ())), preferred_elem...]
    pallas_call x0 -> x4, Pallas kernels: none -> 3.63 us  [the longest x1 2.14 us: first_rows(): pl.pallas_call(functools.partial(first_kernel, per_node, capacity, expert...]
    ppermute x3, waiting for transfers between devices: 2.49 us -> 0.21 us  [body(): total = lax.ppermute(total, AXES, back)]
    ppermute x12, waiting for transfers between devices: 8.19 us -> 10 us  [body(): lax.ppermute(both[i + 1], AXES, flip)]
    unnamed x28 -> x35, local copies, waits for them, and re-layouts: 3.08 us -> 1.4 us
    ppermute x12, starting transfers between devices: 13.3 us -> 15 us  [body(): lax.ppermute(both[i + 1], AXES, flip)]
    ppermute x18 -> x22, starting transfers between devices: 22.1 us -> 22.8 us  [the longest x15 17.8 us: body(): lax.ppermute(c, AXES, flip)]
  transfers between devices with their start and end apart: 34 -> 38, of which waited for: 23 -> 18; matrix products, arithmetic and copies ran while one was open for 6% -> 9% of each run, Pallas kernels for 0% -> 1%
where the time goes in v2:
time: 112 us
  starting transfers between devices  45.3 us (40%)
  waiting for transfers between devices  43.8 us (39%)
  matrix products  15.8 us (14%)
  Pallas kernels  3.63 us (3%)
  local copies, waits for them, and re-layouts  1.75 us (2%)
  between operations  1.22 us (1%)
    ppermute x15, waiting for transfers between devices, body(): lax.ppermute(c, AXES, flip)  18.6 us
    ppermute x15, starting transfers between devices, body(): lax.ppermute(c, AXES, flip)  17.8 us
    ppermute x12, starting transfers between devices, body(): lax.ppermute(both[i + 1], AXES, flip)  15 us
    ppermute x3, waiting for transfers between devices, body(): held = lax.ppermute(held, AXES, ring)  11.2 us
    ppermute x12, waiting for transfers between devices, body(): lax.ppermute(both[i + 1], AXES, flip)  10 us
    ppermute x3, starting transfers between devices, body(): total = lax.ppermute(total, AXES, back)  7.1 us
    dot_general x1, matrix products, body(): lax.dot_general(hidden, dy_rows, (((0,), (0,)), ((), ())), preferred_elem...  4.54 us
    ppermute x3, starting transfers between devices, body(): held = lax.ppermute(held, AXES, ring)  4.49 us
  transfers between devices with their start and end apart: 38, of which 18 were waited for; matrix products, arithmetic and copies ran while one was open for 9% of the time, Pallas kernels for 1%

profile of v2, /device:TPU:0, one launch (start us, length us, event | category | flops | bytes accessed | tf_op | source)
XLA Modules:
  0.0 111.9 jit_solution(7044065335809261188)
XLA Ops:
  0.7 2.1 %first_rows.1 = (bf16[2,16,4096]{2,1,0:T(8,128)(2,1)S(1)}, bf16[2,16,4096]{2,1,0:T(8,128)(2,1)S(1)}, bf16[2,16,4096]{2,1,0:T(8,128)(2,1)S(1)}, bf16[2,16,4096]{2...) custom-call(s32[2]{0:T(128)S(1)} %pad_add_fusion.spot, ...), custom_call_target="tpu_custom_call" | custom-call | tf_op jit(solution)/shard_map/first_rows/pallas_call | solution.py:133
  2.9 3.1 %collective-permute-start = (bf16[32,8320]{1,0:T(8,128)(2,1)S(1)}, bf16[32,8320]{1,0:T(8,128)(2,1)S(1)}, u32[]{:S(2)}, u32[]{:S(2)}) collective-permute-start(bf16[32,8320]{1,0:T(8,128)(2,1)S(1)} %get-tuple-element.52), channel_id=1, source_target_pairs={{0,8},{1,9},{2,10},{3,11},{4,12},{5,13},{6,14},{7,15},{8,24},{9,25... | collective-permute-start | bytes 1597448 | tf_op jit(solution)/shard_map/ppermute | solution.py:211
  7.4 1.5 %collective-permute-start.4 = (bf16[2,16,4096]{2,1,0:T(8,128)(2,1)S(1)}, bf16[2,16,4096]{2,1,0:T(8,128)(2,1)S(1)}, u32[]{:S(2)}, u32[]{:S(2)}) collective-permute-start(bf16[2,16,4096]{2,1,0:T(8,128)(2,1)S(1)} %get-tuple-element.58), channel_id=1, source_target_pairs={{0,4},{1,5},{2,6},{3,7},{4,0},{5,1},{6,2},{7,3},{8,12},{9,13},{10,... | collective-permute-start | bytes 786440 | tf_op jit(solution)/shard_map/ppermute | solution.py:210
  9.5 5.7 %collective-permute-done.1 = bf16[2,16,4096]{2,1,0:T(8,128)(2,1)S(1)} collective-permute-done((bf16[2,16,4096]{2,1,0:T(8,128)(2,1)S(1)}, bf16[2,16,4096]{2,1,0:T(8,128)(2,1)S(1)}, u32[]{:S(2)}, u32[]{:S(2)}) %collective-permute-start.1) | collective-permute-done | bytes 262176 | tf_op jit(solution)/shard_map/ppermute | solution.py:210
  15.2 3.9 %collective-permute-done.held = bf16[32,8320]{1,0:T(8,128)(2,1)S(1)} collective-permute-done((bf16[32,8320]{1,0:T(8,128)(2,1)S(1)}, bf16[32,8320]{1,0:T(8,128)(2,1)S(1)}, u32[]{:S(2)}, u32[]{:S(2)}) %collective-permute-start) | collective-permute-done | bytes 532512 | tf_op jit(solution)/shard_map/ppermute | solution.py:211
  20.4 1.6 %collective-permute-start.3 = (bf16[2,16,4096]{2,1,0:T(8,128)(2,1)S(1)}, bf16[2,16,4096]{2,1,0:T(8,128)(2,1)S(1)}, u32[]{:S(2)}, u32[]{:S(2)}) collective-permute-start(bf16[2,16,4096]{2,1,0:T(8,128)(2,1)S(1)} %get-tuple-element.57), channel_id=1, source_target_pairs={{0,2},{1,3},{2,0},{3,1},{4,6},{5,7},{6,4},{7,5},{8,10},{9,11},{10,... | collective-permute-start | bytes 786440 | tf_op jit(solution)/shard_map/ppermute | solution.py:210
  22.0 1.5 %collective-permute-start.8 = (bf16[2,16,4096]{2,1,0:T(8,128)(2,1)S(1)}, bf16[2,16,4096]{2,1,0:T(8,128)(2,1)S(1)}, u32[]{:S(2)}, u32[]{:S(2)}) collective-permute-start(bf16[2,16,4096]{2,1,0:T(8,128)(2,1)S(1)} %get-tuple-element.66), channel_id=1, source_target_pairs={{0,4},{1,5},{2,6},{3,7},{4,0},{5,1},{6,2},{7,3},{8,12},{9,13},{10,... | collective-permute-start | bytes 786440 | tf_op jit(solution)/shard_map/ppermute | solution.py:210
  24.1 5.6 %collective-permute-done.3 = bf16[2,16,4096]{2,1,0:T(8,128)(2,1)S(1)} collective-permute-done((bf16[2,16,4096]{2,1,0:T(8,128)(2,1)S(1)}, bf16[2,16,4096]{2,1,0:T(8,128)(2,1)S(1)}, u32[]{:S(2)}, u32[]{:S(2)}) %collective-permute-start.3) | collective-permute-done | bytes 262176 | tf_op jit(solution)/shard_map/ppermute | solution.py:210
  29.7 3.5 %collective-permute-done.2.held = bf16[32,8320]{1,0:T(8,128)(2,1)S(1)} collective-permute-done((bf16[32,8320]{1,0:T(8,128)(2,1)S(1)}, bf16[32,8320]{1,0:T(8,128)(2,1)S(1)}, u32[]{:S(2)}, u32[]{:S(2)}) %collective-permute-start.2) | collective-permute-done | bytes 532512 | tf_op jit(solution)/shard_map/ppermute | solution.py:211
  35.8 1.6 %collective-permute-start.10 = (bf16[2,16,4096]{2,1,0:T(8,128)(2,1)S(1)}, bf16[2,16,4096]{2,1,0:T(8,128)(2,1)S(1)}, u32[]{:S(2)}, u32[]{:S(2)}) collective-permute-start(bf16[2,16,4096]{2,1,0:T(8,128)(2,1)S(1)} %get-tuple-element.72), channel_id=1, source_target_pairs={{0,4},{1,5},{2,6},{3,7},{4,0},{5,1},{6,2},{7,3},{8,12},{9,13},{10,... | collective-permute-start | bytes 786440 | tf_op jit(solution)/shard_map/ppermute | solution.py:210
  38.0 5.2 %collective-permute-done.7 = bf16[2,16,4096]{2,1,0:T(8,128)(2,1)S(1)} collective-permute-done((bf16[2,16,4096]{2,1,0:T(8,128)(2,1)S(1)}, bf16[2,16,4096]{2,1,0:T(8,128)(2,1)S(1)}, u32[]{:S(2)}, u32[]{:S(2)}) %collective-permute-start.7) | collective-permute-done | bytes 262176 | tf_op jit(solution)/shard_map/ppermute | solution.py:210
  43.3 3.8 %collective-permute-done.6.held = bf16[32,8320]{1,0:T(8,128)(2,1)S(1)} collective-permute-done((bf16[32,8320]{1,0:T(8,128)(2,1)S(1)}, bf16[32,8320]{1,0:T(8,128)(2,1)S(1)}, u32[]{:S(2)}, u32[]{:S(2)}) %collective-permute-start.6) | collective-permute-done | bytes 532512 | tf_op jit(solution)/shard_map/ppermute | solution.py:211
  48.5 1.5 %collective-permute-start.13 = (bf16[16,4096]{1,0:T(8,128)(2,1)S(1)}, bf16[16,4096]{1,0:T(8,128)(2,1)S(1)}, u32[]{:S(2)}, u32[]{:S(2)}) collective-permute-start(bf16[16,4096]{1,0:T(8,128)(2,1)S(1)} %get-tuple-element.77), channel_id=1, source_target_pairs={{0,4},{1,5},{2,6},{3,7},{4,0},{5,1},{6,2},{7,3},{8,12},{9,13},{10,... | collective-permute-start | bytes 393224 | tf_op jit(solution)/shard_map/ppermute | solution.py:216
  55.2 1.9 %collective-permute-done.14 = bf16[16,4096]{1,0:T(8,128)(2,1)S(1)} collective-permute-done((bf16[16,4096]{1,0:T(8,128)(2,1)S(1)}, bf16[16,4096]{1,0:T(8,128)(2,1)S(1)}, u32[]{:S(2)}, u32[]{:S(2)}) %collective-permute-start.14) | collective-permute-done | bytes 131104 | tf_op jit(solution)/shard_map/ppermute | solution.py:216
  58.8 1.8 %fusion.4 = f32[256,768]{1,0:T(8,128)S(1)} fusion(bf16[256,4096]{1,0:T(8,128)(2,1)S(1)} %constant_dynamic-update-slice_fusion, bf16[1,4096,768]{2,1,0:T(8,128)(2,1)S(1)} %copy-done), kind=kOutput, calls=%fused_computation.5 | convolution fusion | flops 1610612736 | bytes 9175040 | tf_op jit(solution)/shard_map/dot_general | solution.py:159
  61.6 1.8 %fusion.8 = f32[256,768]{1,0:T(8,128)S(1)} fusion(bf16[256,4096]{1,0:T(8,128)(2,1)S(1)} %constant_dynamic-update-slice_fusion, bf16[1,4096,768]{2,1,0:T(8,128)(2,1)S(1)} %bitcast.146), kind=kOutput, calls=%fused_computation.9 | convolution fusion | flops 1610612736 | bytes 9175040 | tf_op jit(solution)/shard_map/dot_general | solution.py:158
  65.2 2.1 %fusion = f32[256,768]{1,0:T(8,128)S(1)} fusion(bf16[256,4096]{1,0:T(8,128)(2,1)S(1)} %constant_dynamic-update-slice_fusion.17, bf16[1,768,4096]{2,1,0:T(8,128)(2,1)S(1)} %bitcast.153), kind=kOutput, calls=%fused_computation.1 | convolution fusion | flops 1610612736 | bytes 9175040 | tf_op jit(solution)/shard_map/dot_general | solution.py:167
  67.3 1.9 %fusion.2 = f32[256,4096]{1,0:T(8,128)S(1)} fusion(bf16[1,4096,768]{2,1,0:T(8,128)(2,1)S(1)} %copy-done, f32[256,768]{1,0:T(8,128)S(1)} %fusion, f32[256,768]{1,0:T(8,128)S(1)} %fusion.8), kind=kOutput, calls=%fused_computation.3 | convolution fusion | flops 1611792384 | bytes 12058624 | tf_op jit(solution)/shard_map/dot_general | solution.py:172
  69.1 2.0 %fusion.13 = bf16[256,4096]{1,0:T(8,128)(2,1)S(1)} fusion(f32[256,4096]{1,0:T(8,128)S(1)} %fusion.2, bf16[1,4096,768]{2,1,0:T(8,128)(2,1)S(1)} %bitcast.146, f32[256,768]{1,0:T(8,128)S(1)} %fusion.8, f32[256,768]{1,0:T(8,128)S(1)} %fusion, f32[256,768]{1,0:T(8,128)S(1)} %fusion.4), kind=kOutput, calls=%fused_computation.12 | convolution fusion | flops 1614675968 | bytes 14942208 | tf_op jit(solution)/shard_map/dot_general | solution.py:171
  74.2 2.2 %collective-permute-start.31 = (bf16[16,4096]{1,0:T(8,128)(2,1)S(1)}, bf16[16,4096]{1,0:T(8,128)(2,1)S(1)}, u32[]{:S(2)}, u32[]{:S(2)}) collective-permute-start(bf16[16,4096]{1,0:T(8,128)(2,1)S(1)} %get-tuple-element.112), channel_id=1, source_target_pairs={{0,6},{1,7},{2,4},{3,5},{4,2},{5,3},{6,0},{7,1},{8,14},{9,15},{10,... | collective-permute-start | bytes 393224 | tf_op jit(solution)/shard_map/ppermute | solution.py:238
  76.7 2.6 %collective-permute-done.29 = bf16[16,4096]{1,0:T(8,128)(2,1)S(1)} collective-permute-done((bf16[16,4096]{1,0:T(8,128)(2,1)S(1)}, bf16[16,4096]{1,0:T(8,128)(2,1)S(1)}, u32[]{:S(2)}, u32[]{:S(2)}) %collective-permute-start.29) | collective-permute-done | bytes 131104 | tf_op jit(solution)/shard_map/ppermute | solution.py:238
  79.3 2.1 %collective-permute-done.30 = bf16[16,4096]{1,0:T(8,128)(2,1)S(1)} collective-permute-done((bf16[16,4096]{1,0:T(8,128)(2,1)S(1)}, bf16[16,4096]{1,0:T(8,128)(2,1)S(1)}, u32[]{:S(2)}, u32[]{:S(2)}) %collective-permute-start.30) | collective-permute-done | bytes 131104 | tf_op jit(solution)/shard_map/ppermute | solution.py:238
  81.6 1.7 %collective-permute-start.32 = (bf16[32,4096]{1,0:T(8,128)(2,1)S(1)}, bf16[32,4096]{1,0:T(8,128)(2,1)S(1)}, u32[]{:S(2)}, u32[]{:S(2)}) collective-permute-start(bf16[32,4096]{1,0:T(8,128)(2,1)S(1)} %convolution_convert_fusion.1), channel_id=1, source_target_pairs={{8,0},{9,1},{10,2},{11,3},{12,4},{13,5},{14,6},{15,7},{24,8},{25,9... | collective-permute-start | bytes 786440 | tf_op jit(solution)/shard_map/ppermute | solution.py:258
  83.4 1.7 %collective-permute-start.25 = (bf16[16,4096]{1,0:T(8,128)(2,1)S(1)}, bf16[16,4096]{1,0:T(8,128)(2,1)S(1)}, u32[]{:S(2)}, u32[]{:S(2)}) collective-permute-start(bf16[16,4096]{1,0:T(8,128)(2,1)S(1)} %get-tuple-element.115), channel_id=1, source_target_pairs={{0,2},{1,3},{2,0},{3,1},{4,6},{5,7},{6,4},{7,5},{8,10},{9,11},{10,... | collective-permute-start | bytes 393224 | tf_op jit(solution)/shard_map/ppermute | solution.py:238
  87.0 1.7 %collective-permute-start.22 = (bf16[16,4096]{1,0:T(8,128)(2,1)S(1)}, bf16[16,4096]{1,0:T(8,128)(2,1)S(1)}, u32[]{:S(2)}, u32[]{:S(2)}) collective-permute-start(bf16[16,4096]{1,0:T(8,128)(2,1)S(1)} %get-tuple-element.119), channel_id=1, source_target_pairs={{0,2},{1,3},{2,0},{3,1},{4,6},{5,7},{6,4},{7,5},{8,10},{9,11},{10,... | collective-permute-start | bytes 393224 | tf_op jit(solution)/shard_map/ppermute | solution.py:238
  89.0 1.6 %collective-permute-start.23 = (bf16[16,4096]{1,0:T(8,128)(2,1)S(1)}, bf16[16,4096]{1,0:T(8,128)(2,1)S(1)}, u32[]{:S(2)}, u32[]{:S(2)}) collective-permute-start(bf16[16,4096]{1,0:T(8,128)(2,1)S(1)} %get-tuple-element.121), channel_id=1, source_target_pairs={{0,4},{1,5},{2,6},{3,7},{4,0},{5,1},{6,2},{7,3},{8,12},{9,13},{10,... | collective-permute-start | bytes 393224 | tf_op jit(solution)/shard_map/ppermute | solution.py:238
  91.7 1.7 %collective-permute-start.34 = (bf16[16,4096]{1,0:T(8,128)(2,1)S(1)}, bf16[16,4096]{1,0:T(8,128)(2,1)S(1)}, u32[]{:S(2)}, u32[]{:S(2)}) collective-permute-start(bf16[16,4096]{1,0:T(8,128)(2,1)S(1)} %get-tuple-element.107), channel_id=1, source_target_pairs={{0,2},{1,3},{2,0},{3,1},{4,6},{5,7},{6,4},{7,5},{8,10},{9,11},{10,... | collective-permute-start | bytes 393224 | tf_op jit(solution)/shard_map/ppermute | solution.py:238
  93.9 2.7 %collective-permute-start.33 = (bf16[32,4096]{1,0:T(8,128)(2,1)S(1)}, bf16[32,4096]{1,0:T(8,128)(2,1)S(1)}, u32[]{:S(2)}, u32[]{:S(2)}) collective-permute-start(bf16[32,4096]{1,0:T(8,128)(2,1)S(1)} %fusion.17), channel_id=1, source_target_pairs={{8,0},{9,1},{10,2},{11,3},{12,4},{13,5},{14,6},{15,7},{24,8},{25,9... | collective-permute-start | bytes 786440 | tf_op jit(solution)/shard_map/ppermute | solution.py:258
  96.6 4.5 %convolution_convert_fusion = bf16[768,4096]{1,0:T(8,128)(2,1)} fusion(bf16[256,768]{1,0:T(8,128)(2,1)S(1)} %multiply_convert_fusion, bf16[256,4096]{1,0:T(8,128)(2,1)S(1)} %constant_dynamic-update-slice_fusion.17), kind=kOutput, calls=%fused_computation | convolution fusion | flops 1613758464 | bytes 8781824 | tf_op jit(solution)/shard_map/dot_general | solution.py:250
  101.4 2.8 %collective-permute-start.37 = (bf16[32,4096]{1,0:T(8,128)(2,1)S(1)}, bf16[32,4096]{1,0:T(8,128)(2,1)S(1)}, u32[]{:S(2)}, u32[]{:S(2)}) collective-permute-start(bf16[32,4096]{1,0:T(8,128)(2,1)S(1)} %fusion.16), channel_id=1, source_target_pairs={{8,0},{9,1},{10,2},{11,3},{12,4},{13,5},{14,6},{15,7},{24,8},{25,9... | collective-permute-start | bytes 786440 | tf_op jit(solution)/shard_map/ppermute | solution.py:258
  106.2 2.9 %collective-permute-done.35 = bf16[16,4096]{1,0:T(8,128)(2,1)S(1)} collective-permute-done((bf16[16,4096]{1,0:T(8,128)(2,1)S(1)}, bf16[16,4096]{1,0:T(8,128)(2,1)S(1)}, u32[]{:S(2)}, u32[]{:S(2)}) %collective-permute-start.35) | collective-permute-done | bytes 131104 | tf_op jit(solution)/shard_map/ppermute | solution.py:238
  109.1 1.8 %collective-permute-done.36 = bf16[16,4096]{1,0:T(8,128)(2,1)S(1)} collective-permute-done((bf16[16,4096]{1,0:T(8,128)(2,1)S(1)}, bf16[16,4096]{1,0:T(8,128)(2,1)S(1)}, u32[]{:S(2)}, u32[]{:S(2)}) %collective-permute-start.36) | collective-permute-done | bytes 131104 | tf_op jit(solution)/shard_map/ppermute | solution.py:238
  (117 shorter events, 28.5 us)
Async XLA Ops:
  2.9 16.2 %collective-permute-start = (bf16[32,8320]{1,0:T(8,128)(2,1)S(1)}, bf16[32,8320]{1,0:T(8,128)(2,1)S(1)}, u32[]{:S(2)}, u32[]{:S(2)}) collective-permute-start(bf16[32,8320]{1,0:T(8,128)(2,1)S(1)} %get-tuple-element.52), channel_id=1, source_target_pairs={{0,8},{1,9},{2,10},{3,11},{4,12},{5,13},{6,14},{7,15},{8,24},{9,25... | collective-permute-start | bytes 1597448 | tf_op jit(solution)/shard_map/ppermute | solution.py:211
  6.0 9.2 %collective-permute-start.1 = (bf16[2,16,4096]{2,1,0:T(8,128)(2,1)S(1)}, bf16[2,16,4096]{2,1,0:T(8,128)(2,1)S(1)}, u32[]{:S(2)}, u32[]{:S(2)}) collective-permute-start(bf16[2,16,4096]{2,1,0:T(8,128)(2,1)S(1)} %get-tuple-element.53), channel_id=1, source_target_pairs={{0,2},{1,3},{2,0},{3,1},{4,6},{5,7},{6,4},{7,5},{8,10},{9,11},{10,... | collective-permute-start | bytes 786440 | tf_op jit(solution)/shard_map/ppermute | solution.py:210
  7.4 16.1 %collective-permute-start.4 = (bf16[2,16,4096]{2,1,0:T(8,128)(2,1)S(1)}, bf16[2,16,4096]{2,1,0:T(8,128)(2,1)S(1)}, u32[]{:S(2)}, u32[]{:S(2)}) collective-permute-start(bf16[2,16,4096]{2,1,0:T(8,128)(2,1)S(1)} %get-tuple-element.58), channel_id=1, source_target_pairs={{0,4},{1,5},{2,6},{3,7},{4,0},{5,1},{6,2},{7,3},{8,12},{9,13},{10,... | collective-permute-start | bytes 786440 | tf_op jit(solution)/shard_map/ppermute | solution.py:210
  9.0 15.1 %collective-permute-start.5 = (bf16[2,16,4096]{2,1,0:T(8,128)(2,1)S(1)}, bf16[2,16,4096]{2,1,0:T(8,128)(2,1)S(1)}, u32[]{:S(2)}, u32[]{:S(2)}) collective-permute-start(bf16[2,16,4096]{2,1,0:T(8,128)(2,1)S(1)} %get-tuple-element.59), channel_id=1, source_target_pairs={{0,6},{1,7},{2,4},{3,5},{4,2},{5,3},{6,0},{7,1},{8,14},{9,15},{10,... | collective-permute-start | bytes 786440 | tf_op jit(solution)/shard_map/ppermute | solution.py:210
  19.1 14.2 %collective-permute-start.2 = (bf16[32,8320]{1,0:T(8,128)(2,1)S(1)}, bf16[32,8320]{1,0:T(8,128)(2,1)S(1)}, u32[]{:S(2)}, u32[]{:S(2)}) collective-permute-start(bf16[32,8320]{1,0:T(8,128)(2,1)S(1)} %collective-permute-done.held), channel_id=1, source_target_pairs={{0,8},{1,9},{2,10},{3,11},{4,12},{5,13},{6,14},{7,15},{8,24},{9,25... | collective-permute-start | bytes 1597448 | tf_op jit(solution)/shard_map/ppermute | solution.py:211
  20.4 9.3 %collective-permute-start.3 = (bf16[2,16,4096]{2,1,0:T(8,128)(2,1)S(1)}, bf16[2,16,4096]{2,1,0:T(8,128)(2,1)S(1)}, u32[]{:S(2)}, u32[]{:S(2)}) collective-permute-start(bf16[2,16,4096]{2,1,0:T(8,128)(2,1)S(1)} %get-tuple-element.57), channel_id=1, source_target_pairs={{0,2},{1,3},{2,0},{3,1},{4,6},{5,7},{6,4},{7,5},{8,10},{9,11},{10,... | collective-permute-start | bytes 786440 | tf_op jit(solution)/shard_map/ppermute | solution.py:210
  22.0 15.6 %collective-permute-start.8 = (bf16[2,16,4096]{2,1,0:T(8,128)(2,1)S(1)}, bf16[2,16,4096]{2,1,0:T(8,128)(2,1)S(1)}, u32[]{:S(2)}, u32[]{:S(2)}) collective-permute-start(bf16[2,16,4096]{2,1,0:T(8,128)(2,1)S(1)} %get-tuple-element.66), channel_id=1, source_target_pairs={{0,4},{1,5},{2,6},{3,7},{4,0},{5,1},{6,2},{7,3},{8,12},{9,13},{10,... | collective-permute-start | bytes 786440 | tf_op jit(solution)/shard_map/ppermute | solution.py:210
  23.5 14.5 %collective-permute-start.9 = (bf16[2,16,4096]{2,1,0:T(8,128)(2,1)S(1)}, bf16[2,16,4096]{2,1,0:T(8,128)(2,1)S(1)}, u32[]{:S(2)}, u32[]{:S(2)}) collective-permute-start(bf16[2,16,4096]{2,1,0:T(8,128)(2,1)S(1)} %get-tuple-element.67), channel_id=1, source_target_pairs={{0,6},{1,7},{2,4},{3,5},{4,2},{5,3},{6,0},{7,1},{8,14},{9,15},{10,... | collective-permute-start | bytes 786440 | tf_op jit(solution)/shard_map/ppermute | solution.py:210
  33.7 13.3 %collective-permute-start.6 = (bf16[32,8320]{1,0:T(8,128)(2,1)S(1)}, bf16[32,8320]{1,0:T(8,128)(2,1)S(1)}, u32[]{:S(2)}, u32[]{:S(2)}) collective-permute-start(bf16[32,8320]{1,0:T(8,128)(2,1)S(1)} %collective-permute-done.2.held), channel_id=1, source_target_pairs={{0,8},{1,9},{2,10},{3,11},{4,12},{5,13},{6,14},{7,15},{8,24},{9,25... | collective-permute-start | bytes 1597448 | tf_op jit(solution)/shard_map/ppermute | solution.py:211
  34.3 8.9 %collective-permute-start.7 = (bf16[2,16,4096]{2,1,0:T(8,128)(2,1)S(1)}, bf16[2,16,4096]{2,1,0:T(8,128)(2,1)S(1)}, u32[]{:S(2)}, u32[]{:S(2)}) collective-permute-start(bf16[2,16,4096]{2,1,0:T(8,128)(2,1)S(1)} %get-tuple-element.65), channel_id=1, source_target_pairs={{0,2},{1,3},{2,0},{3,1},{4,6},{5,7},{6,4},{7,5},{8,10},{9,11},{10,... | collective-permute-start | bytes 786440 | tf_op jit(solution)/shard_map/ppermute | solution.py:210
  35.8 15.4 %collective-permute-start.10 = (bf16[2,16,4096]{2,1,0:T(8,128)(2,1)S(1)}, bf16[2,16,4096]{2,1,0:T(8,128)(2,1)S(1)}, u32[]{:S(2)}, u32[]{:S(2)}) collective-permute-start(bf16[2,16,4096]{2,1,0:T(8,128)(2,1)S(1)} %get-tuple-element.72), channel_id=1, source_target_pairs={{0,4},{1,5},{2,6},{3,7},{4,0},{5,1},{6,2},{7,3},{8,12},{9,13},{10,... | collective-permute-start | bytes 786440 | tf_op jit(solution)/shard_map/ppermute | solution.py:210
  37.5 13.7 %collective-permute-start.11 = (bf16[2,16,4096]{2,1,0:T(8,128)(2,1)S(1)}, bf16[2,16,4096]{2,1,0:T(8,128)(2,1)S(1)}, u32[]{:S(2)}, u32[]{:S(2)}) collective-permute-start(bf16[2,16,4096]{2,1,0:T(8,128)(2,1)S(1)} %get-tuple-element.73), channel_id=1, source_target_pairs={{0,6},{1,7},{2,4},{3,5},{4,2},{5,3},{6,0},{7,1},{8,14},{9,15},{10,... | collective-permute-start | bytes 786440 | tf_op jit(solution)/shard_map/ppermute | solution.py:210
  50.1 7.0 %collective-permute-start.14 = (bf16[16,4096]{1,0:T(8,128)(2,1)S(1)}, bf16[16,4096]{1,0:T(8,128)(2,1)S(1)}, u32[]{:S(2)}, u32[]{:S(2)}) collective-permute-start(bf16[16,4096]{1,0:T(8,128)(2,1)S(1)} %get-tuple-element.78), channel_id=1, source_target_pairs={{0,6},{1,7},{2,4},{3,5},{4,2},{5,3},{6,0},{7,1},{8,14},{9,15},{10,... | collective-permute-start | bytes 393224 | tf_op jit(solution)/shard_map/ppermute | solution.py:216
  51.3 5.9 %collective-permute-start.15 = (bf16[2,96,4096]{2,1,0:T(8,128)(2,1)S(1)}, bf16[2,96,4096]{2,1,0:T(8,128)(2,1)S(1)}, u32[]{:S(2)}, u32[]{:S(2)}) collective-permute-start(bf16[2,96,4096]{2,1,0:T(8,128)(2,1)S(1)} %slice_dynamic-update-slice_fusion), channel_id=1, source_target_pairs={{0,1},{1,0},{2,3},{3,2},{4,5},{5,4},{6,7},{7,6},{8,9},{9,8},{10,11... | collective-permute-start | bytes 4718600 | tf_op jit(solution)/shard_map/ppermute | solution.py:217
  51.3 12.1 %collective-permute-start.17 = (bf16[16,4096]{1,0:T(8,128)(2,1)S(1)}, bf16[16,4096]{1,0:T(8,128)(2,1)S(1)}, u32[]{:S(2)}, u32[]{:S(2)}) collective-permute-start(bf16[16,4096]{1,0:T(8,128)(2,1)S(1)} %get-tuple-element.80), channel_id=1, source_target_pairs={{0,2},{1,3},{2,0},{3,1},{4,6},{5,7},{6,4},{7,5},{8,10},{9,11},{10,... | collective-permute-start | bytes 393224 | tf_op jit(solution)/shard_map/ppermute | solution.py:216
  52.6 10.8 %collective-permute-start.18 = (bf16[16,4096]{1,0:T(8,128)(2,1)S(1)}, bf16[16,4096]{1,0:T(8,128)(2,1)S(1)}, u32[]{:S(2)}, u32[]{:S(2)}) collective-permute-start(bf16[16,4096]{1,0:T(8,128)(2,1)S(1)} %get-tuple-element.81), channel_id=1, source_target_pairs={{0,4},{1,5},{2,6},{3,7},{4,0},{5,1},{6,2},{7,3},{8,12},{9,13},{10,... | collective-permute-start | bytes 393224 | tf_op jit(solution)/shard_map/ppermute | solution.py:216
  54.1 9.3 %collective-permute-start.19 = (bf16[16,4096]{1,0:T(8,128)(2,1)S(1)}, bf16[16,4096]{1,0:T(8,128)(2,1)S(1)}, u32[]{:S(2)}, u32[]{:S(2)}) collective-permute-start(bf16[16,4096]{1,0:T(8,128)(2,1)S(1)} %get-tuple-element.82), channel_id=1, source_target_pairs={{0,6},{1,7},{2,4},{3,5},{4,2},{5,3},{6,0},{7,1},{8,14},{9,15},{10,... | collective-permute-start | bytes 393224 | tf_op jit(solution)/shard_map/ppermute | solution.py:216
  71.5 11.8 %collective-permute-start.21 = (bf16[3,4,8,4096]{3,2,1,0:T(8,128)(2,1)S(1)}, bf16[3,4,8,4096]{3,2,1,0:T(8,128)(2,1)S(1)}, u32[]{:S(2)}, u32[]{:S(2)}) collective-permute-start(bf16[3,4,8,4096]{3,2,1,0:T(8,128)(2,1)S(1)} %bitcast.148), channel_id=1, source_target_pairs={{0,1},{1,0},{2,3},{3,2},{4,5},{5,4},{6,7},{7,6},{8,9},{9,8},{10,11... | collective-permute-start | bytes 2359304 | tf_op jit(solution)/shard_map/ppermute | solution.py:234
  72.9 6.4 %collective-permute-start.29 = (bf16[16,4096]{1,0:T(8,128)(2,1)S(1)}, bf16[16,4096]{1,0:T(8,128)(2,1)S(1)}, u32[]{:S(2)}, u32[]{:S(2)}) collective-permute-start(bf16[16,4096]{1,0:T(8,128)(2,1)S(1)} %get-tuple-element.111), channel_id=1, source_target_pairs={{0,2},{1,3},{2,0},{3,1},{4,6},{5,7},{6,4},{7,5},{8,10},{9,11},{10,... | collective-permute-start | bytes 393224 | tf_op jit(solution)/shard_map/ppermute | solution.py:238
  73.0 8.4 %collective-permute-start.30 = (bf16[16,4096]{1,0:T(8,128)(2,1)S(1)}, bf16[16,4096]{1,0:T(8,128)(2,1)S(1)}, u32[]{:S(2)}, u32[]{:S(2)}) collective-permute-start(bf16[16,4096]{1,0:T(8,128)(2,1)S(1)} %get-tuple-element.113), channel_id=1, source_target_pairs={{0,4},{1,5},{2,6},{3,7},{4,0},{5,1},{6,2},{7,3},{8,12},{9,13},{10,... | collective-permute-start | bytes 393224 | tf_op jit(solution)/shard_map/ppermute | solution.py:238
  74.2 7.2 %collective-permute-start.31 = (bf16[16,4096]{1,0:T(8,128)(2,1)S(1)}, bf16[16,4096]{1,0:T(8,128)(2,1)S(1)}, u32[]{:S(2)}, u32[]{:S(2)}) collective-permute-start(bf16[16,4096]{1,0:T(8,128)(2,1)S(1)} %get-tuple-element.112), channel_id=1, source_target_pairs={{0,6},{1,7},{2,4},{3,5},{4,2},{5,3},{6,0},{7,1},{8,14},{9,15},{10,... | collective-permute-start | bytes 393224 | tf_op jit(solution)/shard_map/ppermute | solution.py:238
  81.6 7.3 %collective-permute-start.32 = (bf16[32,4096]{1,0:T(8,128)(2,1)S(1)}, bf16[32,4096]{1,0:T(8,128)(2,1)S(1)}, u32[]{:S(2)}, u32[]{:S(2)}) collective-permute-start(bf16[32,4096]{1,0:T(8,128)(2,1)S(1)} %convolution_convert_fusion.1), channel_id=1, source_target_pairs={{8,0},{9,1},{10,2},{11,3},{12,4},{13,5},{14,6},{15,7},{24,8},{25,9... | collective-permute-start | bytes 786440 | tf_op jit(solution)/shard_map/ppermute | solution.py:258
  83.4 7.2 %collective-permute-start.25 = (bf16[16,4096]{1,0:T(8,128)(2,1)S(1)}, bf16[16,4096]{1,0:T(8,128)(2,1)S(1)}, u32[]{:S(2)}, u32[]{:S(2)}) collective-permute-start(bf16[16,4096]{1,0:T(8,128)(2,1)S(1)} %get-tuple-element.115), channel_id=1, source_target_pairs={{0,2},{1,3},{2,0},{3,1},{4,6},{5,7},{6,4},{7,5},{8,10},{9,11},{10,... | collective-permute-start | bytes 393224 | tf_op jit(solution)/shard_map/ppermute | solution.py:238
  85.1 6.5 %collective-permute-start.26 = (bf16[16,4096]{1,0:T(8,128)(2,1)S(1)}, bf16[16,4096]{1,0:T(8,128)(2,1)S(1)}, u32[]{:S(2)}, u32[]{:S(2)}) collective-permute-start(bf16[16,4096]{1,0:T(8,128)(2,1)S(1)} %get-tuple-element.117), channel_id=1, source_target_pairs={{0,4},{1,5},{2,6},{3,7},{4,0},{5,1},{6,2},{7,3},{8,12},{9,13},{10,... | collective-permute-start | bytes 393224 | tf_op jit(solution)/shard_map/ppermute | solution.py:238
  85.5 8.1 %collective-permute-start.27 = (bf16[16,4096]{1,0:T(8,128)(2,1)S(1)}, bf16[16,4096]{1,0:T(8,128)(2,1)S(1)}, u32[]{:S(2)}, u32[]{:S(2)}) collective-permute-start(bf16[16,4096]{1,0:T(8,128)(2,1)S(1)} %get-tuple-element.116), channel_id=1, source_target_pairs={{0,6},{1,7},{2,4},{3,5},{4,2},{5,3},{6,0},{7,1},{8,14},{9,15},{10,... | collective-permute-start | bytes 393224 | tf_op jit(solution)/shard_map/ppermute | solution.py:238
  87.0 14.1 %collective-permute-start.22 = (bf16[16,4096]{1,0:T(8,128)(2,1)S(1)}, bf16[16,4096]{1,0:T(8,128)(2,1)S(1)}, u32[]{:S(2)}, u32[]{:S(2)}) collective-permute-start(bf16[16,4096]{1,0:T(8,128)(2,1)S(1)} %get-tuple-element.119), channel_id=1, source_target_pairs={{0,2},{1,3},{2,0},{3,1},{4,6},{5,7},{6,4},{7,5},{8,10},{9,11},{10,... | collective-permute-start | bytes 393224 | tf_op jit(solution)/shard_map/ppermute | solution.py:238
  89.0 12.1 %collective-permute-start.23 = (bf16[16,4096]{1,0:T(8,128)(2,1)S(1)}, bf16[16,4096]{1,0:T(8,128)(2,1)S(1)}, u32[]{:S(2)}, u32[]{:S(2)}) collective-permute-start(bf16[16,4096]{1,0:T(8,128)(2,1)S(1)} %get-tuple-element.121), channel_id=1, source_target_pairs={{0,4},{1,5},{2,6},{3,7},{4,0},{5,1},{6,2},{7,3},{8,12},{9,13},{10,... | collective-permute-start | bytes 393224 | tf_op jit(solution)/shard_map/ppermute | solution.py:238
  90.6 10.5 %collective-permute-start.24 = (bf16[16,4096]{1,0:T(8,128)(2,1)S(1)}, bf16[16,4096]{1,0:T(8,128)(2,1)S(1)}, u32[]{:S(2)}, u32[]{:S(2)}) collective-permute-start(bf16[16,4096]{1,0:T(8,128)(2,1)S(1)} %get-tuple-element.120), channel_id=1, source_target_pairs={{0,6},{1,7},{2,4},{3,5},{4,2},{5,3},{6,0},{7,1},{8,14},{9,15},{10,... | collective-permute-start | bytes 393224 | tf_op jit(solution)/shard_map/ppermute | solution.py:238
  91.7 9.7 %collective-permute-start.34 = (bf16[16,4096]{1,0:T(8,128)(2,1)S(1)}, bf16[16,4096]{1,0:T(8,128)(2,1)S(1)}, u32[]{:S(2)}, u32[]{:S(2)}) collective-permute-start(bf16[16,4096]{1,0:T(8,128)(2,1)S(1)} %get-tuple-element.107), channel_id=1, source_target_pairs={{0,2},{1,3},{2,0},{3,1},{4,6},{5,7},{6,4},{7,5},{8,10},{9,11},{10,... | collective-permute-start | bytes 393224 | tf_op jit(solution)/shard_map/ppermute | solution.py:238
  93.9 7.2 %collective-permute-start.33 = (bf16[32,4096]{1,0:T(8,128)(2,1)S(1)}, bf16[32,4096]{1,0:T(8,128)(2,1)S(1)}, u32[]{:S(2)}, u32[]{:S(2)}) collective-permute-start(bf16[32,4096]{1,0:T(8,128)(2,1)S(1)} %fusion.17), channel_id=1, source_target_pairs={{8,0},{9,1},{10,2},{11,3},{12,4},{13,5},{14,6},{15,7},{24,8},{25,9... | collective-permute-start | bytes 786440 | tf_op jit(solution)/shard_map/ppermute | solution.py:258
  101.4 9.6 %collective-permute-start.37 = (bf16[32,4096]{1,0:T(8,128)(2,1)S(1)}, bf16[32,4096]{1,0:T(8,128)(2,1)S(1)}, u32[]{:S(2)}, u32[]{:S(2)}) collective-permute-start(bf16[32,4096]{1,0:T(8,128)(2,1)S(1)} %fusion.16), channel_id=1, source_target_pairs={{8,0},{9,1},{10,2},{11,3},{12,4},{13,5},{14,6},{15,7},{24,8},{25,9... | collective-permute-start | bytes 786440 | tf_op jit(solution)/shard_map/ppermute | solution.py:258
  105.1 5.9 %collective-permute-start.36 = (bf16[16,4096]{1,0:T(8,128)(2,1)S(1)}, bf16[16,4096]{1,0:T(8,128)(2,1)S(1)}, u32[]{:S(2)}, u32[]{:S(2)}) collective-permute-start(bf16[16,4096]{1,0:T(8,128)(2,1)S(1)} %get-tuple-element.108), channel_id=1, source_target_pairs={{0,6},{1,7},{2,4},{3,5},{4,2},{5,3},{6,0},{7,1},{8,14},{9,15},{10,... | collective-permute-start | bytes 393224 | tf_op jit(solution)/shard_map/ppermute | solution.py:238
  (11 other events, 42.9 us)

commit v3 on v2

--- a/solution.py
+++ b/solution.py
@@ -196,6 +196,7 @@
     node, place = lax.axis_index("node"), lax.axis_index("local")
     spot = jnp.stack([node // 2 * 2 * per_node, (node % 2) * per_node + place])
 
+    flips_back = [flips[i] for i in (0, 2, 1)]
     picks, got = [], []
     for w in range(depth - 1):
         if w == 0:
@@ -207,13 +208,13 @@
             held = ready
             *chosen, pick = next_rows(top, codes, ready, False)
         picks.append(pick)
-        got.append([chosen[0]] + [lax.ppermute(c, AXES, flip) for c, flip in zip(chosen[1:], flips)])
+        got.append([chosen[0]] + [lax.ppermute(chosen[i + 1], AXES, flips[i]) for i in (0, 2, 1)])
         held = lax.ppermute(held, AXES, ring)
     *chosen, pick = next_rows(top, codes, ordered(held, got, depth - 1), True)
     picks.append(pick)
     ends = []
     for part in (chosen[:4], chosen[4:]):
-        ends.append([part[0]] + [lax.ppermute(c, AXES, flip) for c, flip in zip(part[1:], flips)])
+        ends.append([part[0]] + [lax.ppermute(part[i + 1], AXES, flips[i]) for i in (0, 2, 1)])
     most = lax.ppermute(jnp.concatenate([g[:, capacity:] for window in got for g in window], axis=1), AXES, flip_core)
 
     def gather(i, end):
@@ -230,32 +231,48 @@
     half = depth * 4 * capacity
     own = row_grad[:half].reshape(depth, 4, capacity, width)
     theirs = row_grad[half:].reshape(depth, 4, capacity, width)
-    last = lax.ppermute(theirs[depth - 1], AXES, flip_core)
-    rest = lax.ppermute(theirs[: depth - 1], AXES, flip_core)
+    cut = depth // 2
+    swapped = [lax.ppermute(theirs[:cut], AXES, flip_core), lax.ppermute(theirs[cut:], AXES, flip_core)]
+    swapped = [swapped[w // cut][w % cut] for w in range(depth)]
+    BACKPOS = (0, 2, 1)
+    groups = [[2], [3], [1], [0]]
     came = {}
-    for w in reversed(range(depth)):
-        both = jnp.concatenate([own[w], last if w == depth - 1 else rest[w]], axis=1)
-        came[w] = [both[0]] + [lax.ppermute(both[i + 1], AXES, flip) for i, flip in enumerate(flips)]
+    tied = {}
+    for group in groups:
+        both = jnp.concatenate(
+            [jnp.concatenate([own[w], swapped[w]], axis=1).reshape(4, 2 * capacity, width) for w in group], axis=1
+        )
+        tied[group[0]] = [lax.ppermute(both[i + 1], AXES, flips_back[i]) for i in (0, 2, 1)]
+        for n, w in enumerate(group):
+            came[w] = (group[0], n, both[0])
+    total = None
+    sums = {}
     down_local = None
-    total = None
-    for w in reversed(range(depth)):
-        partial = lax.dot_general(
-            picks[w], jnp.concatenate(came[w], axis=0), (((0,), (0,)), ((), ())), preferred_element_type=F32
+    ahead = depth // 2
+    for w in [w for group in groups for w in group]:
+        lead, n, mine = came[w]
+        pair = 2 * capacity
+        parts = [mine[n * pair : (n + 1) * pair]] + [None] * 3
+        for i, t in zip((0, 2, 1), tied[lead]):
+            parts[BACKPOS[i] + 1] = t[n * pair : (n + 1) * pair]
+        total = lax.dot_general(
+            picks[w], jnp.concatenate(parts, axis=0), (((0,), (0,)), ((), ())), preferred_element_type=F32
         )
-        if total is not None:
-            partial = partial + total.astype(F32)
-        total = partial.astype(BF16)
+        for extra in sums.get(w, []):
+            total = total + extra.astype(F32)
+        total = total.astype(BF16)
         if w == 2:
             total, hidden = lax.optimization_barrier((total, hidden))
             down_local = lax.dot_general(
                 hidden, dy_rows, (((0,), (0,)), ((), ())), preferred_element_type=F32
             ).astype(BF16)
+        if w == 0:
+            total, down_local = lax.optimization_barrier((total, down_local))
+        if w == 2:
+            total, tied[3][:1] = lax.optimization_barrier((total, tied[3][:1]))
         if w:
-            if w == 1:
-                total, down_local = lax.optimization_barrier((total, down_local))
-            if w == 1:
-                total, came[w - 1][1:2] = lax.optimization_barrier((total, came[w - 1][1:2]))
-            total = lax.ppermute(total, AXES, back)
+            dest, perm = (w - 1, back) if w <= ahead else ((w + 1) % depth, ring)
+            sums.setdefault(dest, []).append(lax.ppermute(total, AXES, perm))
     return total, down_local[None]
 
 

time: 112 us -> 107 us (0.955)
  starting transfers between devices: 45.3 us -> 42.8 us
  waiting for transfers between devices: 43.8 us -> 41.5 us
    ppermute x32, starting transfers between devices: 40.4 us -> 37.9 us  [the longest x12 13.6 us: body(): lax.ppermute(both[i + 1], AXES, flips_back[i])]
    ppermute x32, waiting for transfers between devices: 29.8 us -> 27.7 us  [the longest x9 16.6 us: body(): lax.ppermute(chosen[i + 1], AXES, flips[i])]
  transfers between devices with their start and end apart: 38 -> 38, of which waited for: 18 -> 17; matrix products, arithmetic and copies ran while one was open for 9% -> 9% of each run, Pallas kernels for 1% -> 1%
where the time goes in v3:
time: 107 us
  starting transfers between devices  42.8 us (40%)
  waiting for transfers between devices  41.5 us (39%)
  matrix products  15.8 us (15%)
  Pallas kernels  3.63 us (3%)
  local copies, waits for them, and re-layouts  1.78 us (2%)
  between operations  1.23 us (1%)
    ppermute x9, waiting for transfers between devices, body(): lax.ppermute(chosen[i + 1], AXES, flips[i])  16.6 us
    ppermute x12, starting transfers between devices, body(): lax.ppermute(both[i + 1], AXES, flips_back[i])  13.6 us
    ppermute x3, waiting for transfers between devices, body(): held = lax.ppermute(held, AXES, ring)  11.2 us
    ppermute x9, starting transfers between devices, body(): lax.ppermute(chosen[i + 1], AXES, flips[i])  10.7 us
    ppermute x6, starting transfers between devices, body(): lax.ppermute(part[i + 1], AXES, flips[i])  7.95 us
    ppermute x12, waiting for transfers between devices, body(): lax.ppermute(both[i + 1], AXES, flips_back[i])  5.9 us
    ppermute x3, starting transfers between devices, body(): sums.setdefault(dest, []).append(lax.ppermute(total, AXES, perm))  5.08 us
    dot_general x1, matrix products, body(): lax.dot_general(hidden, dy_rows, (((0,), (0,)), ((), ())), preferred_elem...  4.54 us
  transfers between devices with their start and end apart: 38, of which 17 were waited for; matrix products, arithmetic and copies ran while one was open for 9% of the time, Pallas kernels for 1%

profile of v3, /device:TPU:0, one launch (start us, length us, event | category | flops | bytes accessed | tf_op | source)
XLA Modules:
  0.0 107.1 jit_solution(13763542510748911493)
XLA Ops:
  0.7 2.1 %first_rows.1 = (bf16[2,16,4096]{2,1,0:T(8,128)(2,1)S(1)}, bf16[2,16,4096]{2,1,0:T(8,128)(2,1)S(1)}, bf16[2,16,4096]{2,1,0:T(8,128)(2,1)S(1)}, bf16[2,16,4096]{2...) custom-call(s32[2]{0:T(128)S(1)} %pad_add_fusion.spot, ...), custom_call_target="tpu_custom_call" | custom-call | tf_op jit(solution)/shard_map/first_rows/pallas_call | solution.py:133
  2.9 3.1 %collective-permute-start = (bf16[32,8320]{1,0:T(8,128)(2,1)S(1)}, bf16[32,8320]{1,0:T(8,128)(2,1)S(1)}, u32[]{:S(2)}, u32[]{:S(2)}) collective-permute-start(bf16[32,8320]{1,0:T(8,128)(2,1)S(1)} %get-tuple-element.52), channel_id=1, source_target_pairs={{0,8},{1,9},{2,10},{3,11},{4,12},{5,13},{6,14},{7,15},{8,24},{9,25... | collective-permute-start | bytes 1597448 | tf_op jit(solution)/shard_map/ppermute | solution.py:212
  7.4 1.5 %collective-permute-start.4 = (bf16[2,16,4096]{2,1,0:T(8,128)(2,1)S(1)}, bf16[2,16,4096]{2,1,0:T(8,128)(2,1)S(1)}, u32[]{:S(2)}, u32[]{:S(2)}) collective-permute-start(bf16[2,16,4096]{2,1,0:T(8,128)(2,1)S(1)} %get-tuple-element.58), channel_id=1, source_target_pairs={{0,6},{1,7},{2,4},{3,5},{4,2},{5,3},{6,0},{7,1},{8,14},{9,15},{10,... | collective-permute-start | bytes 786440 | tf_op jit(solution)/shard_map/ppermute | solution.py:211
  9.5 5.7 %collective-permute-done.1 = bf16[2,16,4096]{2,1,0:T(8,128)(2,1)S(1)} collective-permute-done((bf16[2,16,4096]{2,1,0:T(8,128)(2,1)S(1)}, bf16[2,16,4096]{2,1,0:T(8,128)(2,1)S(1)}, u32[]{:S(2)}, u32[]{:S(2)}) %collective-permute-start.1) | collective-permute-done | bytes 262176 | tf_op jit(solution)/shard_map/ppermute | solution.py:211
  15.2 3.9 %collective-permute-done.held = bf16[32,8320]{1,0:T(8,128)(2,1)S(1)} collective-permute-done((bf16[32,8320]{1,0:T(8,128)(2,1)S(1)}, bf16[32,8320]{1,0:T(8,128)(2,1)S(1)}, u32[]{:S(2)}, u32[]{:S(2)}) %collective-permute-start) | collective-permute-done | bytes 532512 | tf_op jit(solution)/shard_map/ppermute | solution.py:212
  20.4 1.6 %collective-permute-start.3 = (bf16[2,16,4096]{2,1,0:T(8,128)(2,1)S(1)}, bf16[2,16,4096]{2,1,0:T(8,128)(2,1)S(1)}, u32[]{:S(2)}, u32[]{:S(2)}) collective-permute-start(bf16[2,16,4096]{2,1,0:T(8,128)(2,1)S(1)} %get-tuple-element.57), channel_id=1, source_target_pairs={{0,2},{1,3},{2,0},{3,1},{4,6},{5,7},{6,4},{7,5},{8,10},{9,11},{10,... | collective-permute-start | bytes 786440 | tf_op jit(solution)/shard_map/ppermute | solution.py:211
  22.0 1.5 %collective-permute-start.8 = (bf16[2,16,4096]{2,1,0:T(8,128)(2,1)S(1)}, bf16[2,16,4096]{2,1,0:T(8,128)(2,1)S(1)}, u32[]{:S(2)}, u32[]{:S(2)}) collective-permute-start(bf16[2,16,4096]{2,1,0:T(8,128)(2,1)S(1)} %get-tuple-element.66), channel_id=1, source_target_pairs={{0,6},{1,7},{2,4},{3,5},{4,2},{5,3},{6,0},{7,1},{8,14},{9,15},{10,... | collective-permute-start | bytes 786440 | tf_op jit(solution)/shard_map/ppermute | solution.py:211
  24.1 5.6 %collective-permute-done.3 = bf16[2,16,4096]{2,1,0:T(8,128)(2,1)S(1)} collective-permute-done((bf16[2,16,4096]{2,1,0:T(8,128)(2,1)S(1)}, bf16[2,16,4096]{2,1,0:T(8,128)(2,1)S(1)}, u32[]{:S(2)}, u32[]{:S(2)}) %collective-permute-start.3) | collective-permute-done | bytes 262176 | tf_op jit(solution)/shard_map/ppermute | solution.py:211
  29.7 3.5 %collective-permute-done.2.held = bf16[32,8320]{1,0:T(8,128)(2,1)S(1)} collective-permute-done((bf16[32,8320]{1,0:T(8,128)(2,1)S(1)}, bf16[32,8320]{1,0:T(8,128)(2,1)S(1)}, u32[]{:S(2)}, u32[]{:S(2)}) %collective-permute-start.2) | collective-permute-done | bytes 532512 | tf_op jit(solution)/shard_map/ppermute | solution.py:212
  34.3 1.5 %collective-permute-start.7 = (bf16[2,16,4096]{2,1,0:T(8,128)(2,1)S(1)}, bf16[2,16,4096]{2,1,0:T(8,128)(2,1)S(1)}, u32[]{:S(2)}, u32[]{:S(2)}) collective-permute-start(bf16[2,16,4096]{2,1,0:T(8,128)(2,1)S(1)} %get-tuple-element.65), channel_id=1, source_target_pairs={{0,2},{1,3},{2,0},{3,1},{4,6},{5,7},{6,4},{7,5},{8,10},{9,11},{10,... | collective-permute-start | bytes 786440 | tf_op jit(solution)/shard_map/ppermute | solution.py:211
  35.8 1.5 %collective-permute-start.10 = (bf16[2,16,4096]{2,1,0:T(8,128)(2,1)S(1)}, bf16[2,16,4096]{2,1,0:T(8,128)(2,1)S(1)}, u32[]{:S(2)}, u32[]{:S(2)}) collective-permute-start(bf16[2,16,4096]{2,1,0:T(8,128)(2,1)S(1)} %get-tuple-element.72), channel_id=1, source_target_pairs={{0,6},{1,7},{2,4},{3,5},{4,2},{5,3},{6,0},{7,1},{8,14},{9,15},{10,... | collective-permute-start | bytes 786440 | tf_op jit(solution)/shard_map/ppermute | solution.py:211
  38.0 5.2 %collective-permute-done.7 = bf16[2,16,4096]{2,1,0:T(8,128)(2,1)S(1)} collective-permute-done((bf16[2,16,4096]{2,1,0:T(8,128)(2,1)S(1)}, bf16[2,16,4096]{2,1,0:T(8,128)(2,1)S(1)}, u32[]{:S(2)}, u32[]{:S(2)}) %collective-permute-start.7) | collective-permute-done | bytes 262176 | tf_op jit(solution)/shard_map/ppermute | solution.py:211
  43.3 3.8 %collective-permute-done.6.held = bf16[32,8320]{1,0:T(8,128)(2,1)S(1)} collective-permute-done((bf16[32,8320]{1,0:T(8,128)(2,1)S(1)}, bf16[32,8320]{1,0:T(8,128)(2,1)S(1)}, u32[]{:S(2)}, u32[]{:S(2)}) %collective-permute-start.6) | collective-permute-done | bytes 532512 | tf_op jit(solution)/shard_map/ppermute | solution.py:212
  48.5 1.5 %collective-permute-start.13 = (bf16[16,4096]{1,0:T(8,128)(2,1)S(1)}, bf16[16,4096]{1,0:T(8,128)(2,1)S(1)}, u32[]{:S(2)}, u32[]{:S(2)}) collective-permute-start(bf16[16,4096]{1,0:T(8,128)(2,1)S(1)} %get-tuple-element.77), channel_id=1, source_target_pairs={{0,6},{1,7},{2,4},{3,5},{4,2},{5,3},{6,0},{7,1},{8,14},{9,15},{10,... | collective-permute-start | bytes 393224 | tf_op jit(solution)/shard_map/ppermute | solution.py:217
  52.6 1.9 %collective-permute-start.18 = (bf16[16,4096]{1,0:T(8,128)(2,1)S(1)}, bf16[16,4096]{1,0:T(8,128)(2,1)S(1)}, u32[]{:S(2)}, u32[]{:S(2)}) collective-permute-start(bf16[16,4096]{1,0:T(8,128)(2,1)S(1)} %get-tuple-element.81), channel_id=1, source_target_pairs={{0,6},{1,7},{2,4},{3,5},{4,2},{5,3},{6,0},{7,1},{8,14},{9,15},{10,... | collective-permute-start | bytes 393224 | tf_op jit(solution)/shard_map/ppermute | solution.py:217
  54.5 1.5 %collective-permute-start.19 = (bf16[16,4096]{1,0:T(8,128)(2,1)S(1)}, bf16[16,4096]{1,0:T(8,128)(2,1)S(1)}, u32[]{:S(2)}, u32[]{:S(2)}) collective-permute-start(bf16[16,4096]{1,0:T(8,128)(2,1)S(1)} %get-tuple-element.82), channel_id=1, source_target_pairs={{0,4},{1,5},{2,6},{3,7},{4,0},{5,1},{6,2},{7,3},{8,12},{9,13},{10,... | collective-permute-start | bytes 393224 | tf_op jit(solution)/shard_map/ppermute | solution.py:217
  57.8 1.8 %fusion.4 = f32[256,768]{1,0:T(8,128)S(1)} fusion(bf16[256,4096]{1,0:T(8,128)(2,1)S(1)} %constant_dynamic-update-slice_fusion, bf16[1,4096,768]{2,1,0:T(8,128)(2,1)S(1)} %copy-done), kind=kOutput, calls=%fused_computation.5 | convolution fusion | flops 1610612736 | bytes 9175040 | tf_op jit(solution)/shard_map/dot_general | solution.py:159
  60.6 1.8 %fusion.8 = f32[256,768]{1,0:T(8,128)S(1)} fusion(bf16[256,4096]{1,0:T(8,128)(2,1)S(1)} %constant_dynamic-update-slice_fusion, bf16[1,4096,768]{2,1,0:T(8,128)(2,1)S(1)} %bitcast.147), kind=kOutput, calls=%fused_computation.9 | convolution fusion | flops 1610612736 | bytes 9175040 | tf_op jit(solution)/shard_map/dot_general | solution.py:158
  64.2 2.1 %fusion = f32[256,768]{1,0:T(8,128)S(1)} fusion(bf16[256,4096]{1,0:T(8,128)(2,1)S(1)} %constant_dynamic-update-slice_fusion.17, bf16[1,768,4096]{2,1,0:T(8,128)(2,1)S(1)} %bitcast.155), kind=kOutput, calls=%fused_computation.1 | convolution fusion | flops 1610612736 | bytes 9175040 | tf_op jit(solution)/shard_map/dot_general | solution.py:167
  66.3 1.9 %fusion.2 = f32[256,4096]{1,0:T(8,128)S(1)} fusion(bf16[1,4096,768]{2,1,0:T(8,128)(2,1)S(1)} %copy-done, f32[256,768]{1,0:T(8,128)S(1)} %fusion, f32[256,768]{1,0:T(8,128)S(1)} %fusion.8), kind=kOutput, calls=%fused_computation.3 | convolution fusion | flops 1611792384 | bytes 12058624 | tf_op jit(solution)/shard_map/dot_general | solution.py:172
  68.1 2.0 %fusion.13 = bf16[256,4096]{1,0:T(8,128)(2,1)S(1)} fusion(f32[256,4096]{1,0:T(8,128)S(1)} %fusion.2, bf16[1,4096,768]{2,1,0:T(8,128)(2,1)S(1)} %bitcast.147, f32[256,768]{1,0:T(8,128)S(1)} %fusion.8, f32[256,768]{1,0:T(8,128)S(1)} %fusion, f32[256,768]{1,0:T(8,128)S(1)} %fusion.4), kind=kOutput, calls=%fused_computation.12 | convolution fusion | flops 1614675968 | bytes 14942208 | tf_op jit(solution)/shard_map/dot_general | solution.py:171
  74.3 1.5 %collective-permute-start.28 = (bf16[16,4096]{1,0:T(8,128)(2,1)S(1)}, bf16[16,4096]{1,0:T(8,128)(2,1)S(1)}, u32[]{:S(2)}, u32[]{:S(2)}) collective-permute-start(bf16[16,4096]{1,0:T(8,128)(2,1)S(1)} %get-tuple-element.112), channel_id=1, source_target_pairs={{0,6},{1,7},{2,4},{3,5},{4,2},{5,3},{6,0},{7,1},{8,14},{9,15},{10,... | collective-permute-start | bytes 393224 | tf_op jit(solution)/shard_map/ppermute | solution.py:245
  79.8 2.3 %collective-permute-done.27 = bf16[16,4096]{1,0:T(8,128)(2,1)S(1)} collective-permute-done((bf16[16,4096]{1,0:T(8,128)(2,1)S(1)}, bf16[16,4096]{1,0:T(8,128)(2,1)S(1)}, u32[]{:S(2)}, u32[]{:S(2)}) %collective-permute-start.27) | collective-permute-done | bytes 131104 | tf_op jit(solution)/shard_map/ppermute | solution.py:245
  82.7 1.5 %collective-permute-start.34 = (bf16[16,4096]{1,0:T(8,128)(2,1)S(1)}, bf16[16,4096]{1,0:T(8,128)(2,1)S(1)}, u32[]{:S(2)}, u32[]{:S(2)}) collective-permute-start(bf16[16,4096]{1,0:T(8,128)(2,1)S(1)} %get-tuple-element.117), channel_id=1, source_target_pairs={{0,4},{1,5},{2,6},{3,7},{4,0},{5,1},{6,2},{7,3},{8,12},{9,13},{10,... | collective-permute-start | bytes 393224 | tf_op jit(solution)/shard_map/ppermute | solution.py:245
  84.4 2.1 %collective-permute-start.36 = (bf16[32,4096]{1,0:T(8,128)(2,1)S(1)}, bf16[32,4096]{1,0:T(8,128)(2,1)S(1)}, u32[]{:S(2)}, u32[]{:S(2)}) collective-permute-start(bf16[32,4096]{1,0:T(8,128)(2,1)S(1)} %convolution_convert_fusion.2), channel_id=1, source_target_pairs={{8,0},{9,1},{10,2},{11,3},{12,4},{13,5},{14,6},{15,7},{24,8},{25,9... | collective-permute-start | bytes 786440 | tf_op jit(solution)/shard_map/ppermute | solution.py:275
  87.7 1.5 %collective-permute-start.35 = (bf16[16,4096]{1,0:T(8,128)(2,1)S(1)}, bf16[16,4096]{1,0:T(8,128)(2,1)S(1)}, u32[]{:S(2)}, u32[]{:S(2)}) collective-permute-start(bf16[16,4096]{1,0:T(8,128)(2,1)S(1)} %get-tuple-element.116), channel_id=1, source_target_pairs={{0,6},{1,7},{2,4},{3,5},{4,2},{5,3},{6,0},{7,1},{8,14},{9,15},{10,... | collective-permute-start | bytes 393224 | tf_op jit(solution)/shard_map/ppermute | solution.py:245
  90.0 1.5 %collective-permute-start.23 = (bf16[16,4096]{1,0:T(8,128)(2,1)S(1)}, bf16[16,4096]{1,0:T(8,128)(2,1)S(1)}, u32[]{:S(2)}, u32[]{:S(2)}) collective-permute-start(bf16[16,4096]{1,0:T(8,128)(2,1)S(1)} %get-tuple-element.123), channel_id=1, source_target_pairs={{0,4},{1,5},{2,6},{3,7},{4,0},{5,1},{6,2},{7,3},{8,12},{9,13},{10,... | collective-permute-start | bytes 393224 | tf_op jit(solution)/shard_map/ppermute | solution.py:245
  93.0 1.6 %collective-permute-done.35 = bf16[16,4096]{1,0:T(8,128)(2,1)S(1)} collective-permute-done((bf16[16,4096]{1,0:T(8,128)(2,1)S(1)}, bf16[16,4096]{1,0:T(8,128)(2,1)S(1)}, u32[]{:S(2)}, u32[]{:S(2)}) %collective-permute-start.35) | collective-permute-done | bytes 131104 | tf_op jit(solution)/shard_map/ppermute | solution.py:245
  94.6 2.1 %collective-permute-start.32 = (bf16[32,4096]{1,0:T(8,128)(2,1)S(1)}, bf16[32,4096]{1,0:T(8,128)(2,1)S(1)}, u32[]{:S(2)}, u32[]{:S(2)}) collective-permute-start(bf16[32,4096]{1,0:T(8,128)(2,1)S(1)} %convolution_convert_fusion.1), channel_id=1, source_target_pairs={{0,8},{1,9},{2,10},{3,11},{4,12},{5,13},{6,14},{7,15},{8,24},{9,25... | collective-permute-start | bytes 786440 | tf_op jit(solution)/shard_map/ppermute | solution.py:275
  97.9 4.5 %convolution_convert_fusion = bf16[768,4096]{1,0:T(8,128)(2,1)} fusion(bf16[256,768]{1,0:T(8,128)(2,1)S(1)} %multiply_convert_fusion, bf16[256,4096]{1,0:T(8,128)(2,1)S(1)} %constant_dynamic-update-slice_fusion.17), kind=kOutput, calls=%fused_computation | convolution fusion | flops 1613758464 | bytes 8781824 | tf_op jit(solution)/shard_map/dot_general | solution.py:266
  102.4 1.7 %collective-permute-done.32 = bf16[32,4096]{1,0:T(8,128)(2,1)S(1)} collective-permute-done((bf16[32,4096]{1,0:T(8,128)(2,1)S(1)}, bf16[32,4096]{1,0:T(8,128)(2,1)S(1)}, u32[]{:S(2)}, u32[]{:S(2)}) %collective-permute-start.32) | collective-permute-done | bytes 262176 | tf_op jit(solution)/shard_map/ppermute | solution.py:275
  104.1 2.0 %collective-permute-done.37 = bf16[32,4096]{1,0:T(8,128)(2,1)S(1)} collective-permute-done((bf16[32,4096]{1,0:T(8,128)(2,1)S(1)}, bf16[32,4096]{1,0:T(8,128)(2,1)S(1)}, u32[]{:S(2)}, u32[]{:S(2)}) %collective-permute-start.37) | collective-permute-done | bytes 262176 | tf_op jit(solution)/shard_map/ppermute | solution.py:275
  (118 shorter events, 28.5 us)
Async XLA Ops:
  2.9 16.2 %collective-permute-start = (bf16[32,8320]{1,0:T(8,128)(2,1)S(1)}, bf16[32,8320]{1,0:T(8,128)(2,1)S(1)}, u32[]{:S(2)}, u32[]{:S(2)}) collective-permute-start(bf16[32,8320]{1,0:T(8,128)(2,1)S(1)} %get-tuple-element.52), channel_id=1, source_target_pairs={{0,8},{1,9},{2,10},{3,11},{4,12},{5,13},{6,14},{7,15},{8,24},{9,25... | collective-permute-start | bytes 1597448 | tf_op jit(solution)/shard_map/ppermute | solution.py:212
  6.0 9.2 %collective-permute-start.1 = (bf16[2,16,4096]{2,1,0:T(8,128)(2,1)S(1)}, bf16[2,16,4096]{2,1,0:T(8,128)(2,1)S(1)}, u32[]{:S(2)}, u32[]{:S(2)}) collective-permute-start(bf16[2,16,4096]{2,1,0:T(8,128)(2,1)S(1)} %get-tuple-element.53), channel_id=1, source_target_pairs={{0,2},{1,3},{2,0},{3,1},{4,6},{5,7},{6,4},{7,5},{8,10},{9,11},{10,... | collective-permute-start | bytes 786440 | tf_op jit(solution)/shard_map/ppermute | solution.py:211
  7.4 16.0 %collective-permute-start.4 = (bf16[2,16,4096]{2,1,0:T(8,128)(2,1)S(1)}, bf16[2,16,4096]{2,1,0:T(8,128)(2,1)S(1)}, u32[]{:S(2)}, u32[]{:S(2)}) collective-permute-start(bf16[2,16,4096]{2,1,0:T(8,128)(2,1)S(1)} %get-tuple-element.58), channel_id=1, source_target_pairs={{0,6},{1,7},{2,4},{3,5},{4,2},{5,3},{6,0},{7,1},{8,14},{9,15},{10,... | collective-permute-start | bytes 786440 | tf_op jit(solution)/shard_map/ppermute | solution.py:211
  8.9 15.1 %collective-permute-start.5 = (bf16[2,16,4096]{2,1,0:T(8,128)(2,1)S(1)}, bf16[2,16,4096]{2,1,0:T(8,128)(2,1)S(1)}, u32[]{:S(2)}, u32[]{:S(2)}) collective-permute-start(bf16[2,16,4096]{2,1,0:T(8,128)(2,1)S(1)} %get-tuple-element.59), channel_id=1, source_target_pairs={{0,4},{1,5},{2,6},{3,7},{4,0},{5,1},{6,2},{7,3},{8,12},{9,13},{10,... | collective-permute-start | bytes 786440 | tf_op jit(solution)/shard_map/ppermute | solution.py:211
  19.1 14.2 %collective-permute-start.2 = (bf16[32,8320]{1,0:T(8,128)(2,1)S(1)}, bf16[32,8320]{1,0:T(8,128)(2,1)S(1)}, u32[]{:S(2)}, u32[]{:S(2)}) collective-permute-start(bf16[32,8320]{1,0:T(8,128)(2,1)S(1)} %collective-permute-done.held), channel_id=1, source_target_pairs={{0,8},{1,9},{2,10},{3,11},{4,12},{5,13},{6,14},{7,15},{8,24},{9,25... | collective-permute-start | bytes 1597448 | tf_op jit(solution)/shard_map/ppermute | solution.py:212
  20.4 9.3 %collective-permute-start.3 = (bf16[2,16,4096]{2,1,0:T(8,128)(2,1)S(1)}, bf16[2,16,4096]{2,1,0:T(8,128)(2,1)S(1)}, u32[]{:S(2)}, u32[]{:S(2)}) collective-permute-start(bf16[2,16,4096]{2,1,0:T(8,128)(2,1)S(1)} %get-tuple-element.57), channel_id=1, source_target_pairs={{0,2},{1,3},{2,0},{3,1},{4,6},{5,7},{6,4},{7,5},{8,10},{9,11},{10,... | collective-permute-start | bytes 786440 | tf_op jit(solution)/shard_map/ppermute | solution.py:211
  22.0 15.5 %collective-permute-start.8 = (bf16[2,16,4096]{2,1,0:T(8,128)(2,1)S(1)}, bf16[2,16,4096]{2,1,0:T(8,128)(2,1)S(1)}, u32[]{:S(2)}, u32[]{:S(2)}) collective-permute-start(bf16[2,16,4096]{2,1,0:T(8,128)(2,1)S(1)} %get-tuple-element.66), channel_id=1, source_target_pairs={{0,6},{1,7},{2,4},{3,5},{4,2},{5,3},{6,0},{7,1},{8,14},{9,15},{10,... | collective-permute-start | bytes 786440 | tf_op jit(solution)/shard_map/ppermute | solution.py:211
  23.5 14.5 %collective-permute-start.9 = (bf16[2,16,4096]{2,1,0:T(8,128)(2,1)S(1)}, bf16[2,16,4096]{2,1,0:T(8,128)(2,1)S(1)}, u32[]{:S(2)}, u32[]{:S(2)}) collective-permute-start(bf16[2,16,4096]{2,1,0:T(8,128)(2,1)S(1)} %get-tuple-element.67), channel_id=1, source_target_pairs={{0,4},{1,5},{2,6},{3,7},{4,0},{5,1},{6,2},{7,3},{8,12},{9,13},{10,... | collective-permute-start | bytes 786440 | tf_op jit(solution)/shard_map/ppermute | solution.py:211
  33.7 13.3 %collective-permute-start.6 = (bf16[32,8320]{1,0:T(8,128)(2,1)S(1)}, bf16[32,8320]{1,0:T(8,128)(2,1)S(1)}, u32[]{:S(2)}, u32[]{:S(2)}) collective-permute-start(bf16[32,8320]{1,0:T(8,128)(2,1)S(1)} %collective-permute-done.2.held), channel_id=1, source_target_pairs={{0,8},{1,9},{2,10},{3,11},{4,12},{5,13},{6,14},{7,15},{8,24},{9,25... | collective-permute-start | bytes 1597448 | tf_op jit(solution)/shard_map/ppermute | solution.py:212
  34.3 8.9 %collective-permute-start.7 = (bf16[2,16,4096]{2,1,0:T(8,128)(2,1)S(1)}, bf16[2,16,4096]{2,1,0:T(8,128)(2,1)S(1)}, u32[]{:S(2)}, u32[]{:S(2)}) collective-permute-start(bf16[2,16,4096]{2,1,0:T(8,128)(2,1)S(1)} %get-tuple-element.65), channel_id=1, source_target_pairs={{0,2},{1,3},{2,0},{3,1},{4,6},{5,7},{6,4},{7,5},{8,10},{9,11},{10,... | collective-permute-start | bytes 786440 | tf_op jit(solution)/shard_map/ppermute | solution.py:211
  35.8 15.4 %collective-permute-start.10 = (bf16[2,16,4096]{2,1,0:T(8,128)(2,1)S(1)}, bf16[2,16,4096]{2,1,0:T(8,128)(2,1)S(1)}, u32[]{:S(2)}, u32[]{:S(2)}) collective-permute-start(bf16[2,16,4096]{2,1,0:T(8,128)(2,1)S(1)} %get-tuple-element.72), channel_id=1, source_target_pairs={{0,6},{1,7},{2,4},{3,5},{4,2},{5,3},{6,0},{7,1},{8,14},{9,15},{10,... | collective-permute-start | bytes 786440 | tf_op jit(solution)/shard_map/ppermute | solution.py:211
  37.5 13.8 %collective-permute-start.11 = (bf16[2,16,4096]{2,1,0:T(8,128)(2,1)S(1)}, bf16[2,16,4096]{2,1,0:T(8,128)(2,1)S(1)}, u32[]{:S(2)}, u32[]{:S(2)}) collective-permute-start(bf16[2,16,4096]{2,1,0:T(8,128)(2,1)S(1)} %get-tuple-element.73), channel_id=1, source_target_pairs={{0,4},{1,5},{2,6},{3,7},{4,0},{5,1},{6,2},{7,3},{8,12},{9,13},{10,... | collective-permute-start | bytes 786440 | tf_op jit(solution)/shard_map/ppermute | solution.py:211
  50.0 6.0 %collective-permute-start.14 = (bf16[16,4096]{1,0:T(8,128)(2,1)S(1)}, bf16[16,4096]{1,0:T(8,128)(2,1)S(1)}, u32[]{:S(2)}, u32[]{:S(2)}) collective-permute-start(bf16[16,4096]{1,0:T(8,128)(2,1)S(1)} %get-tuple-element.78), channel_id=1, source_target_pairs={{0,4},{1,5},{2,6},{3,7},{4,0},{5,1},{6,2},{7,3},{8,12},{9,13},{10,... | collective-permute-start | bytes 393224 | tf_op jit(solution)/shard_map/ppermute | solution.py:217
  51.3 11.1 %collective-permute-start.17 = (bf16[16,4096]{1,0:T(8,128)(2,1)S(1)}, bf16[16,4096]{1,0:T(8,128)(2,1)S(1)}, u32[]{:S(2)}, u32[]{:S(2)}) collective-permute-start(bf16[16,4096]{1,0:T(8,128)(2,1)S(1)} %get-tuple-element.80), channel_id=1, source_target_pairs={{0,2},{1,3},{2,0},{3,1},{4,6},{5,7},{6,4},{7,5},{8,10},{9,11},{10,... | collective-permute-start | bytes 393224 | tf_op jit(solution)/shard_map/ppermute | solution.py:217
  52.6 9.8 %collective-permute-start.18 = (bf16[16,4096]{1,0:T(8,128)(2,1)S(1)}, bf16[16,4096]{1,0:T(8,128)(2,1)S(1)}, u32[]{:S(2)}, u32[]{:S(2)}) collective-permute-start(bf16[16,4096]{1,0:T(8,128)(2,1)S(1)} %get-tuple-element.81), channel_id=1, source_target_pairs={{0,6},{1,7},{2,4},{3,5},{4,2},{5,3},{6,0},{7,1},{8,14},{9,15},{10,... | collective-permute-start | bytes 393224 | tf_op jit(solution)/shard_map/ppermute | solution.py:217
  54.5 7.9 %collective-permute-start.19 = (bf16[16,4096]{1,0:T(8,128)(2,1)S(1)}, bf16[16,4096]{1,0:T(8,128)(2,1)S(1)}, u32[]{:S(2)}, u32[]{:S(2)}) collective-permute-start(bf16[16,4096]{1,0:T(8,128)(2,1)S(1)} %get-tuple-element.82), channel_id=1, source_target_pairs={{0,4},{1,5},{2,6},{3,7},{4,0},{5,1},{6,2},{7,3},{8,12},{9,13},{10,... | collective-permute-start | bytes 393224 | tf_op jit(solution)/shard_map/ppermute | solution.py:217
  70.4 6.8 %collective-permute-start.21 = (bf16[2,4,8,4096]{3,2,1,0:T(8,128)(2,1)S(1)}, bf16[2,4,8,4096]{3,2,1,0:T(8,128)(2,1)S(1)}, u32[]{:S(2)}, u32[]{:S(2)}) collective-permute-start(bf16[2,4,8,4096]{3,2,1,0:T(8,128)(2,1)S(1)} %bitcast.149), channel_id=1, source_target_pairs={{0,1},{1,0},{2,3},{3,2},{4,5},{5,4},{6,7},{7,6},{8,9},{9,8},{10,11... | collective-permute-start | bytes 1572872 | tf_op jit(solution)/shard_map/ppermute | solution.py:235
  72.3 6.2 %collective-permute-start.26 = (bf16[16,4096]{1,0:T(8,128)(2,1)S(1)}, bf16[16,4096]{1,0:T(8,128)(2,1)S(1)}, u32[]{:S(2)}, u32[]{:S(2)}) collective-permute-start(bf16[16,4096]{1,0:T(8,128)(2,1)S(1)} %get-tuple-element.111), channel_id=1, source_target_pairs={{0,2},{1,3},{2,0},{3,1},{4,6},{5,7},{6,4},{7,5},{8,10},{9,11},{10,... | collective-permute-start | bytes 393224 | tf_op jit(solution)/shard_map/ppermute | solution.py:245
  73.6 8.5 %collective-permute-start.27 = (bf16[16,4096]{1,0:T(8,128)(2,1)S(1)}, bf16[16,4096]{1,0:T(8,128)(2,1)S(1)}, u32[]{:S(2)}, u32[]{:S(2)}) collective-permute-start(bf16[16,4096]{1,0:T(8,128)(2,1)S(1)} %get-tuple-element.113), channel_id=1, source_target_pairs={{0,4},{1,5},{2,6},{3,7},{4,0},{5,1},{6,2},{7,3},{8,12},{9,13},{10,... | collective-permute-start | bytes 393224 | tf_op jit(solution)/shard_map/ppermute | solution.py:245
  74.3 8.4 %collective-permute-start.28 = (bf16[16,4096]{1,0:T(8,128)(2,1)S(1)}, bf16[16,4096]{1,0:T(8,128)(2,1)S(1)}, u32[]{:S(2)}, u32[]{:S(2)}) collective-permute-start(bf16[16,4096]{1,0:T(8,128)(2,1)S(1)} %get-tuple-element.112), channel_id=1, source_target_pairs={{0,6},{1,7},{2,4},{3,5},{4,2},{5,3},{6,0},{7,1},{8,14},{9,15},{10,... | collective-permute-start | bytes 393224 | tf_op jit(solution)/shard_map/ppermute | solution.py:245
  75.9 8.5 %collective-permute-start.29 = (bf16[16,4096]{1,0:T(8,128)(2,1)S(1)}, bf16[16,4096]{1,0:T(8,128)(2,1)S(1)}, u32[]{:S(2)}, u32[]{:S(2)}) collective-permute-start(bf16[16,4096]{1,0:T(8,128)(2,1)S(1)} %get-tuple-element.105), channel_id=1, source_target_pairs={{0,2},{1,3},{2,0},{3,1},{4,6},{5,7},{6,4},{7,5},{8,10},{9,11},{10,... | collective-permute-start | bytes 393224 | tf_op jit(solution)/shard_map/ppermute | solution.py:245
  77.2 10.5 %collective-permute-start.30 = (bf16[16,4096]{1,0:T(8,128)(2,1)S(1)}, bf16[16,4096]{1,0:T(8,128)(2,1)S(1)}, u32[]{:S(2)}, u32[]{:S(2)}) collective-permute-start(bf16[16,4096]{1,0:T(8,128)(2,1)S(1)} %get-tuple-element.107), channel_id=1, source_target_pairs={{0,4},{1,5},{2,6},{3,7},{4,0},{5,1},{6,2},{7,3},{8,12},{9,13},{10,... | collective-permute-start | bytes 393224 | tf_op jit(solution)/shard_map/ppermute | solution.py:245
  78.5 10.7 %collective-permute-start.31 = (bf16[16,4096]{1,0:T(8,128)(2,1)S(1)}, bf16[16,4096]{1,0:T(8,128)(2,1)S(1)}, u32[]{:S(2)}, u32[]{:S(2)}) collective-permute-start(bf16[16,4096]{1,0:T(8,128)(2,1)S(1)} %get-tuple-element.106), channel_id=1, source_target_pairs={{0,6},{1,7},{2,4},{3,5},{4,2},{5,3},{6,0},{7,1},{8,14},{9,15},{10,... | collective-permute-start | bytes 393224 | tf_op jit(solution)/shard_map/ppermute | solution.py:245
  82.1 7.9 %collective-permute-start.33 = (bf16[16,4096]{1,0:T(8,128)(2,1)S(1)}, bf16[16,4096]{1,0:T(8,128)(2,1)S(1)}, u32[]{:S(2)}, u32[]{:S(2)}) collective-permute-start(bf16[16,4096]{1,0:T(8,128)(2,1)S(1)} %get-tuple-element.115), channel_id=1, source_target_pairs={{0,2},{1,3},{2,0},{3,1},{4,6},{5,7},{6,4},{7,5},{8,10},{9,11},{10,... | collective-permute-start | bytes 393224 | tf_op jit(solution)/shard_map/ppermute | solution.py:245
  82.7 8.9 %collective-permute-start.34 = (bf16[16,4096]{1,0:T(8,128)(2,1)S(1)}, bf16[16,4096]{1,0:T(8,128)(2,1)S(1)}, u32[]{:S(2)}, u32[]{:S(2)}) collective-permute-start(bf16[16,4096]{1,0:T(8,128)(2,1)S(1)} %get-tuple-element.117), channel_id=1, source_target_pairs={{0,4},{1,5},{2,6},{3,7},{4,0},{5,1},{6,2},{7,3},{8,12},{9,13},{10,... | collective-permute-start | bytes 393224 | tf_op jit(solution)/shard_map/ppermute | solution.py:245
  84.4 12.3 %collective-permute-start.36 = (bf16[32,4096]{1,0:T(8,128)(2,1)S(1)}, bf16[32,4096]{1,0:T(8,128)(2,1)S(1)}, u32[]{:S(2)}, u32[]{:S(2)}) collective-permute-start(bf16[32,4096]{1,0:T(8,128)(2,1)S(1)} %convolution_convert_fusion.2), channel_id=1, source_target_pairs={{8,0},{9,1},{10,2},{11,3},{12,4},{13,5},{14,6},{15,7},{24,8},{25,9... | collective-permute-start | bytes 786440 | tf_op jit(solution)/shard_map/ppermute | solution.py:275
  87.7 6.9 %collective-permute-start.35 = (bf16[16,4096]{1,0:T(8,128)(2,1)S(1)}, bf16[16,4096]{1,0:T(8,128)(2,1)S(1)}, u32[]{:S(2)}, u32[]{:S(2)}) collective-permute-start(bf16[16,4096]{1,0:T(8,128)(2,1)S(1)} %get-tuple-element.116), channel_id=1, source_target_pairs={{0,6},{1,7},{2,4},{3,5},{4,2},{5,3},{6,0},{7,1},{8,14},{9,15},{10,... | collective-permute-start | bytes 393224 | tf_op jit(solution)/shard_map/ppermute | solution.py:245
  89.2 13.2 %collective-permute-start.22 = (bf16[16,4096]{1,0:T(8,128)(2,1)S(1)}, bf16[16,4096]{1,0:T(8,128)(2,1)S(1)}, u32[]{:S(2)}, u32[]{:S(2)}) collective-permute-start(bf16[16,4096]{1,0:T(8,128)(2,1)S(1)} %get-tuple-element.121), channel_id=1, source_target_pairs={{0,2},{1,3},{2,0},{3,1},{4,6},{5,7},{6,4},{7,5},{8,10},{9,11},{10,... | collective-permute-start | bytes 393224 | tf_op jit(solution)/shard_map/ppermute | solution.py:245
  90.0 12.4 %collective-permute-start.23 = (bf16[16,4096]{1,0:T(8,128)(2,1)S(1)}, bf16[16,4096]{1,0:T(8,128)(2,1)S(1)}, u32[]{:S(2)}, u32[]{:S(2)}) collective-permute-start(bf16[16,4096]{1,0:T(8,128)(2,1)S(1)} %get-tuple-element.123), channel_id=1, source_target_pairs={{0,4},{1,5},{2,6},{3,7},{4,0},{5,1},{6,2},{7,3},{8,12},{9,13},{10,... | collective-permute-start | bytes 393224 | tf_op jit(solution)/shard_map/ppermute | solution.py:245
  91.5 10.9 %collective-permute-start.24 = (bf16[16,4096]{1,0:T(8,128)(2,1)S(1)}, bf16[16,4096]{1,0:T(8,128)(2,1)S(1)}, u32[]{:S(2)}, u32[]{:S(2)}) collective-permute-start(bf16[16,4096]{1,0:T(8,128)(2,1)S(1)} %get-tuple-element.122), channel_id=1, source_target_pairs={{0,6},{1,7},{2,4},{3,5},{4,2},{5,3},{6,0},{7,1},{8,14},{9,15},{10,... | collective-permute-start | bytes 393224 | tf_op jit(solution)/shard_map/ppermute | solution.py:245
  94.6 9.5 %collective-permute-start.32 = (bf16[32,4096]{1,0:T(8,128)(2,1)S(1)}, bf16[32,4096]{1,0:T(8,128)(2,1)S(1)}, u32[]{:S(2)}, u32[]{:S(2)}) collective-permute-start(bf16[32,4096]{1,0:T(8,128)(2,1)S(1)} %convolution_convert_fusion.1), channel_id=1, source_target_pairs={{0,8},{1,9},{2,10},{3,11},{4,12},{5,13},{6,14},{7,15},{8,24},{9,25... | collective-permute-start | bytes 786440 | tf_op jit(solution)/shard_map/ppermute | solution.py:275
  97.0 9.1 %collective-permute-start.37 = (bf16[32,4096]{1,0:T(8,128)(2,1)S(1)}, bf16[32,4096]{1,0:T(8,128)(2,1)S(1)}, u32[]{:S(2)}, u32[]{:S(2)}) collective-permute-start(bf16[32,4096]{1,0:T(8,128)(2,1)S(1)} %fusion.18), channel_id=1, source_target_pairs={{8,0},{9,1},{10,2},{11,3},{12,4},{13,5},{14,6},{15,7},{24,8},{25,9... | collective-permute-start | bytes 786440 | tf_op jit(solution)/shard_map/ppermute | solution.py:275
  (11 other events, 42.7 us)

commit v4 on v2

--- a/solution.py
+++ b/solution.py
@@ -174,6 +174,10 @@
     return hidden, row_grad
 
 
+def turn(rows, flips):
+    return [rows[0]] + [lax.ppermute(rows[i + 1], AXES, flips[i]) for i in (0, 2, 1)]
+
+
 def ordered(held, got, w):
     near, far = got[w - 1][1:NEAR], got[w - 2][NEAR:] if w > 1 else []
     held, near, far = lax.optimization_barrier((held, near, far))
@@ -196,6 +200,7 @@
     node, place = lax.axis_index("node"), lax.axis_index("local")
     spot = jnp.stack([node // 2 * 2 * per_node, (node % 2) * per_node + place])
 
+    flips_back = [flips[i] for i in (0, 2, 1)]
     picks, got = [], []
     for w in range(depth - 1):
         if w == 0:
@@ -203,17 +208,14 @@
                 per_node, capacity, experts, spot, node_lists.T, expert_local.T, gate_fixed.T, tokens, out_grad
             )
         else:
-            ready = ordered(held, got, w)
-            held = ready
-            *chosen, pick = next_rows(top, codes, ready, False)
+            held = ordered(held, got, w)
+            *chosen, pick = next_rows(top, codes, held, False)
         picks.append(pick)
-        got.append([chosen[0]] + [lax.ppermute(c, AXES, flip) for c, flip in zip(chosen[1:], flips)])
+        got.append(turn(chosen, flips))
         held = lax.ppermute(held, AXES, ring)
     *chosen, pick = next_rows(top, codes, ordered(held, got, depth - 1), True)
     picks.append(pick)
-    ends = []
-    for part in (chosen[:4], chosen[4:]):
-        ends.append([part[0]] + [lax.ppermute(c, AXES, flip) for c, flip in zip(part[1:], flips)])
+    ends = [turn(part, flips) for part in (chosen[:4], chosen[4:])]
     most = lax.ppermute(jnp.concatenate([g[:, capacity:] for window in got for g in window], axis=1), AXES, flip_core)
 
     def gather(i, end):
@@ -227,35 +229,40 @@
     dy_rows = gather(1, ends[1])
     hidden, row_grad = gradients(gate_act, up_act, dy_rows, gate_weight[0], up_weight[0], down_weight[0])
 
+    ahead, order = depth // 2, []
+    for i in range(ahead):
+        order += [ahead - i] + ([ahead + 1 + i] if ahead + 1 + i < depth else [])
+    order.append(0)
     half = depth * 4 * capacity
     own = row_grad[:half].reshape(depth, 4, capacity, width)
     theirs = row_grad[half:].reshape(depth, 4, capacity, width)
-    last = lax.ppermute(theirs[depth - 1], AXES, flip_core)
-    rest = lax.ppermute(theirs[: depth - 1], AXES, flip_core)
-    came = {}
-    for w in reversed(range(depth)):
-        both = jnp.concatenate([own[w], last if w == depth - 1 else rest[w]], axis=1)
-        came[w] = [both[0]] + [lax.ppermute(both[i + 1], AXES, flip) for i, flip in enumerate(flips)]
-    down_local = None
-    total = None
-    for w in reversed(range(depth)):
-        partial = lax.dot_general(
-            picks[w], jnp.concatenate(came[w], axis=0), (((0,), (0,)), ((), ())), preferred_element_type=F32
-        )
-        if total is not None:
-            partial = partial + total.astype(F32)
-        total = partial.astype(BF16)
-        if w == 2:
+    cut = depth // 2
+    swapped = [lax.ppermute(theirs[:cut], AXES, flip_core), lax.ppermute(theirs[cut:], AXES, flip_core)]
+    swapped = [swapped[w // cut][w % cut] for w in range(depth)]
+    mine, sent = {}, {}
+    for w in order:
+        both = jnp.concatenate([own[w], swapped[w]], axis=1)
+        mine[w] = both[0]
+        sent[w] = [lax.ppermute(both[n], AXES, flip) for n, flip in ((1, flips[0]), (3, flips[1]), (2, flips[2]))]
+    sums = {w: [] for w in order}
+    for w in order:
+        from_x, from_y, from_xy = sent[w]
+        rows = jnp.concatenate([mine[w], from_x, from_y, from_xy], axis=0)
+        total = lax.dot_general(picks[w], rows, (((0,), (0,)), ((), ())), preferred_element_type=F32)
+        for part in sums[w]:
+            total = total + part.astype(F32)
+        total = total.astype(BF16)
+        if w == order[0]:
             total, hidden = lax.optimization_barrier((total, hidden))
             down_local = lax.dot_general(
                 hidden, dy_rows, (((0,), (0,)), ((), ())), preferred_element_type=F32
             ).astype(BF16)
+            total, sent[order[1]][:1] = lax.optimization_barrier((total, sent[order[1]][:1]))
+        if w == 0:
+            total, down_local = lax.optimization_barrier((total, down_local))
         if w:
-            if w == 1:
-                total, down_local = lax.optimization_barrier((total, down_local))
-            if w == 1:
-                total, came[w - 1][1:2] = lax.optimization_barrier((total, came[w - 1][1:2]))
-            total = lax.ppermute(total, AXES, back)
+            dest, perm = (w - 1, back) if w <= ahead else ((w + 1) % depth, ring)
+            sums[dest].append(lax.ppermute(total, AXES, perm))
     return total, down_local[None]
 
 

time: 112 us -> 107 us (0.955)
  starting transfers between devices: 45.3 us -> 42.8 us
  waiting for transfers between devices: 43.8 us -> 41.5 us
    ppermute x32, starting transfers between devices: 40.4 us -> 37.9 us  [the longest x15 18.6 us: turn(): lax.ppermute(rows[i + 1], AXES, flips[i])]
    ppermute x32, waiting for transfers between devices: 29.8 us -> 27.7 us  [the longest x15 16.8 us: turn(): lax.ppermute(rows[i + 1], AXES, flips[i])]
  transfers between devices with their start and end apart: 38 -> 38, of which waited for: 18 -> 17; matrix products, arithmetic and copies ran while one was open for 9% -> 9% of each run, Pallas kernels for 1% -> 1%
where the time goes in v4:
time: 107 us
  starting transfers between devices  42.8 us (40%)
  waiting for transfers between devices  41.5 us (39%)
  matrix products  15.8 us (15%)
  Pallas kernels  3.63 us (3%)
  local copies, waits for them, and re-layouts  1.78 us (2%)
  between operations  1.23 us (1%)
    ppermute x15, starting transfers between devices, turn(): lax.ppermute(rows[i + 1], AXES, flips[i])  18.6 us
    ppermute x15, waiting for transfers between devices, turn(): lax.ppermute(rows[i + 1], AXES, flips[i])  16.8 us
    ppermute x12, starting transfers between devices, body(): lax.ppermute(both[n], AXES, flip)  13.6 us
    ppermute x3, waiting for transfers between devices, body(): held = lax.ppermute(held, AXES, ring)  11.2 us
    ppermute x12, waiting for transfers between devices, body(): lax.ppermute(both[n], AXES, flip)  5.9 us
    ppermute x3, starting transfers between devices, body(): sums[dest].append(lax.ppermute(total, AXES, perm))  5.08 us
    dot_general x1, matrix products, body(): lax.dot_general(hidden, dy_rows, (((0,), (0,)), ((), ())), preferred_elem...  4.54 us
    ppermute x3, starting transfers between devices, body(): held = lax.ppermute(held, AXES, ring)  4.49 us
  transfers between devices with their start and end apart: 38, of which 17 were waited for; matrix products, arithmetic and copies ran while one was open for 9% of the time, Pallas kernels for 1%

profile of v4, /device:TPU:0, one launch (start us, length us, event | category | flops | bytes accessed | tf_op | source)
XLA Modules:
  0.0 107.1 jit_solution(13763542510748911493)
XLA Ops:
  0.7 2.1 %first_rows.1 = (bf16[2,16,4096]{2,1,0:T(8,128)(2,1)S(1)}, bf16[2,16,4096]{2,1,0:T(8,128)(2,1)S(1)}, bf16[2,16,4096]{2,1,0:T(8,128)(2,1)S(1)}, bf16[2,16,4096]{2...) custom-call(s32[2]{0:T(128)S(1)} %pad_add_fusion.spot, ...), custom_call_target="tpu_custom_call" | custom-call | tf_op jit(solution)/shard_map/first_rows/pallas_call | solution.py:133
  2.9 3.1 %collective-permute-start = (bf16[32,8320]{1,0:T(8,128)(2,1)S(1)}, bf16[32,8320]{1,0:T(8,128)(2,1)S(1)}, u32[]{:S(2)}, u32[]{:S(2)}) collective-permute-start(bf16[32,8320]{1,0:T(8,128)(2,1)S(1)} %get-tuple-element.52), channel_id=1, source_target_pairs={{0,8},{1,9},{2,10},{3,11},{4,12},{5,13},{6,14},{7,15},{8,24},{9,25... | collective-permute-start | bytes 1597448 | tf_op jit(solution)/shard_map/ppermute | solution.py:215
  7.4 1.5 %collective-permute-start.4 = (bf16[2,16,4096]{2,1,0:T(8,128)(2,1)S(1)}, bf16[2,16,4096]{2,1,0:T(8,128)(2,1)S(1)}, u32[]{:S(2)}, u32[]{:S(2)}) collective-permute-start(bf16[2,16,4096]{2,1,0:T(8,128)(2,1)S(1)} %get-tuple-element.58), channel_id=1, source_target_pairs={{0,6},{1,7},{2,4},{3,5},{4,2},{5,3},{6,0},{7,1},{8,14},{9,15},{10,... | collective-permute-start | bytes 786440 | tf_op jit(solution)/shard_map/ppermute | solution.py:178
  9.5 5.7 %collective-permute-done.1 = bf16[2,16,4096]{2,1,0:T(8,128)(2,1)S(1)} collective-permute-done((bf16[2,16,4096]{2,1,0:T(8,128)(2,1)S(1)}, bf16[2,16,4096]{2,1,0:T(8,128)(2,1)S(1)}, u32[]{:S(2)}, u32[]{:S(2)}) %collective-permute-start.1) | collective-permute-done | bytes 262176 | tf_op jit(solution)/shard_map/ppermute | solution.py:178
  15.2 3.9 %collective-permute-done.held = bf16[32,8320]{1,0:T(8,128)(2,1)S(1)} collective-permute-done((bf16[32,8320]{1,0:T(8,128)(2,1)S(1)}, bf16[32,8320]{1,0:T(8,128)(2,1)S(1)}, u32[]{:S(2)}, u32[]{:S(2)}) %collective-permute-start) | collective-permute-done | bytes 532512 | tf_op jit(solution)/shard_map/ppermute | solution.py:215
  20.4 1.6 %collective-permute-start.3 = (bf16[2,16,4096]{2,1,0:T(8,128)(2,1)S(1)}, bf16[2,16,4096]{2,1,0:T(8,128)(2,1)S(1)}, u32[]{:S(2)}, u32[]{:S(2)}) collective-permute-start(bf16[2,16,4096]{2,1,0:T(8,128)(2,1)S(1)} %get-tuple-element.57), channel_id=1, source_target_pairs={{0,2},{1,3},{2,0},{3,1},{4,6},{5,7},{6,4},{7,5},{8,10},{9,11},{10,... | collective-permute-start | bytes 786440 | tf_op jit(solution)/shard_map/ppermute | solution.py:178
  22.0 1.5 %collective-permute-start.8 = (bf16[2,16,4096]{2,1,0:T(8,128)(2,1)S(1)}, bf16[2,16,4096]{2,1,0:T(8,128)(2,1)S(1)}, u32[]{:S(2)}, u32[]{:S(2)}) collective-permute-start(bf16[2,16,4096]{2,1,0:T(8,128)(2,1)S(1)} %get-tuple-element.66), channel_id=1, source_target_pairs={{0,6},{1,7},{2,4},{3,5},{4,2},{5,3},{6,0},{7,1},{8,14},{9,15},{10,... | collective-permute-start | bytes 786440 | tf_op jit(solution)/shard_map/ppermute | solution.py:178
  24.1 5.6 %collective-permute-done.3 = bf16[2,16,4096]{2,1,0:T(8,128)(2,1)S(1)} collective-permute-done((bf16[2,16,4096]{2,1,0:T(8,128)(2,1)S(1)}, bf16[2,16,4096]{2,1,0:T(8,128)(2,1)S(1)}, u32[]{:S(2)}, u32[]{:S(2)}) %collective-permute-start.3) | collective-permute-done | bytes 262176 | tf_op jit(solution)/shard_map/ppermute | solution.py:178
  29.7 3.5 %collective-permute-done.2.held = bf16[32,8320]{1,0:T(8,128)(2,1)S(1)} collective-permute-done((bf16[32,8320]{1,0:T(8,128)(2,1)S(1)}, bf16[32,8320]{1,0:T(8,128)(2,1)S(1)}, u32[]{:S(2)}, u32[]{:S(2)}) %collective-permute-start.2) | collective-permute-done | bytes 532512 | tf_op jit(solution)/shard_map/ppermute | solution.py:215
  34.3 1.5 %collective-permute-start.7 = (bf16[2,16,4096]{2,1,0:T(8,128)(2,1)S(1)}, bf16[2,16,4096]{2,1,0:T(8,128)(2,1)S(1)}, u32[]{:S(2)}, u32[]{:S(2)}) collective-permute-start(bf16[2,16,4096]{2,1,0:T(8,128)(2,1)S(1)} %get-tuple-element.65), channel_id=1, source_target_pairs={{0,2},{1,3},{2,0},{3,1},{4,6},{5,7},{6,4},{7,5},{8,10},{9,11},{10,... | collective-permute-start | bytes 786440 | tf_op jit(solution)/shard_map/ppermute | solution.py:178
  35.8 1.5 %collective-permute-start.10 = (bf16[2,16,4096]{2,1,0:T(8,128)(2,1)S(1)}, bf16[2,16,4096]{2,1,0:T(8,128)(2,1)S(1)}, u32[]{:S(2)}, u32[]{:S(2)}) collective-permute-start(bf16[2,16,4096]{2,1,0:T(8,128)(2,1)S(1)} %get-tuple-element.72), channel_id=1, source_target_pairs={{0,6},{1,7},{2,4},{3,5},{4,2},{5,3},{6,0},{7,1},{8,14},{9,15},{10,... | collective-permute-start | bytes 786440 | tf_op jit(solution)/shard_map/ppermute | solution.py:178
  38.0 5.2 %collective-permute-done.7 = bf16[2,16,4096]{2,1,0:T(8,128)(2,1)S(1)} collective-permute-done((bf16[2,16,4096]{2,1,0:T(8,128)(2,1)S(1)}, bf16[2,16,4096]{2,1,0:T(8,128)(2,1)S(1)}, u32[]{:S(2)}, u32[]{:S(2)}) %collective-permute-start.7) | collective-permute-done | bytes 262176 | tf_op jit(solution)/shard_map/ppermute | solution.py:178
  43.3 3.8 %collective-permute-done.6.held = bf16[32,8320]{1,0:T(8,128)(2,1)S(1)} collective-permute-done((bf16[32,8320]{1,0:T(8,128)(2,1)S(1)}, bf16[32,8320]{1,0:T(8,128)(2,1)S(1)}, u32[]{:S(2)}, u32[]{:S(2)}) %collective-permute-start.6) | collective-permute-done | bytes 532512 | tf_op jit(solution)/shard_map/ppermute | solution.py:215
  48.5 1.5 %collective-permute-start.13 = (bf16[16,4096]{1,0:T(8,128)(2,1)S(1)}, bf16[16,4096]{1,0:T(8,128)(2,1)S(1)}, u32[]{:S(2)}, u32[]{:S(2)}) collective-permute-start(bf16[16,4096]{1,0:T(8,128)(2,1)S(1)} %get-tuple-element.77), channel_id=1, source_target_pairs={{0,6},{1,7},{2,4},{3,5},{4,2},{5,3},{6,0},{7,1},{8,14},{9,15},{10,... | collective-permute-start | bytes 393224 | tf_op jit(solution)/shard_map/ppermute | solution.py:178
  52.6 1.9 %collective-permute-start.18 = (bf16[16,4096]{1,0:T(8,128)(2,1)S(1)}, bf16[16,4096]{1,0:T(8,128)(2,1)S(1)}, u32[]{:S(2)}, u32[]{:S(2)}) collective-permute-start(bf16[16,4096]{1,0:T(8,128)(2,1)S(1)} %get-tuple-element.81), channel_id=1, source_target_pairs={{0,6},{1,7},{2,4},{3,5},{4,2},{5,3},{6,0},{7,1},{8,14},{9,15},{10,... | collective-permute-start | bytes 393224 | tf_op jit(solution)/shard_map/ppermute | solution.py:178
  54.5 1.5 %collective-permute-start.19 = (bf16[16,4096]{1,0:T(8,128)(2,1)S(1)}, bf16[16,4096]{1,0:T(8,128)(2,1)S(1)}, u32[]{:S(2)}, u32[]{:S(2)}) collective-permute-start(bf16[16,4096]{1,0:T(8,128)(2,1)S(1)} %get-tuple-element.82), channel_id=1, source_target_pairs={{0,4},{1,5},{2,6},{3,7},{4,0},{5,1},{6,2},{7,3},{8,12},{9,13},{10,... | collective-permute-start | bytes 393224 | tf_op jit(solution)/shard_map/ppermute | solution.py:178
  57.8 1.8 %fusion.4 = f32[256,768]{1,0:T(8,128)S(1)} fusion(bf16[256,4096]{1,0:T(8,128)(2,1)S(1)} %constant_dynamic-update-slice_fusion, bf16[1,4096,768]{2,1,0:T(8,128)(2,1)S(1)} %copy-done), kind=kOutput, calls=%fused_computation.5 | convolution fusion | flops 1610612736 | bytes 9175040 | tf_op jit(solution)/shard_map/dot_general | solution.py:159
  60.6 1.8 %fusion.8 = f32[256,768]{1,0:T(8,128)S(1)} fusion(bf16[256,4096]{1,0:T(8,128)(2,1)S(1)} %constant_dynamic-update-slice_fusion, bf16[1,4096,768]{2,1,0:T(8,128)(2,1)S(1)} %bitcast.147), kind=kOutput, calls=%fused_computation.9 | convolution fusion | flops 1610612736 | bytes 9175040 | tf_op jit(solution)/shard_map/dot_general | solution.py:158
  64.2 2.1 %fusion = f32[256,768]{1,0:T(8,128)S(1)} fusion(bf16[256,4096]{1,0:T(8,128)(2,1)S(1)} %constant_dynamic-update-slice_fusion.17, bf16[1,768,4096]{2,1,0:T(8,128)(2,1)S(1)} %bitcast.155), kind=kOutput, calls=%fused_computation.1 | convolution fusion | flops 1610612736 | bytes 9175040 | tf_op jit(solution)/shard_map/dot_general | solution.py:167
  66.3 1.9 %fusion.2 = f32[256,4096]{1,0:T(8,128)S(1)} fusion(bf16[1,4096,768]{2,1,0:T(8,128)(2,1)S(1)} %copy-done, f32[256,768]{1,0:T(8,128)S(1)} %fusion, f32[256,768]{1,0:T(8,128)S(1)} %fusion.8), kind=kOutput, calls=%fused_computation.3 | convolution fusion | flops 1611792384 | bytes 12058624 | tf_op jit(solution)/shard_map/dot_general | solution.py:172
  68.1 2.0 %fusion.13 = bf16[256,4096]{1,0:T(8,128)(2,1)S(1)} fusion(f32[256,4096]{1,0:T(8,128)S(1)} %fusion.2, bf16[1,4096,768]{2,1,0:T(8,128)(2,1)S(1)} %bitcast.147, f32[256,768]{1,0:T(8,128)S(1)} %fusion.8, f32[256,768]{1,0:T(8,128)S(1)} %fusion, f32[256,768]{1,0:T(8,128)S(1)} %fusion.4), kind=kOutput, calls=%fused_computation.12 | convolution fusion | flops 1614675968 | bytes 14942208 | tf_op jit(solution)/shard_map/dot_general | solution.py:171
  74.3 1.5 %collective-permute-start.28 = (bf16[16,4096]{1,0:T(8,128)(2,1)S(1)}, bf16[16,4096]{1,0:T(8,128)(2,1)S(1)}, u32[]{:S(2)}, u32[]{:S(2)}) collective-permute-start(bf16[16,4096]{1,0:T(8,128)(2,1)S(1)} %get-tuple-element.112), channel_id=1, source_target_pairs={{0,6},{1,7},{2,4},{3,5},{4,2},{5,3},{6,0},{7,1},{8,14},{9,15},{10,... | collective-permute-start | bytes 393224 | tf_op jit(solution)/shard_map/ppermute | solution.py:246
  79.8 2.3 %collective-permute-done.27 = bf16[16,4096]{1,0:T(8,128)(2,1)S(1)} collective-permute-done((bf16[16,4096]{1,0:T(8,128)(2,1)S(1)}, bf16[16,4096]{1,0:T(8,128)(2,1)S(1)}, u32[]{:S(2)}, u32[]{:S(2)}) %collective-permute-start.27) | collective-permute-done | bytes 131104 | tf_op jit(solution)/shard_map/ppermute | solution.py:246
  82.7 1.5 %collective-permute-start.34 = (bf16[16,4096]{1,0:T(8,128)(2,1)S(1)}, bf16[16,4096]{1,0:T(8,128)(2,1)S(1)}, u32[]{:S(2)}, u32[]{:S(2)}) collective-permute-start(bf16[16,4096]{1,0:T(8,128)(2,1)S(1)} %get-tuple-element.117), channel_id=1, source_target_pairs={{0,4},{1,5},{2,6},{3,7},{4,0},{5,1},{6,2},{7,3},{8,12},{9,13},{10,... | collective-permute-start | bytes 393224 | tf_op jit(solution)/shard_map/ppermute | solution.py:246
  84.4 2.1 %collective-permute-start.36 = (bf16[32,4096]{1,0:T(8,128)(2,1)S(1)}, bf16[32,4096]{1,0:T(8,128)(2,1)S(1)}, u32[]{:S(2)}, u32[]{:S(2)}) collective-permute-start(bf16[32,4096]{1,0:T(8,128)(2,1)S(1)} %convolution_convert_fusion.2), channel_id=1, source_target_pairs={{8,0},{9,1},{10,2},{11,3},{12,4},{13,5},{14,6},{15,7},{24,8},{25,9... | collective-permute-start | bytes 786440 | tf_op jit(solution)/shard_map/ppermute | solution.py:265
  87.7 1.5 %collective-permute-start.35 = (bf16[16,4096]{1,0:T(8,128)(2,1)S(1)}, bf16[16,4096]{1,0:T(8,128)(2,1)S(1)}, u32[]{:S(2)}, u32[]{:S(2)}) collective-permute-start(bf16[16,4096]{1,0:T(8,128)(2,1)S(1)} %get-tuple-element.116), channel_id=1, source_target_pairs={{0,6},{1,7},{2,4},{3,5},{4,2},{5,3},{6,0},{7,1},{8,14},{9,15},{10,... | collective-permute-start | bytes 393224 | tf_op jit(solution)/shard_map/ppermute | solution.py:246
  90.0 1.5 %collective-permute-start.23 = (bf16[16,4096]{1,0:T(8,128)(2,1)S(1)}, bf16[16,4096]{1,0:T(8,128)(2,1)S(1)}, u32[]{:S(2)}, u32[]{:S(2)}) collective-permute-start(bf16[16,4096]{1,0:T(8,128)(2,1)S(1)} %get-tuple-element.123), channel_id=1, source_target_pairs={{0,4},{1,5},{2,6},{3,7},{4,0},{5,1},{6,2},{7,3},{8,12},{9,13},{10,... | collective-permute-start | bytes 393224 | tf_op jit(solution)/shard_map/ppermute | solution.py:246
  93.0 1.6 %collective-permute-done.35 = bf16[16,4096]{1,0:T(8,128)(2,1)S(1)} collective-permute-done((bf16[16,4096]{1,0:T(8,128)(2,1)S(1)}, bf16[16,4096]{1,0:T(8,128)(2,1)S(1)}, u32[]{:S(2)}, u32[]{:S(2)}) %collective-permute-start.35) | collective-permute-done | bytes 131104 | tf_op jit(solution)/shard_map/ppermute | solution.py:246
  94.6 2.1 %collective-permute-start.32 = (bf16[32,4096]{1,0:T(8,128)(2,1)S(1)}, bf16[32,4096]{1,0:T(8,128)(2,1)S(1)}, u32[]{:S(2)}, u32[]{:S(2)}) collective-permute-start(bf16[32,4096]{1,0:T(8,128)(2,1)S(1)} %convolution_convert_fusion.1), channel_id=1, source_target_pairs={{0,8},{1,9},{2,10},{3,11},{4,12},{5,13},{6,14},{7,15},{8,24},{9,25... | collective-permute-start | bytes 786440 | tf_op jit(solution)/shard_map/ppermute | solution.py:265
  97.9 4.5 %convolution_convert_fusion = bf16[768,4096]{1,0:T(8,128)(2,1)} fusion(bf16[256,768]{1,0:T(8,128)(2,1)S(1)} %multiply_convert_fusion, bf16[256,4096]{1,0:T(8,128)(2,1)S(1)} %constant_dynamic-update-slice_fusion.17), kind=kOutput, calls=%fused_computation | convolution fusion | flops 1613758464 | bytes 8781824 | tf_op jit(solution)/shard_map/dot_general | solution.py:257
  102.4 1.7 %collective-permute-done.32 = bf16[32,4096]{1,0:T(8,128)(2,1)S(1)} collective-permute-done((bf16[32,4096]{1,0:T(8,128)(2,1)S(1)}, bf16[32,4096]{1,0:T(8,128)(2,1)S(1)}, u32[]{:S(2)}, u32[]{:S(2)}) %collective-permute-start.32) | collective-permute-done | bytes 262176 | tf_op jit(solution)/shard_map/ppermute | solution.py:265
  104.1 2.0 %collective-permute-done.37 = bf16[32,4096]{1,0:T(8,128)(2,1)S(1)} collective-permute-done((bf16[32,4096]{1,0:T(8,128)(2,1)S(1)}, bf16[32,4096]{1,0:T(8,128)(2,1)S(1)}, u32[]{:S(2)}, u32[]{:S(2)}) %collective-permute-start.37) | collective-permute-done | bytes 262176 | tf_op jit(solution)/shard_map/ppermute | solution.py:265
  (118 shorter events, 28.5 us)
Async XLA Ops:
  2.9 16.2 %collective-permute-start = (bf16[32,8320]{1,0:T(8,128)(2,1)S(1)}, bf16[32,8320]{1,0:T(8,128)(2,1)S(1)}, u32[]{:S(2)}, u32[]{:S(2)}) collective-permute-start(bf16[32,8320]{1,0:T(8,128)(2,1)S(1)} %get-tuple-element.52), channel_id=1, source_target_pairs={{0,8},{1,9},{2,10},{3,11},{4,12},{5,13},{6,14},{7,15},{8,24},{9,25... | collective-permute-start | bytes 1597448 | tf_op jit(solution)/shard_map/ppermute | solution.py:215
  6.0 9.2 %collective-permute-start.1 = (bf16[2,16,4096]{2,1,0:T(8,128)(2,1)S(1)}, bf16[2,16,4096]{2,1,0:T(8,128)(2,1)S(1)}, u32[]{:S(2)}, u32[]{:S(2)}) collective-permute-start(bf16[2,16,4096]{2,1,0:T(8,128)(2,1)S(1)} %get-tuple-element.53), channel_id=1, source_target_pairs={{0,2},{1,3},{2,0},{3,1},{4,6},{5,7},{6,4},{7,5},{8,10},{9,11},{10,... | collective-permute-start | bytes 786440 | tf_op jit(solution)/shard_map/ppermute | solution.py:178
  7.4 16.0 %collective-permute-start.4 = (bf16[2,16,4096]{2,1,0:T(8,128)(2,1)S(1)}, bf16[2,16,4096]{2,1,0:T(8,128)(2,1)S(1)}, u32[]{:S(2)}, u32[]{:S(2)}) collective-permute-start(bf16[2,16,4096]{2,1,0:T(8,128)(2,1)S(1)} %get-tuple-element.58), channel_id=1, source_target_pairs={{0,6},{1,7},{2,4},{3,5},{4,2},{5,3},{6,0},{7,1},{8,14},{9,15},{10,... | collective-permute-start | bytes 786440 | tf_op jit(solution)/shard_map/ppermute | solution.py:178
  8.9 15.1 %collective-permute-start.5 = (bf16[2,16,4096]{2,1,0:T(8,128)(2,1)S(1)}, bf16[2,16,4096]{2,1,0:T(8,128)(2,1)S(1)}, u32[]{:S(2)}, u32[]{:S(2)}) collective-permute-start(bf16[2,16,4096]{2,1,0:T(8,128)(2,1)S(1)} %get-tuple-element.59), channel_id=1, source_target_pairs={{0,4},{1,5},{2,6},{3,7},{4,0},{5,1},{6,2},{7,3},{8,12},{9,13},{10,... | collective-permute-start | bytes 786440 | tf_op jit(solution)/shard_map/ppermute | solution.py:178
  19.1 14.2 %collective-permute-start.2 = (bf16[32,8320]{1,0:T(8,128)(2,1)S(1)}, bf16[32,8320]{1,0:T(8,128)(2,1)S(1)}, u32[]{:S(2)}, u32[]{:S(2)}) collective-permute-start(bf16[32,8320]{1,0:T(8,128)(2,1)S(1)} %collective-permute-done.held), channel_id=1, source_target_pairs={{0,8},{1,9},{2,10},{3,11},{4,12},{5,13},{6,14},{7,15},{8,24},{9,25... | collective-permute-start | bytes 1597448 | tf_op jit(solution)/shard_map/ppermute | solution.py:215
  20.4 9.3 %collective-permute-start.3 = (bf16[2,16,4096]{2,1,0:T(8,128)(2,1)S(1)}, bf16[2,16,4096]{2,1,0:T(8,128)(2,1)S(1)}, u32[]{:S(2)}, u32[]{:S(2)}) collective-permute-start(bf16[2,16,4096]{2,1,0:T(8,128)(2,1)S(1)} %get-tuple-element.57), channel_id=1, source_target_pairs={{0,2},{1,3},{2,0},{3,1},{4,6},{5,7},{6,4},{7,5},{8,10},{9,11},{10,... | collective-permute-start | bytes 786440 | tf_op jit(solution)/shard_map/ppermute | solution.py:178
  22.0 15.5 %collective-permute-start.8 = (bf16[2,16,4096]{2,1,0:T(8,128)(2,1)S(1)}, bf16[2,16,4096]{2,1,0:T(8,128)(2,1)S(1)}, u32[]{:S(2)}, u32[]{:S(2)}) collective-permute-start(bf16[2,16,4096]{2,1,0:T(8,128)(2,1)S(1)} %get-tuple-element.66), channel_id=1, source_target_pairs={{0,6},{1,7},{2,4},{3,5},{4,2},{5,3},{6,0},{7,1},{8,14},{9,15},{10,... | collective-permute-start | bytes 786440 | tf_op jit(solution)/shard_map/ppermute | solution.py:178
  23.5 14.5 %collective-permute-start.9 = (bf16[2,16,4096]{2,1,0:T(8,128)(2,1)S(1)}, bf16[2,16,4096]{2,1,0:T(8,128)(2,1)S(1)}, u32[]{:S(2)}, u32[]{:S(2)}) collective-permute-start(bf16[2,16,4096]{2,1,0:T(8,128)(2,1)S(1)} %get-tuple-element.67), channel_id=1, source_target_pairs={{0,4},{1,5},{2,6},{3,7},{4,0},{5,1},{6,2},{7,3},{8,12},{9,13},{10,... | collective-permute-start | bytes 786440 | tf_op jit(solution)/shard_map/ppermute | solution.py:178
  33.7 13.3 %collective-permute-start.6 = (bf16[32,8320]{1,0:T(8,128)(2,1)S(1)}, bf16[32,8320]{1,0:T(8,128)(2,1)S(1)}, u32[]{:S(2)}, u32[]{:S(2)}) collective-permute-start(bf16[32,8320]{1,0:T(8,128)(2,1)S(1)} %collective-permute-done.2.held), channel_id=1, source_target_pairs={{0,8},{1,9},{2,10},{3,11},{4,12},{5,13},{6,14},{7,15},{8,24},{9,25... | collective-permute-start | bytes 1597448 | tf_op jit(solution)/shard_map/ppermute | solution.py:215
  34.3 8.9 %collective-permute-start.7 = (bf16[2,16,4096]{2,1,0:T(8,128)(2,1)S(1)}, bf16[2,16,4096]{2,1,0:T(8,128)(2,1)S(1)}, u32[]{:S(2)}, u32[]{:S(2)}) collective-permute-start(bf16[2,16,4096]{2,1,0:T(8,128)(2,1)S(1)} %get-tuple-element.65), channel_id=1, source_target_pairs={{0,2},{1,3},{2,0},{3,1},{4,6},{5,7},{6,4},{7,5},{8,10},{9,11},{10,... | collective-permute-start | bytes 786440 | tf_op jit(solution)/shard_map/ppermute | solution.py:178
  35.8 15.4 %collective-permute-start.10 = (bf16[2,16,4096]{2,1,0:T(8,128)(2,1)S(1)}, bf16[2,16,4096]{2,1,0:T(8,128)(2,1)S(1)}, u32[]{:S(2)}, u32[]{:S(2)}) collective-permute-start(bf16[2,16,4096]{2,1,0:T(8,128)(2,1)S(1)} %get-tuple-element.72), channel_id=1, source_target_pairs={{0,6},{1,7},{2,4},{3,5},{4,2},{5,3},{6,0},{7,1},{8,14},{9,15},{10,... | collective-permute-start | bytes 786440 | tf_op jit(solution)/shard_map/ppermute | solution.py:178
  37.5 13.8 %collective-permute-start.11 = (bf16[2,16,4096]{2,1,0:T(8,128)(2,1)S(1)}, bf16[2,16,4096]{2,1,0:T(8,128)(2,1)S(1)}, u32[]{:S(2)}, u32[]{:S(2)}) collective-permute-start(bf16[2,16,4096]{2,1,0:T(8,128)(2,1)S(1)} %get-tuple-element.73), channel_id=1, source_target_pairs={{0,4},{1,5},{2,6},{3,7},{4,0},{5,1},{6,2},{7,3},{8,12},{9,13},{10,... | collective-permute-start | bytes 786440 | tf_op jit(solution)/shard_map/ppermute | solution.py:178
  50.0 6.0 %collective-permute-start.14 = (bf16[16,4096]{1,0:T(8,128)(2,1)S(1)}, bf16[16,4096]{1,0:T(8,128)(2,1)S(1)}, u32[]{:S(2)}, u32[]{:S(2)}) collective-permute-start(bf16[16,4096]{1,0:T(8,128)(2,1)S(1)} %get-tuple-element.78), channel_id=1, source_target_pairs={{0,4},{1,5},{2,6},{3,7},{4,0},{5,1},{6,2},{7,3},{8,12},{9,13},{10,... | collective-permute-start | bytes 393224 | tf_op jit(solution)/shard_map/ppermute | solution.py:178
  51.3 11.1 %collective-permute-start.17 = (bf16[16,4096]{1,0:T(8,128)(2,1)S(1)}, bf16[16,4096]{1,0:T(8,128)(2,1)S(1)}, u32[]{:S(2)}, u32[]{:S(2)}) collective-permute-start(bf16[16,4096]{1,0:T(8,128)(2,1)S(1)} %get-tuple-element.80), channel_id=1, source_target_pairs={{0,2},{1,3},{2,0},{3,1},{4,6},{5,7},{6,4},{7,5},{8,10},{9,11},{10,... | collective-permute-start | bytes 393224 | tf_op jit(solution)/shard_map/ppermute | solution.py:178
  52.6 9.8 %collective-permute-start.18 = (bf16[16,4096]{1,0:T(8,128)(2,1)S(1)}, bf16[16,4096]{1,0:T(8,128)(2,1)S(1)}, u32[]{:S(2)}, u32[]{:S(2)}) collective-permute-start(bf16[16,4096]{1,0:T(8,128)(2,1)S(1)} %get-tuple-element.81), channel_id=1, source_target_pairs={{0,6},{1,7},{2,4},{3,5},{4,2},{5,3},{6,0},{7,1},{8,14},{9,15},{10,... | collective-permute-start | bytes 393224 | tf_op jit(solution)/shard_map/ppermute | solution.py:178
  54.5 7.9 %collective-permute-start.19 = (bf16[16,4096]{1,0:T(8,128)(2,1)S(1)}, bf16[16,4096]{1,0:T(8,128)(2,1)S(1)}, u32[]{:S(2)}, u32[]{:S(2)}) collective-permute-start(bf16[16,4096]{1,0:T(8,128)(2,1)S(1)} %get-tuple-element.82), channel_id=1, source_target_pairs={{0,4},{1,5},{2,6},{3,7},{4,0},{5,1},{6,2},{7,3},{8,12},{9,13},{10,... | collective-permute-start | bytes 393224 | tf_op jit(solution)/shard_map/ppermute | solution.py:178
  70.4 6.8 %collective-permute-start.21 = (bf16[2,4,8,4096]{3,2,1,0:T(8,128)(2,1)S(1)}, bf16[2,4,8,4096]{3,2,1,0:T(8,128)(2,1)S(1)}, u32[]{:S(2)}, u32[]{:S(2)}) collective-permute-start(bf16[2,4,8,4096]{3,2,1,0:T(8,128)(2,1)S(1)} %bitcast.149), channel_id=1, source_target_pairs={{0,1},{1,0},{2,3},{3,2},{4,5},{5,4},{6,7},{7,6},{8,9},{9,8},{10,11... | collective-permute-start | bytes 1572872 | tf_op jit(solution)/shard_map/ppermute | solution.py:240
  72.3 6.2 %collective-permute-start.26 = (bf16[16,4096]{1,0:T(8,128)(2,1)S(1)}, bf16[16,4096]{1,0:T(8,128)(2,1)S(1)}, u32[]{:S(2)}, u32[]{:S(2)}) collective-permute-start(bf16[16,4096]{1,0:T(8,128)(2,1)S(1)} %get-tuple-element.111), channel_id=1, source_target_pairs={{0,2},{1,3},{2,0},{3,1},{4,6},{5,7},{6,4},{7,5},{8,10},{9,11},{10,... | collective-permute-start | bytes 393224 | tf_op jit(solution)/shard_map/ppermute | solution.py:246
  73.6 8.5 %collective-permute-start.27 = (bf16[16,4096]{1,0:T(8,128)(2,1)S(1)}, bf16[16,4096]{1,0:T(8,128)(2,1)S(1)}, u32[]{:S(2)}, u32[]{:S(2)}) collective-permute-start(bf16[16,4096]{1,0:T(8,128)(2,1)S(1)} %get-tuple-element.113), channel_id=1, source_target_pairs={{0,4},{1,5},{2,6},{3,7},{4,0},{5,1},{6,2},{7,3},{8,12},{9,13},{10,... | collective-permute-start | bytes 393224 | tf_op jit(solution)/shard_map/ppermute | solution.py:246
  74.3 8.4 %collective-permute-start.28 = (bf16[16,4096]{1,0:T(8,128)(2,1)S(1)}, bf16[16,4096]{1,0:T(8,128)(2,1)S(1)}, u32[]{:S(2)}, u32[]{:S(2)}) collective-permute-start(bf16[16,4096]{1,0:T(8,128)(2,1)S(1)} %get-tuple-element.112), channel_id=1, source_target_pairs={{0,6},{1,7},{2,4},{3,5},{4,2},{5,3},{6,0},{7,1},{8,14},{9,15},{10,... | collective-permute-start | bytes 393224 | tf_op jit(solution)/shard_map/ppermute | solution.py:246
  75.9 8.5 %collective-permute-start.29 = (bf16[16,4096]{1,0:T(8,128)(2,1)S(1)}, bf16[16,4096]{1,0:T(8,128)(2,1)S(1)}, u32[]{:S(2)}, u32[]{:S(2)}) collective-permute-start(bf16[16,4096]{1,0:T(8,128)(2,1)S(1)} %get-tuple-element.105), channel_id=1, source_target_pairs={{0,2},{1,3},{2,0},{3,1},{4,6},{5,7},{6,4},{7,5},{8,10},{9,11},{10,... | collective-permute-start | bytes 393224 | tf_op jit(solution)/shard_map/ppermute | solution.py:246
  77.2 10.5 %collective-permute-start.30 = (bf16[16,4096]{1,0:T(8,128)(2,1)S(1)}, bf16[16,4096]{1,0:T(8,128)(2,1)S(1)}, u32[]{:S(2)}, u32[]{:S(2)}) collective-permute-start(bf16[16,4096]{1,0:T(8,128)(2,1)S(1)} %get-tuple-element.107), channel_id=1, source_target_pairs={{0,4},{1,5},{2,6},{3,7},{4,0},{5,1},{6,2},{7,3},{8,12},{9,13},{10,... | collective-permute-start | bytes 393224 | tf_op jit(solution)/shard_map/ppermute | solution.py:246
  78.5 10.7 %collective-permute-start.31 = (bf16[16,4096]{1,0:T(8,128)(2,1)S(1)}, bf16[16,4096]{1,0:T(8,128)(2,1)S(1)}, u32[]{:S(2)}, u32[]{:S(2)}) collective-permute-start(bf16[16,4096]{1,0:T(8,128)(2,1)S(1)} %get-tuple-element.106), channel_id=1, source_target_pairs={{0,6},{1,7},{2,4},{3,5},{4,2},{5,3},{6,0},{7,1},{8,14},{9,15},{10,... | collective-permute-start | bytes 393224 | tf_op jit(solution)/shard_map/ppermute | solution.py:246
  82.1 7.9 %collective-permute-start.33 = (bf16[16,4096]{1,0:T(8,128)(2,1)S(1)}, bf16[16,4096]{1,0:T(8,128)(2,1)S(1)}, u32[]{:S(2)}, u32[]{:S(2)}) collective-permute-start(bf16[16,4096]{1,0:T(8,128)(2,1)S(1)} %get-tuple-element.115), channel_id=1, source_target_pairs={{0,2},{1,3},{2,0},{3,1},{4,6},{5,7},{6,4},{7,5},{8,10},{9,11},{10,... | collective-permute-start | bytes 393224 | tf_op jit(solution)/shard_map/ppermute | solution.py:246
  82.7 8.9 %collective-permute-start.34 = (bf16[16,4096]{1,0:T(8,128)(2,1)S(1)}, bf16[16,4096]{1,0:T(8,128)(2,1)S(1)}, u32[]{:S(2)}, u32[]{:S(2)}) collective-permute-start(bf16[16,4096]{1,0:T(8,128)(2,1)S(1)} %get-tuple-element.117), channel_id=1, source_target_pairs={{0,4},{1,5},{2,6},{3,7},{4,0},{5,1},{6,2},{7,3},{8,12},{9,13},{10,... | collective-permute-start | bytes 393224 | tf_op jit(solution)/shard_map/ppermute | solution.py:246
  84.4 12.3 %collective-permute-start.36 = (bf16[32,4096]{1,0:T(8,128)(2,1)S(1)}, bf16[32,4096]{1,0:T(8,128)(2,1)S(1)}, u32[]{:S(2)}, u32[]{:S(2)}) collective-permute-start(bf16[32,4096]{1,0:T(8,128)(2,1)S(1)} %convolution_convert_fusion.2), channel_id=1, source_target_pairs={{8,0},{9,1},{10,2},{11,3},{12,4},{13,5},{14,6},{15,7},{24,8},{25,9... | collective-permute-start | bytes 786440 | tf_op jit(solution)/shard_map/ppermute | solution.py:265
  87.7 6.9 %collective-permute-start.35 = (bf16[16,4096]{1,0:T(8,128)(2,1)S(1)}, bf16[16,4096]{1,0:T(8,128)(2,1)S(1)}, u32[]{:S(2)}, u32[]{:S(2)}) collective-permute-start(bf16[16,4096]{1,0:T(8,128)(2,1)S(1)} %get-tuple-element.116), channel_id=1, source_target_pairs={{0,6},{1,7},{2,4},{3,5},{4,2},{5,3},{6,0},{7,1},{8,14},{9,15},{10,... | collective-permute-start | bytes 393224 | tf_op jit(solution)/shard_map/ppermute | solution.py:246
  89.2 13.2 %collective-permute-start.22 = (bf16[16,4096]{1,0:T(8,128)(2,1)S(1)}, bf16[16,4096]{1,0:T(8,128)(2,1)S(1)}, u32[]{:S(2)}, u32[]{:S(2)}) collective-permute-start(bf16[16,4096]{1,0:T(8,128)(2,1)S(1)} %get-tuple-element.121), channel_id=1, source_target_pairs={{0,2},{1,3},{2,0},{3,1},{4,6},{5,7},{6,4},{7,5},{8,10},{9,11},{10,... | collective-permute-start | bytes 393224 | tf_op jit(solution)/shard_map/ppermute | solution.py:246
  90.0 12.4 %collective-permute-start.23 = (bf16[16,4096]{1,0:T(8,128)(2,1)S(1)}, bf16[16,4096]{1,0:T(8,128)(2,1)S(1)}, u32[]{:S(2)}, u32[]{:S(2)}) collective-permute-start(bf16[16,4096]{1,0:T(8,128)(2,1)S(1)} %get-tuple-element.123), channel_id=1, source_target_pairs={{0,4},{1,5},{2,6},{3,7},{4,0},{5,1},{6,2},{7,3},{8,12},{9,13},{10,... | collective-permute-start | bytes 393224 | tf_op jit(solution)/shard_map/ppermute | solution.py:246
  91.5 10.9 %collective-permute-start.24 = (bf16[16,4096]{1,0:T(8,128)(2,1)S(1)}, bf16[16,4096]{1,0:T(8,128)(2,1)S(1)}, u32[]{:S(2)}, u32[]{:S(2)}) collective-permute-start(bf16[16,4096]{1,0:T(8,128)(2,1)S(1)} %get-tuple-element.122), channel_id=1, source_target_pairs={{0,6},{1,7},{2,4},{3,5},{4,2},{5,3},{6,0},{7,1},{8,14},{9,15},{10,... | collective-permute-start | bytes 393224 | tf_op jit(solution)/shard_map/ppermute | solution.py:246
  94.6 9.5 %collective-permute-start.32 = (bf16[32,4096]{1,0:T(8,128)(2,1)S(1)}, bf16[32,4096]{1,0:T(8,128)(2,1)S(1)}, u32[]{:S(2)}, u32[]{:S(2)}) collective-permute-start(bf16[32,4096]{1,0:T(8,128)(2,1)S(1)} %convolution_convert_fusion.1), channel_id=1, source_target_pairs={{0,8},{1,9},{2,10},{3,11},{4,12},{5,13},{6,14},{7,15},{8,24},{9,25... | collective-permute-start | bytes 786440 | tf_op jit(solution)/shard_map/ppermute | solution.py:265
  97.0 9.1 %collective-permute-start.37 = (bf16[32,4096]{1,0:T(8,128)(2,1)S(1)}, bf16[32,4096]{1,0:T(8,128)(2,1)S(1)}, u32[]{:S(2)}, u32[]{:S(2)}) collective-permute-start(bf16[32,4096]{1,0:T(8,128)(2,1)S(1)} %fusion.18), channel_id=1, source_target_pairs={{8,0},{9,1},{10,2},{11,3},{12,4},{13,5},{14,6},{15,7},{24,8},{25,9... | collective-permute-start | bytes 786440 | tf_op jit(solution)/shard_map/ppermute | solution.py:265
  (11 other events, 42.7 us)

commit v5 on v4

--- a/solution.py
+++ b/solution.py
@@ -34,10 +34,17 @@
     return depth, ring, back, (flip_x, flip_y, flip_xy), flip_core
 
 
+def split_int(value, size):
+    if size & (size - 1):
+        return value // size, value % size
+    return value >> (size.bit_length() - 1), value & (size - 1)
+
+
 def slot_codes(spot, per_node, capacity):
     rank = lax.broadcasted_iota(jnp.int32, (8 * capacity, 1), 0)
-    flip, slot = rank // capacity, rank % capacity
-    reach = flip // 4 * per_node + flip % 4
+    flip, slot = split_int(rank, capacity)
+    side, local = split_int(flip, 4)
+    reach = side * per_node + local
     return ((spot[0] + (spot[1] ^ reach)) * capacity + slot).astype(F32)
 
 
@@ -65,19 +72,20 @@
 
 def first_kernel(per_node, capacity, experts, spot, *refs):
     far, (*outs, pick_ref, held, codes_ref) = refs[:5], refs[5:12]
-    (lists, local, gate, tok, grad), meta, sems = refs[12:17], refs[17], refs[18]
-    copies = [pltpu.make_async_copy(a, b, sems.at[i]) for i, (a, b) in enumerate(zip(far, refs[12:17]))]
+    (lists, local, gate), meta, sems = refs[12:15], refs[15], refs[16]
+    width = far[3].shape[1]
+    tok, grad = held.at[:, :width], held.at[:, width : 2 * width]
+    copies = [pltpu.make_async_copy(a, b, sems.at[i]) for i, (a, b) in enumerate(zip(far, (lists, local, gate, tok, grad)))]
     for copy in copies:
         copy.start()
     for copy in copies[:3]:
         copy.wait()
     top, tok_dev = local.shape
-    width = tok.shape[1]
-    place = local[...] // per_node
+    place, member_of = split_int(local[...], per_node)
     group = jnp.zeros_like(place)
     for j in range(lists.shape[0]):
         group = jnp.where(place == j, lists[j : j + 1, :], group)
-    expert = group * per_node + local[...] % per_node
+    expert = group * per_node + member_of
     ids = lax.broadcasted_iota(jnp.int32, (experts, tok_dev), 0)
     member = None
     for k in range(top):
@@ -92,12 +100,11 @@
         slot = jnp.sum(jnp.where(ids == expert[k : k + 1, :], before, 0.0), axis=0, keepdims=True)
         code = expert[k : k + 1, :].astype(F32) * capacity + slot
         meta[k : k + 1, :tok_dev] = jnp.where(slot < capacity, code, -1.0)
-    meta[top : 2 * top, :tok_dev] = (gate[...] // 256).astype(F32)
-    meta[2 * top : 3 * top, :tok_dev] = (gate[...] % 256).astype(F32)
+    high, low = split_int(gate[...], 256)
+    meta[top : 2 * top, :tok_dev] = high.astype(F32)
+    meta[2 * top : 3 * top, :tok_dev] = low.astype(F32)
     for copy in copies[3:]:
         copy.wait()
-    held[:, :width] = tok[...]
-    held[:, width : 2 * width] = grad[...]
     held[:, 2 * width :] = meta[...].astype(BF16)
     codes = slot_codes(spot, per_node, capacity)
     codes_ref[...] = codes
@@ -135,7 +142,7 @@
         in_specs=[pl.BlockSpec(memory_space=pltpu.SMEM)] + [pl.BlockSpec(memory_space=pltpu.HBM)] * 5,
         out_specs=whole(7),
         out_shape=row_shapes(capacity, *tok.shape) + extra,
-        scratch_shapes=[pltpu.VMEM(a.shape, a.dtype) for a in (lists, local, gate, tok, grad)]
+        scratch_shapes=[pltpu.VMEM(a.shape, a.dtype) for a in (lists, local, gate)]
         + [pltpu.VMEM((tok.shape[0], META), F32), pltpu.SemaphoreType.DMA((5,))],
         compiler_params=PARAMS,
         name="first_rows",
@@ -200,7 +207,6 @@
     node, place = lax.axis_index("node"), lax.axis_index("local")
     spot = jnp.stack([node // 2 * 2 * per_node, (node % 2) * per_node + place])
 
-    flips_back = [flips[i] for i in (0, 2, 1)]
     picks, got = [], []
     for w in range(depth - 1):
         if w == 0:
@@ -211,8 +217,9 @@
             held = ordered(held, got, w)
             *chosen, pick = next_rows(top, codes, held, False)
         picks.append(pick)
+        after = lax.ppermute(held, AXES, ring)
         got.append(turn(chosen, flips))
-        held = lax.ppermute(held, AXES, ring)
+        held = after
     *chosen, pick = next_rows(top, codes, ordered(held, got, depth - 1), True)
     picks.append(pick)
     ends = [turn(part, flips) for part in (chosen[:4], chosen[4:])]
@@ -260,6 +267,8 @@
             total, sent[order[1]][:1] = lax.optimization_barrier((total, sent[order[1]][:1]))
         if w == 0:
             total, down_local = lax.optimization_barrier((total, down_local))
+        if w == order[1]:
+            total, sent[order[2]][:1] = lax.optimization_barrier((total, sent[order[2]][:1]))
         if w:
             dest, perm = (w - 1, back) if w <= ahead else ((w + 1) % depth, ring)
             sums[dest].append(lax.ppermute(total, AXES, perm))

time: 107 us -> 107 us (level)
  no operation moved by 1% of the time
where the time goes in v5:
time: 107 us
  starting transfers between devices  42.5 us (40%)
  waiting for transfers between devices  41.8 us (39%)
  matrix products  15.8 us (15%)
  Pallas kernels  3.61 us (3%)
  local copies, waits for them, and re-layouts  1.78 us (2%)
  between operations  1.22 us (1%)
    ppermute x15, starting transfers between devices, turn(): lax.ppermute(rows[i + 1], AXES, flips[i])  18.5 us
    ppermute x15, waiting for transfers between devices, turn(): lax.ppermute(rows[i + 1], AXES, flips[i])  16.8 us
    ppermute x12, starting transfers between devices, body(): lax.ppermute(both[n], AXES, flip)  13.7 us
    ppermute x3, waiting for transfers between devices, body(): after = lax.ppermute(held, AXES, ring)  11.2 us
    ppermute x12, waiting for transfers between devices, body(): lax.ppermute(both[n], AXES, flip)  6.14 us
    ppermute x3, starting transfers between devices, body(): sums[dest].append(lax.ppermute(total, AXES, perm))  4.84 us
    dot_general x1, matrix products, body(): lax.dot_general(hidden, dy_rows, (((0,), (0,)), ((), ())), preferred_elem...  4.54 us
    ppermute x3, starting transfers between devices, body(): after = lax.ppermute(held, AXES, ring)  4.5 us
  transfers between devices with their start and end apart: 38, of which 17 were waited for; matrix products, arithmetic and copies ran while one was open for 9% of the time, Pallas kernels for 1%

profile of v5, /device:TPU:0, one launch (start us, length us, event | category | flops | bytes accessed | tf_op | source)
XLA Modules:
  0.0 107.1 jit_solution(11443219880014110846)
XLA Ops:
  0.7 2.1 %first_rows.1 = (bf16[2,16,4096]{2,1,0:T(8,128)(2,1)S(1)}, bf16[2,16,4096]{2,1,0:T(8,128)(2,1)S(1)}, bf16[2,16,4096]{2,1,0:T(8,128)(2,1)S(1)}, bf16[2,16,4096]{2...) custom-call(s32[2]{0:T(128)S(1)} %pad_add_fusion.spot, ...), custom_call_target="tpu_custom_call" | custom-call | tf_op jit(solution)/shard_map/first_rows/pallas_call | solution.py:140
  2.8 3.1 %collective-permute-start = (bf16[32,8320]{1,0:T(8,128)(2,1)S(1)}, bf16[32,8320]{1,0:T(8,128)(2,1)S(1)}, u32[]{:S(2)}, u32[]{:S(2)}) collective-permute-start(bf16[32,8320]{1,0:T(8,128)(2,1)S(1)} %get-tuple-element.54), channel_id=1, source_target_pairs={{0,8},{1,9},{2,10},{3,11},{4,12},{5,13},{6,14},{7,15},{8,24},{9,25... | collective-permute-start | bytes 1597448 | tf_op jit(solution)/shard_map/ppermute | solution.py:220
  7.4 1.5 %collective-permute-start.4 = (bf16[2,16,4096]{2,1,0:T(8,128)(2,1)S(1)}, bf16[2,16,4096]{2,1,0:T(8,128)(2,1)S(1)}, u32[]{:S(2)}, u32[]{:S(2)}) collective-permute-start(bf16[2,16,4096]{2,1,0:T(8,128)(2,1)S(1)} %get-tuple-element.60), channel_id=1, source_target_pairs={{0,6},{1,7},{2,4},{3,5},{4,2},{5,3},{6,0},{7,1},{8,14},{9,15},{10,... | collective-permute-start | bytes 786440 | tf_op jit(solution)/shard_map/ppermute | solution.py:185
  9.5 5.7 %collective-permute-done.1 = bf16[2,16,4096]{2,1,0:T(8,128)(2,1)S(1)} collective-permute-done((bf16[2,16,4096]{2,1,0:T(8,128)(2,1)S(1)}, bf16[2,16,4096]{2,1,0:T(8,128)(2,1)S(1)}, u32[]{:S(2)}, u32[]{:S(2)}) %collective-permute-start.1) | collective-permute-done | bytes 262176 | tf_op jit(solution)/shard_map/ppermute | solution.py:185
  15.2 3.9 %collective-permute-done.held = bf16[32,8320]{1,0:T(8,128)(2,1)S(1)} collective-permute-done((bf16[32,8320]{1,0:T(8,128)(2,1)S(1)}, bf16[32,8320]{1,0:T(8,128)(2,1)S(1)}, u32[]{:S(2)}, u32[]{:S(2)}) %collective-permute-start) | collective-permute-done | bytes 532512 | tf_op jit(solution)/shard_map/ppermute | solution.py:220
  20.4 1.5 %collective-permute-start.3 = (bf16[2,16,4096]{2,1,0:T(8,128)(2,1)S(1)}, bf16[2,16,4096]{2,1,0:T(8,128)(2,1)S(1)}, u32[]{:S(2)}, u32[]{:S(2)}) collective-permute-start(bf16[2,16,4096]{2,1,0:T(8,128)(2,1)S(1)} %get-tuple-element.59), channel_id=1, source_target_pairs={{0,2},{1,3},{2,0},{3,1},{4,6},{5,7},{6,4},{7,5},{8,10},{9,11},{10,... | collective-permute-start | bytes 786440 | tf_op jit(solution)/shard_map/ppermute | solution.py:185
  21.9 1.5 %collective-permute-start.8 = (bf16[2,16,4096]{2,1,0:T(8,128)(2,1)S(1)}, bf16[2,16,4096]{2,1,0:T(8,128)(2,1)S(1)}, u32[]{:S(2)}, u32[]{:S(2)}) collective-permute-start(bf16[2,16,4096]{2,1,0:T(8,128)(2,1)S(1)} %get-tuple-element.68), channel_id=1, source_target_pairs={{0,6},{1,7},{2,4},{3,5},{4,2},{5,3},{6,0},{7,1},{8,14},{9,15},{10,... | collective-permute-start | bytes 786440 | tf_op jit(solution)/shard_map/ppermute | solution.py:185
  24.0 5.6 %collective-permute-done.3 = bf16[2,16,4096]{2,1,0:T(8,128)(2,1)S(1)} collective-permute-done((bf16[2,16,4096]{2,1,0:T(8,128)(2,1)S(1)}, bf16[2,16,4096]{2,1,0:T(8,128)(2,1)S(1)}, u32[]{:S(2)}, u32[]{:S(2)}) %collective-permute-start.3) | collective-permute-done | bytes 262176 | tf_op jit(solution)/shard_map/ppermute | solution.py:185
  29.7 3.5 %collective-permute-done.2.held = bf16[32,8320]{1,0:T(8,128)(2,1)S(1)} collective-permute-done((bf16[32,8320]{1,0:T(8,128)(2,1)S(1)}, bf16[32,8320]{1,0:T(8,128)(2,1)S(1)}, u32[]{:S(2)}, u32[]{:S(2)}) %collective-permute-start.2) | collective-permute-done | bytes 532512 | tf_op jit(solution)/shard_map/ppermute | solution.py:220
  35.8 1.5 %collective-permute-start.10 = (bf16[2,16,4096]{2,1,0:T(8,128)(2,1)S(1)}, bf16[2,16,4096]{2,1,0:T(8,128)(2,1)S(1)}, u32[]{:S(2)}, u32[]{:S(2)}) collective-permute-start(bf16[2,16,4096]{2,1,0:T(8,128)(2,1)S(1)} %get-tuple-element.74), channel_id=1, source_target_pairs={{0,6},{1,7},{2,4},{3,5},{4,2},{5,3},{6,0},{7,1},{8,14},{9,15},{10,... | collective-permute-start | bytes 786440 | tf_op jit(solution)/shard_map/ppermute | solution.py:185
  38.0 5.2 %collective-permute-done.7 = bf16[2,16,4096]{2,1,0:T(8,128)(2,1)S(1)} collective-permute-done((bf16[2,16,4096]{2,1,0:T(8,128)(2,1)S(1)}, bf16[2,16,4096]{2,1,0:T(8,128)(2,1)S(1)}, u32[]{:S(2)}, u32[]{:S(2)}) %collective-permute-start.7) | collective-permute-done | bytes 262176 | tf_op jit(solution)/shard_map/ppermute | solution.py:185
  43.2 3.8 %collective-permute-done.6.held = bf16[32,8320]{1,0:T(8,128)(2,1)S(1)} collective-permute-done((bf16[32,8320]{1,0:T(8,128)(2,1)S(1)}, bf16[32,8320]{1,0:T(8,128)(2,1)S(1)}, u32[]{:S(2)}, u32[]{:S(2)}) %collective-permute-start.6) | collective-permute-done | bytes 532512 | tf_op jit(solution)/shard_map/ppermute | solution.py:220
  48.5 1.6 %collective-permute-start.13 = (bf16[16,4096]{1,0:T(8,128)(2,1)S(1)}, bf16[16,4096]{1,0:T(8,128)(2,1)S(1)}, u32[]{:S(2)}, u32[]{:S(2)}) collective-permute-start(bf16[16,4096]{1,0:T(8,128)(2,1)S(1)} %get-tuple-element.79), channel_id=1, source_target_pairs={{0,6},{1,7},{2,4},{3,5},{4,2},{5,3},{6,0},{7,1},{8,14},{9,15},{10,... | collective-permute-start | bytes 393224 | tf_op jit(solution)/shard_map/ppermute | solution.py:185
  52.6 1.9 %collective-permute-start.18 = (bf16[16,4096]{1,0:T(8,128)(2,1)S(1)}, bf16[16,4096]{1,0:T(8,128)(2,1)S(1)}, u32[]{:S(2)}, u32[]{:S(2)}) collective-permute-start(bf16[16,4096]{1,0:T(8,128)(2,1)S(1)} %get-tuple-element.83), channel_id=1, source_target_pairs={{0,6},{1,7},{2,4},{3,5},{4,2},{5,3},{6,0},{7,1},{8,14},{9,15},{10,... | collective-permute-start | bytes 393224 | tf_op jit(solution)/shard_map/ppermute | solution.py:185
  54.5 1.5 %collective-permute-start.19 = (bf16[16,4096]{1,0:T(8,128)(2,1)S(1)}, bf16[16,4096]{1,0:T(8,128)(2,1)S(1)}, u32[]{:S(2)}, u32[]{:S(2)}) collective-permute-start(bf16[16,4096]{1,0:T(8,128)(2,1)S(1)} %get-tuple-element.84), channel_id=1, source_target_pairs={{0,4},{1,5},{2,6},{3,7},{4,0},{5,1},{6,2},{7,3},{8,12},{9,13},{10,... | collective-permute-start | bytes 393224 | tf_op jit(solution)/shard_map/ppermute | solution.py:185
  57.7 1.8 %fusion.4 = f32[256,768]{1,0:T(8,128)S(1)} fusion(bf16[256,4096]{1,0:T(8,128)(2,1)S(1)} %constant_dynamic-update-slice_fusion, bf16[1,4096,768]{2,1,0:T(8,128)(2,1)S(1)} %copy-done), kind=kOutput, calls=%fused_computation.5 | convolution fusion | flops 1610612736 | bytes 9175040 | tf_op jit(solution)/shard_map/dot_general | solution.py:166
  60.6 1.8 %fusion.8 = f32[256,768]{1,0:T(8,128)S(1)} fusion(bf16[256,4096]{1,0:T(8,128)(2,1)S(1)} %constant_dynamic-update-slice_fusion, bf16[1,4096,768]{2,1,0:T(8,128)(2,1)S(1)} %bitcast.147), kind=kOutput, calls=%fused_computation.9 | convolution fusion | flops 1610612736 | bytes 9175040 | tf_op jit(solution)/shard_map/dot_general | solution.py:165
  64.2 2.1 %fusion = f32[256,768]{1,0:T(8,128)S(1)} fusion(bf16[256,4096]{1,0:T(8,128)(2,1)S(1)} %constant_dynamic-update-slice_fusion.17, bf16[1,768,4096]{2,1,0:T(8,128)(2,1)S(1)} %bitcast.155), kind=kOutput, calls=%fused_computation.1 | convolution fusion | flops 1610612736 | bytes 9175040 | tf_op jit(solution)/shard_map/dot_general | solution.py:174
  66.2 1.9 %fusion.2 = f32[256,4096]{1,0:T(8,128)S(1)} fusion(bf16[1,4096,768]{2,1,0:T(8,128)(2,1)S(1)} %copy-done, f32[256,768]{1,0:T(8,128)S(1)} %fusion, f32[256,768]{1,0:T(8,128)S(1)} %fusion.8), kind=kOutput, calls=%fused_computation.3 | convolution fusion | flops 1611792384 | bytes 12058624 | tf_op jit(solution)/shard_map/dot_general | solution.py:179
  68.1 2.0 %fusion.13 = bf16[256,4096]{1,0:T(8,128)(2,1)S(1)} fusion(f32[256,4096]{1,0:T(8,128)S(1)} %fusion.2, bf16[1,4096,768]{2,1,0:T(8,128)(2,1)S(1)} %bitcast.147, f32[256,768]{1,0:T(8,128)S(1)} %fusion.8, f32[256,768]{1,0:T(8,128)S(1)} %fusion, f32[256,768]{1,0:T(8,128)S(1)} %fusion.4), kind=kOutput, calls=%fused_computation.12 | convolution fusion | flops 1614675968 | bytes 14942208 | tf_op jit(solution)/shard_map/dot_general | solution.py:178
  74.3 1.5 %collective-permute-start.28 = (bf16[16,4096]{1,0:T(8,128)(2,1)S(1)}, bf16[16,4096]{1,0:T(8,128)(2,1)S(1)}, u32[]{:S(2)}, u32[]{:S(2)}) collective-permute-start(bf16[16,4096]{1,0:T(8,128)(2,1)S(1)} %get-tuple-element.118), channel_id=1, source_target_pairs={{0,6},{1,7},{2,4},{3,5},{4,2},{5,3},{6,0},{7,1},{8,14},{9,15},{10,... | collective-permute-start | bytes 393224 | tf_op jit(solution)/shard_map/ppermute | solution.py:253
  79.7 2.3 %collective-permute-done.27 = bf16[16,4096]{1,0:T(8,128)(2,1)S(1)} collective-permute-done((bf16[16,4096]{1,0:T(8,128)(2,1)S(1)}, bf16[16,4096]{1,0:T(8,128)(2,1)S(1)}, u32[]{:S(2)}, u32[]{:S(2)}) %collective-permute-start.27) | collective-permute-done | bytes 131104 | tf_op jit(solution)/shard_map/ppermute | solution.py:253
  82.6 1.5 %collective-permute-start.34 = (bf16[16,4096]{1,0:T(8,128)(2,1)S(1)}, bf16[16,4096]{1,0:T(8,128)(2,1)S(1)}, u32[]{:S(2)}, u32[]{:S(2)}) collective-permute-start(bf16[16,4096]{1,0:T(8,128)(2,1)S(1)} %get-tuple-element.111), channel_id=1, source_target_pairs={{0,4},{1,5},{2,6},{3,7},{4,0},{5,1},{6,2},{7,3},{8,12},{9,13},{10,... | collective-permute-start | bytes 393224 | tf_op jit(solution)/shard_map/ppermute | solution.py:253
  84.4 1.9 %collective-permute-start.36 = (bf16[32,4096]{1,0:T(8,128)(2,1)S(1)}, bf16[32,4096]{1,0:T(8,128)(2,1)S(1)}, u32[]{:S(2)}, u32[]{:S(2)}) collective-permute-start(bf16[32,4096]{1,0:T(8,128)(2,1)S(1)} %convolution_convert_fusion.2), channel_id=1, source_target_pairs={{8,0},{9,1},{10,2},{11,3},{12,4},{13,5},{14,6},{15,7},{24,8},{25,9... | collective-permute-start | bytes 786440 | tf_op jit(solution)/shard_map/ppermute | solution.py:274
  87.7 1.5 %collective-permute-start.35 = (bf16[16,4096]{1,0:T(8,128)(2,1)S(1)}, bf16[16,4096]{1,0:T(8,128)(2,1)S(1)}, u32[]{:S(2)}, u32[]{:S(2)}) collective-permute-start(bf16[16,4096]{1,0:T(8,128)(2,1)S(1)} %get-tuple-element.110), channel_id=1, source_target_pairs={{0,6},{1,7},{2,4},{3,5},{4,2},{5,3},{6,0},{7,1},{8,14},{9,15},{10,... | collective-permute-start | bytes 393224 | tf_op jit(solution)/shard_map/ppermute | solution.py:253
  90.0 1.5 %collective-permute-start.23 = (bf16[16,4096]{1,0:T(8,128)(2,1)S(1)}, bf16[16,4096]{1,0:T(8,128)(2,1)S(1)}, u32[]{:S(2)}, u32[]{:S(2)}) collective-permute-start(bf16[16,4096]{1,0:T(8,128)(2,1)S(1)} %get-tuple-element.127), channel_id=1, source_target_pairs={{0,4},{1,5},{2,6},{3,7},{4,0},{5,1},{6,2},{7,3},{8,12},{9,13},{10,... | collective-permute-start | bytes 393224 | tf_op jit(solution)/shard_map/ppermute | solution.py:253
  91.5 1.5 %collective-permute-start.24 = (bf16[16,4096]{1,0:T(8,128)(2,1)S(1)}, bf16[16,4096]{1,0:T(8,128)(2,1)S(1)}, u32[]{:S(2)}, u32[]{:S(2)}) collective-permute-start(bf16[16,4096]{1,0:T(8,128)(2,1)S(1)} %get-tuple-element.126), channel_id=1, source_target_pairs={{0,6},{1,7},{2,4},{3,5},{4,2},{5,3},{6,0},{7,1},{8,14},{9,15},{10,... | collective-permute-start | bytes 393224 | tf_op jit(solution)/shard_map/ppermute | solution.py:253
  93.0 1.6 %collective-permute-done.35 = bf16[16,4096]{1,0:T(8,128)(2,1)S(1)} collective-permute-done((bf16[16,4096]{1,0:T(8,128)(2,1)S(1)}, bf16[16,4096]{1,0:T(8,128)(2,1)S(1)}, u32[]{:S(2)}, u32[]{:S(2)}) %collective-permute-start.35) | collective-permute-done | bytes 131104 | tf_op jit(solution)/shard_map/ppermute | solution.py:253
  94.6 2.1 %collective-permute-start.33 = (bf16[32,4096]{1,0:T(8,128)(2,1)S(1)}, bf16[32,4096]{1,0:T(8,128)(2,1)S(1)}, u32[]{:S(2)}, u32[]{:S(2)}) collective-permute-start(bf16[32,4096]{1,0:T(8,128)(2,1)S(1)} %convolution_convert_fusion.1), channel_id=1, source_target_pairs={{0,8},{1,9},{2,10},{3,11},{4,12},{5,13},{6,14},{7,15},{8,24},{9,25... | collective-permute-start | bytes 786440 | tf_op jit(solution)/shard_map/ppermute | solution.py:274
  97.8 4.5 %convolution_convert_fusion = bf16[768,4096]{1,0:T(8,128)(2,1)} fusion(bf16[256,768]{1,0:T(8,128)(2,1)S(1)} %multiply_convert_fusion, bf16[256,4096]{1,0:T(8,128)(2,1)S(1)} %constant_dynamic-update-slice_fusion.17), kind=kOutput, calls=%fused_computation | convolution fusion | flops 1613758464 | bytes 8781824 | tf_op jit(solution)/shard_map/dot_general | solution.py:264
  102.4 1.7 %collective-permute-done.33 = bf16[32,4096]{1,0:T(8,128)(2,1)S(1)} collective-permute-done((bf16[32,4096]{1,0:T(8,128)(2,1)S(1)}, bf16[32,4096]{1,0:T(8,128)(2,1)S(1)}, u32[]{:S(2)}, u32[]{:S(2)}) %collective-permute-start.33) | collective-permute-done | bytes 262176 | tf_op jit(solution)/shard_map/ppermute | solution.py:274
  104.1 2.0 %collective-permute-done.37 = bf16[32,4096]{1,0:T(8,128)(2,1)S(1)} collective-permute-done((bf16[32,4096]{1,0:T(8,128)(2,1)S(1)}, bf16[32,4096]{1,0:T(8,128)(2,1)S(1)}, u32[]{:S(2)}, u32[]{:S(2)}) %collective-permute-start.37) | collective-permute-done | bytes 262176 | tf_op jit(solution)/shard_map/ppermute | solution.py:274
  (118 shorter events, 28.7 us)
Async XLA Ops:
  2.8 16.2 %collective-permute-start = (bf16[32,8320]{1,0:T(8,128)(2,1)S(1)}, bf16[32,8320]{1,0:T(8,128)(2,1)S(1)}, u32[]{:S(2)}, u32[]{:S(2)}) collective-permute-start(bf16[32,8320]{1,0:T(8,128)(2,1)S(1)} %get-tuple-element.54), channel_id=1, source_target_pairs={{0,8},{1,9},{2,10},{3,11},{4,12},{5,13},{6,14},{7,15},{8,24},{9,25... | collective-permute-start | bytes 1597448 | tf_op jit(solution)/shard_map/ppermute | solution.py:220
  5.9 9.2 %collective-permute-start.1 = (bf16[2,16,4096]{2,1,0:T(8,128)(2,1)S(1)}, bf16[2,16,4096]{2,1,0:T(8,128)(2,1)S(1)}, u32[]{:S(2)}, u32[]{:S(2)}) collective-permute-start(bf16[2,16,4096]{2,1,0:T(8,128)(2,1)S(1)} %get-tuple-element.55), channel_id=1, source_target_pairs={{0,2},{1,3},{2,0},{3,1},{4,6},{5,7},{6,4},{7,5},{8,10},{9,11},{10,... | collective-permute-start | bytes 786440 | tf_op jit(solution)/shard_map/ppermute | solution.py:185
  7.4 16.0 %collective-permute-start.4 = (bf16[2,16,4096]{2,1,0:T(8,128)(2,1)S(1)}, bf16[2,16,4096]{2,1,0:T(8,128)(2,1)S(1)}, u32[]{:S(2)}, u32[]{:S(2)}) collective-permute-start(bf16[2,16,4096]{2,1,0:T(8,128)(2,1)S(1)} %get-tuple-element.60), channel_id=1, source_target_pairs={{0,6},{1,7},{2,4},{3,5},{4,2},{5,3},{6,0},{7,1},{8,14},{9,15},{10,... | collective-permute-start | bytes 786440 | tf_op jit(solution)/shard_map/ppermute | solution.py:185
  8.9 15.1 %collective-permute-start.5 = (bf16[2,16,4096]{2,1,0:T(8,128)(2,1)S(1)}, bf16[2,16,4096]{2,1,0:T(8,128)(2,1)S(1)}, u32[]{:S(2)}, u32[]{:S(2)}) collective-permute-start(bf16[2,16,4096]{2,1,0:T(8,128)(2,1)S(1)} %get-tuple-element.61), channel_id=1, source_target_pairs={{0,4},{1,5},{2,6},{3,7},{4,0},{5,1},{6,2},{7,3},{8,12},{9,13},{10,... | collective-permute-start | bytes 786440 | tf_op jit(solution)/shard_map/ppermute | solution.py:185
  19.0 14.2 %collective-permute-start.2 = (bf16[32,8320]{1,0:T(8,128)(2,1)S(1)}, bf16[32,8320]{1,0:T(8,128)(2,1)S(1)}, u32[]{:S(2)}, u32[]{:S(2)}) collective-permute-start(bf16[32,8320]{1,0:T(8,128)(2,1)S(1)} %collective-permute-done.held), channel_id=1, source_target_pairs={{0,8},{1,9},{2,10},{3,11},{4,12},{5,13},{6,14},{7,15},{8,24},{9,25... | collective-permute-start | bytes 1597448 | tf_op jit(solution)/shard_map/ppermute | solution.py:220
  20.4 9.3 %collective-permute-start.3 = (bf16[2,16,4096]{2,1,0:T(8,128)(2,1)S(1)}, bf16[2,16,4096]{2,1,0:T(8,128)(2,1)S(1)}, u32[]{:S(2)}, u32[]{:S(2)}) collective-permute-start(bf16[2,16,4096]{2,1,0:T(8,128)(2,1)S(1)} %get-tuple-element.59), channel_id=1, source_target_pairs={{0,2},{1,3},{2,0},{3,1},{4,6},{5,7},{6,4},{7,5},{8,10},{9,11},{10,... | collective-permute-start | bytes 786440 | tf_op jit(solution)/shard_map/ppermute | solution.py:185
  21.9 15.5 %collective-permute-start.8 = (bf16[2,16,4096]{2,1,0:T(8,128)(2,1)S(1)}, bf16[2,16,4096]{2,1,0:T(8,128)(2,1)S(1)}, u32[]{:S(2)}, u32[]{:S(2)}) collective-permute-start(bf16[2,16,4096]{2,1,0:T(8,128)(2,1)S(1)} %get-tuple-element.68), channel_id=1, source_target_pairs={{0,6},{1,7},{2,4},{3,5},{4,2},{5,3},{6,0},{7,1},{8,14},{9,15},{10,... | collective-permute-start | bytes 786440 | tf_op jit(solution)/shard_map/ppermute | solution.py:185
  23.5 14.5 %collective-permute-start.9 = (bf16[2,16,4096]{2,1,0:T(8,128)(2,1)S(1)}, bf16[2,16,4096]{2,1,0:T(8,128)(2,1)S(1)}, u32[]{:S(2)}, u32[]{:S(2)}) collective-permute-start(bf16[2,16,4096]{2,1,0:T(8,128)(2,1)S(1)} %get-tuple-element.69), channel_id=1, source_target_pairs={{0,4},{1,5},{2,6},{3,7},{4,0},{5,1},{6,2},{7,3},{8,12},{9,13},{10,... | collective-permute-start | bytes 786440 | tf_op jit(solution)/shard_map/ppermute | solution.py:185
  33.7 13.3 %collective-permute-start.6 = (bf16[32,8320]{1,0:T(8,128)(2,1)S(1)}, bf16[32,8320]{1,0:T(8,128)(2,1)S(1)}, u32[]{:S(2)}, u32[]{:S(2)}) collective-permute-start(bf16[32,8320]{1,0:T(8,128)(2,1)S(1)} %collective-permute-done.2.held), channel_id=1, source_target_pairs={{0,8},{1,9},{2,10},{3,11},{4,12},{5,13},{6,14},{7,15},{8,24},{9,25... | collective-permute-start | bytes 1597448 | tf_op jit(solution)/shard_map/ppermute | solution.py:220
  34.3 9.0 %collective-permute-start.7 = (bf16[2,16,4096]{2,1,0:T(8,128)(2,1)S(1)}, bf16[2,16,4096]{2,1,0:T(8,128)(2,1)S(1)}, u32[]{:S(2)}, u32[]{:S(2)}) collective-permute-start(bf16[2,16,4096]{2,1,0:T(8,128)(2,1)S(1)} %get-tuple-element.67), channel_id=1, source_target_pairs={{0,2},{1,3},{2,0},{3,1},{4,6},{5,7},{6,4},{7,5},{8,10},{9,11},{10,... | collective-permute-start | bytes 786440 | tf_op jit(solution)/shard_map/ppermute | solution.py:185
  35.8 15.4 %collective-permute-start.10 = (bf16[2,16,4096]{2,1,0:T(8,128)(2,1)S(1)}, bf16[2,16,4096]{2,1,0:T(8,128)(2,1)S(1)}, u32[]{:S(2)}, u32[]{:S(2)}) collective-permute-start(bf16[2,16,4096]{2,1,0:T(8,128)(2,1)S(1)} %get-tuple-element.74), channel_id=1, source_target_pairs={{0,6},{1,7},{2,4},{3,5},{4,2},{5,3},{6,0},{7,1},{8,14},{9,15},{10,... | collective-permute-start | bytes 786440 | tf_op jit(solution)/shard_map/ppermute | solution.py:185
  37.4 13.8 %collective-permute-start.11 = (bf16[2,16,4096]{2,1,0:T(8,128)(2,1)S(1)}, bf16[2,16,4096]{2,1,0:T(8,128)(2,1)S(1)}, u32[]{:S(2)}, u32[]{:S(2)}) collective-permute-start(bf16[2,16,4096]{2,1,0:T(8,128)(2,1)S(1)} %get-tuple-element.75), channel_id=1, source_target_pairs={{0,4},{1,5},{2,6},{3,7},{4,0},{5,1},{6,2},{7,3},{8,12},{9,13},{10,... | collective-permute-start | bytes 786440 | tf_op jit(solution)/shard_map/ppermute | solution.py:185
  48.5 6.0 %collective-permute-start.13 = (bf16[16,4096]{1,0:T(8,128)(2,1)S(1)}, bf16[16,4096]{1,0:T(8,128)(2,1)S(1)}, u32[]{:S(2)}, u32[]{:S(2)}) collective-permute-start(bf16[16,4096]{1,0:T(8,128)(2,1)S(1)} %get-tuple-element.79), channel_id=1, source_target_pairs={{0,6},{1,7},{2,4},{3,5},{4,2},{5,3},{6,0},{7,1},{8,14},{9,15},{10,... | collective-permute-start | bytes 393224 | tf_op jit(solution)/shard_map/ppermute | solution.py:185
  51.3 11.0 %collective-permute-start.17 = (bf16[16,4096]{1,0:T(8,128)(2,1)S(1)}, bf16[16,4096]{1,0:T(8,128)(2,1)S(1)}, u32[]{:S(2)}, u32[]{:S(2)}) collective-permute-start(bf16[16,4096]{1,0:T(8,128)(2,1)S(1)} %get-tuple-element.82), channel_id=1, source_target_pairs={{0,2},{1,3},{2,0},{3,1},{4,6},{5,7},{6,4},{7,5},{8,10},{9,11},{10,... | collective-permute-start | bytes 393224 | tf_op jit(solution)/shard_map/ppermute | solution.py:185
  52.6 9.8 %collective-permute-start.18 = (bf16[16,4096]{1,0:T(8,128)(2,1)S(1)}, bf16[16,4096]{1,0:T(8,128)(2,1)S(1)}, u32[]{:S(2)}, u32[]{:S(2)}) collective-permute-start(bf16[16,4096]{1,0:T(8,128)(2,1)S(1)} %get-tuple-element.83), channel_id=1, source_target_pairs={{0,6},{1,7},{2,4},{3,5},{4,2},{5,3},{6,0},{7,1},{8,14},{9,15},{10,... | collective-permute-start | bytes 393224 | tf_op jit(solution)/shard_map/ppermute | solution.py:185
  54.5 7.9 %collective-permute-start.19 = (bf16[16,4096]{1,0:T(8,128)(2,1)S(1)}, bf16[16,4096]{1,0:T(8,128)(2,1)S(1)}, u32[]{:S(2)}, u32[]{:S(2)}) collective-permute-start(bf16[16,4096]{1,0:T(8,128)(2,1)S(1)} %get-tuple-element.84), channel_id=1, source_target_pairs={{0,4},{1,5},{2,6},{3,7},{4,0},{5,1},{6,2},{7,3},{8,12},{9,13},{10,... | collective-permute-start | bytes 393224 | tf_op jit(solution)/shard_map/ppermute | solution.py:185
  70.4 6.8 %collective-permute-start.21 = (bf16[2,4,8,4096]{3,2,1,0:T(8,128)(2,1)S(1)}, bf16[2,4,8,4096]{3,2,1,0:T(8,128)(2,1)S(1)}, u32[]{:S(2)}, u32[]{:S(2)}) collective-permute-start(bf16[2,4,8,4096]{3,2,1,0:T(8,128)(2,1)S(1)} %bitcast.149), channel_id=1, source_target_pairs={{0,1},{1,0},{2,3},{3,2},{4,5},{5,4},{6,7},{7,6},{8,9},{9,8},{10,11... | collective-permute-start | bytes 1572872 | tf_op jit(solution)/shard_map/ppermute | solution.py:247
  72.3 6.2 %collective-permute-start.26 = (bf16[16,4096]{1,0:T(8,128)(2,1)S(1)}, bf16[16,4096]{1,0:T(8,128)(2,1)S(1)}, u32[]{:S(2)}, u32[]{:S(2)}) collective-permute-start(bf16[16,4096]{1,0:T(8,128)(2,1)S(1)} %get-tuple-element.117), channel_id=1, source_target_pairs={{0,2},{1,3},{2,0},{3,1},{4,6},{5,7},{6,4},{7,5},{8,10},{9,11},{10,... | collective-permute-start | bytes 393224 | tf_op jit(solution)/shard_map/ppermute | solution.py:253
  73.6 8.5 %collective-permute-start.27 = (bf16[16,4096]{1,0:T(8,128)(2,1)S(1)}, bf16[16,4096]{1,0:T(8,128)(2,1)S(1)}, u32[]{:S(2)}, u32[]{:S(2)}) collective-permute-start(bf16[16,4096]{1,0:T(8,128)(2,1)S(1)} %get-tuple-element.119), channel_id=1, source_target_pairs={{0,4},{1,5},{2,6},{3,7},{4,0},{5,1},{6,2},{7,3},{8,12},{9,13},{10,... | collective-permute-start | bytes 393224 | tf_op jit(solution)/shard_map/ppermute | solution.py:253
  74.3 8.4 %collective-permute-start.28 = (bf16[16,4096]{1,0:T(8,128)(2,1)S(1)}, bf16[16,4096]{1,0:T(8,128)(2,1)S(1)}, u32[]{:S(2)}, u32[]{:S(2)}) collective-permute-start(bf16[16,4096]{1,0:T(8,128)(2,1)S(1)} %get-tuple-element.118), channel_id=1, source_target_pairs={{0,6},{1,7},{2,4},{3,5},{4,2},{5,3},{6,0},{7,1},{8,14},{9,15},{10,... | collective-permute-start | bytes 393224 | tf_op jit(solution)/shard_map/ppermute | solution.py:253
  75.9 8.5 %collective-permute-start.29 = (bf16[16,4096]{1,0:T(8,128)(2,1)S(1)}, bf16[16,4096]{1,0:T(8,128)(2,1)S(1)}, u32[]{:S(2)}, u32[]{:S(2)}) collective-permute-start(bf16[16,4096]{1,0:T(8,128)(2,1)S(1)} %get-tuple-element.113), channel_id=1, source_target_pairs={{0,2},{1,3},{2,0},{3,1},{4,6},{5,7},{6,4},{7,5},{8,10},{9,11},{10,... | collective-permute-start | bytes 393224 | tf_op jit(solution)/shard_map/ppermute | solution.py:253
  77.2 10.5 %collective-permute-start.30 = (bf16[16,4096]{1,0:T(8,128)(2,1)S(1)}, bf16[16,4096]{1,0:T(8,128)(2,1)S(1)}, u32[]{:S(2)}, u32[]{:S(2)}) collective-permute-start(bf16[16,4096]{1,0:T(8,128)(2,1)S(1)} %get-tuple-element.115), channel_id=1, source_target_pairs={{0,4},{1,5},{2,6},{3,7},{4,0},{5,1},{6,2},{7,3},{8,12},{9,13},{10,... | collective-permute-start | bytes 393224 | tf_op jit(solution)/shard_map/ppermute | solution.py:253
  78.5 10.7 %collective-permute-start.31 = (bf16[16,4096]{1,0:T(8,128)(2,1)S(1)}, bf16[16,4096]{1,0:T(8,128)(2,1)S(1)}, u32[]{:S(2)}, u32[]{:S(2)}) collective-permute-start(bf16[16,4096]{1,0:T(8,128)(2,1)S(1)} %get-tuple-element.114), channel_id=1, source_target_pairs={{0,6},{1,7},{2,4},{3,5},{4,2},{5,3},{6,0},{7,1},{8,14},{9,15},{10,... | collective-permute-start | bytes 393224 | tf_op jit(solution)/shard_map/ppermute | solution.py:253
  82.1 7.9 %collective-permute-start.32 = (bf16[16,4096]{1,0:T(8,128)(2,1)S(1)}, bf16[16,4096]{1,0:T(8,128)(2,1)S(1)}, u32[]{:S(2)}, u32[]{:S(2)}) collective-permute-start(bf16[16,4096]{1,0:T(8,128)(2,1)S(1)} %get-tuple-element.109), channel_id=1, source_target_pairs={{0,2},{1,3},{2,0},{3,1},{4,6},{5,7},{6,4},{7,5},{8,10},{9,11},{10,... | collective-permute-start | bytes 393224 | tf_op jit(solution)/shard_map/ppermute | solution.py:253
  82.6 8.9 %collective-permute-start.34 = (bf16[16,4096]{1,0:T(8,128)(2,1)S(1)}, bf16[16,4096]{1,0:T(8,128)(2,1)S(1)}, u32[]{:S(2)}, u32[]{:S(2)}) collective-permute-start(bf16[16,4096]{1,0:T(8,128)(2,1)S(1)} %get-tuple-element.111), channel_id=1, source_target_pairs={{0,4},{1,5},{2,6},{3,7},{4,0},{5,1},{6,2},{7,3},{8,12},{9,13},{10,... | collective-permute-start | bytes 393224 | tf_op jit(solution)/shard_map/ppermute | solution.py:253
  84.4 12.3 %collective-permute-start.36 = (bf16[32,4096]{1,0:T(8,128)(2,1)S(1)}, bf16[32,4096]{1,0:T(8,128)(2,1)S(1)}, u32[]{:S(2)}, u32[]{:S(2)}) collective-permute-start(bf16[32,4096]{1,0:T(8,128)(2,1)S(1)} %convolution_convert_fusion.2), channel_id=1, source_target_pairs={{8,0},{9,1},{10,2},{11,3},{12,4},{13,5},{14,6},{15,7},{24,8},{25,9... | collective-permute-start | bytes 786440 | tf_op jit(solution)/shard_map/ppermute | solution.py:274
  87.7 6.9 %collective-permute-start.35 = (bf16[16,4096]{1,0:T(8,128)(2,1)S(1)}, bf16[16,4096]{1,0:T(8,128)(2,1)S(1)}, u32[]{:S(2)}, u32[]{:S(2)}) collective-permute-start(bf16[16,4096]{1,0:T(8,128)(2,1)S(1)} %get-tuple-element.110), channel_id=1, source_target_pairs={{0,6},{1,7},{2,4},{3,5},{4,2},{5,3},{6,0},{7,1},{8,14},{9,15},{10,... | collective-permute-start | bytes 393224 | tf_op jit(solution)/shard_map/ppermute | solution.py:253
  89.1 13.2 %collective-permute-start.22 = (bf16[16,4096]{1,0:T(8,128)(2,1)S(1)}, bf16[16,4096]{1,0:T(8,128)(2,1)S(1)}, u32[]{:S(2)}, u32[]{:S(2)}) collective-permute-start(bf16[16,4096]{1,0:T(8,128)(2,1)S(1)} %get-tuple-element.125), channel_id=1, source_target_pairs={{0,2},{1,3},{2,0},{3,1},{4,6},{5,7},{6,4},{7,5},{8,10},{9,11},{10,... | collective-permute-start | bytes 393224 | tf_op jit(solution)/shard_map/ppermute | solution.py:253
  90.0 12.4 %collective-permute-start.23 = (bf16[16,4096]{1,0:T(8,128)(2,1)S(1)}, bf16[16,4096]{1,0:T(8,128)(2,1)S(1)}, u32[]{:S(2)}, u32[]{:S(2)}) collective-permute-start(bf16[16,4096]{1,0:T(8,128)(2,1)S(1)} %get-tuple-element.127), channel_id=1, source_target_pairs={{0,4},{1,5},{2,6},{3,7},{4,0},{5,1},{6,2},{7,3},{8,12},{9,13},{10,... | collective-permute-start | bytes 393224 | tf_op jit(solution)/shard_map/ppermute | solution.py:253
  91.5 10.9 %collective-permute-start.24 = (bf16[16,4096]{1,0:T(8,128)(2,1)S(1)}, bf16[16,4096]{1,0:T(8,128)(2,1)S(1)}, u32[]{:S(2)}, u32[]{:S(2)}) collective-permute-start(bf16[16,4096]{1,0:T(8,128)(2,1)S(1)} %get-tuple-element.126), channel_id=1, source_target_pairs={{0,6},{1,7},{2,4},{3,5},{4,2},{5,3},{6,0},{7,1},{8,14},{9,15},{10,... | collective-permute-start | bytes 393224 | tf_op jit(solution)/shard_map/ppermute | solution.py:253
  94.6 9.5 %collective-permute-start.33 = (bf16[32,4096]{1,0:T(8,128)(2,1)S(1)}, bf16[32,4096]{1,0:T(8,128)(2,1)S(1)}, u32[]{:S(2)}, u32[]{:S(2)}) collective-permute-start(bf16[32,4096]{1,0:T(8,128)(2,1)S(1)} %convolution_convert_fusion.1), channel_id=1, source_target_pairs={{0,8},{1,9},{2,10},{3,11},{4,12},{5,13},{6,14},{7,15},{8,24},{9,25... | collective-permute-start | bytes 786440 | tf_op jit(solution)/shard_map/ppermute | solution.py:274
  96.9 9.2 %collective-permute-start.37 = (bf16[32,4096]{1,0:T(8,128)(2,1)S(1)}, bf16[32,4096]{1,0:T(8,128)(2,1)S(1)}, u32[]{:S(2)}, u32[]{:S(2)}) collective-permute-start(bf16[32,4096]{1,0:T(8,128)(2,1)S(1)} %fusion.18), channel_id=1, source_target_pairs={{8,0},{9,1},{10,2},{11,3},{12,4},{13,5},{14,6},{15,7},{24,8},{25,9... | collective-permute-start | bytes 786440 | tf_op jit(solution)/shard_map/ppermute | solution.py:274
  (11 other events, 42.7 us)

commit v6 on v4

--- a/solution.py
+++ b/solution.py
@@ -12,7 +12,7 @@
 F32 = jnp.float32
 COLUMNS = 1024
 META = 128
-NEAR = 2
+NEAR = 1
 
 
 def device_perms(nodes, per_node):
@@ -96,19 +96,18 @@
     meta[2 * top : 3 * top, :tok_dev] = (gate[...] % 256).astype(F32)
     for copy in copies[3:]:
         copy.wait()
-    held[:, :width] = tok[...]
-    held[:, width : 2 * width] = grad[...]
-    held[:, 2 * width :] = meta[...].astype(BF16)
+    held[:, :width] = grad[...]
+    held[:, width:] = meta[...].astype(BF16)
     codes = slot_codes(spot, per_node, capacity)
     codes_ref[...] = codes
     pick_rows(meta, codes, tok, grad, top, [(out.at[0], out.at[1]) for out in outs], pick_ref)
 
 
-def next_kernel(top, codes, held, *refs):
+def next_kernel(top, codes, tok, held, *refs):
     *outs, pick_ref = refs
     width = outs[0].shape[-1]
-    meta = held[:, 2 * width :].astype(F32)
-    tok, grad = held.at[:, :width], held.at[:, width : 2 * width]
+    meta = held[:, width:].astype(F32)
+    grad = held.at[:, :width]
     pairs = list(zip(outs[:4], outs[4:])) if len(outs) == 8 else [(out.at[0], out.at[1]) for out in outs]
     pick_rows(meta, codes[...], tok, grad, top, pairs, pick_ref)
 
@@ -127,7 +126,7 @@
 
 
 def first_rows(per_node, capacity, experts, spot, lists, local, gate, tok, grad):
-    shape = (tok.shape[0], 2 * tok.shape[1] + META)
+    shape = (tok.shape[0], tok.shape[1] + META)
     operands = [pltpu.with_memory_space_constraint(a, pltpu.HBM) for a in (lists, local, gate, tok, grad)]
     extra = [jax.ShapeDtypeStruct(shape, BF16), jax.ShapeDtypeStruct((8 * capacity, 1), F32)]
     return pl.pallas_call(
@@ -142,16 +141,16 @@
     )(spot, *operands)
 
 
-def next_rows(top, codes, held, apart):
-    shapes = row_shapes(codes.shape[0] // 8, held.shape[0], (held.shape[1] - META) // 2, apart)
+def next_rows(top, codes, tok, held, apart):
+    shapes = row_shapes(codes.shape[0] // 8, *tok.shape, apart)
     return pl.pallas_call(
         functools.partial(next_kernel, top),
-        in_specs=whole(2),
+        in_specs=whole(3),
         out_specs=whole(len(shapes)),
         out_shape=shapes,
         compiler_params=PARAMS,
         name="next_rows",
-    )(codes, held)
+    )(codes, tok, held)
 
 
 def products(x_rows, w_gate_e, w_up_e):
@@ -200,8 +199,7 @@
     node, place = lax.axis_index("node"), lax.axis_index("local")
     spot = jnp.stack([node // 2 * 2 * per_node, (node % 2) * per_node + place])
 
-    flips_back = [flips[i] for i in (0, 2, 1)]
-    picks, got = [], []
+    tok, picks, got = tokens, [], []
     for w in range(depth - 1):
         if w == 0:
             *chosen, pick, held, codes = first_rows(
@@ -209,11 +207,11 @@
             )
         else:
             held = ordered(held, got, w)
-            *chosen, pick = next_rows(top, codes, held, False)
+            *chosen, pick = next_rows(top, codes, tok, held, False)
         picks.append(pick)
         got.append(turn(chosen, flips))
-        held = lax.ppermute(held, AXES, ring)
-    *chosen, pick = next_rows(top, codes, ordered(held, got, depth - 1), True)
+        tok, held = lax.ppermute(tok, AXES, ring), lax.ppermute(held, AXES, ring)
+    *chosen, pick = next_rows(top, codes, tok, ordered(held, got, depth - 1), True)
     picks.append(pick)
     ends = [turn(part, flips) for part in (chosen[:4], chosen[4:])]
     most = lax.ppermute(jnp.concatenate([g[:, capacity:] for window in got for g in window], axis=1), AXES, flip_core)
@@ -260,6 +258,8 @@
             total, sent[order[1]][:1] = lax.optimization_barrier((total, sent[order[1]][:1]))
         if w == 0:
             total, down_local = lax.optimization_barrier((total, down_local))
+        if w == order[1]:
+            total, sent[order[2]][:1] = lax.optimization_barrier((total, sent[order[2]][:1]))
         if w:
             dest, perm = (w - 1, back) if w <= ahead else ((w + 1) % depth, ring)
             sums[dest].append(lax.ppermute(total, AXES, perm))

time: 107 us -> 108 us (level)
  starting transfers between devices: 42.8 us -> 48.4 us
  waiting for transfers between devices: 41.5 us -> 36.1 us
    ppermute x3 -> x6, starting transfers between devices: 4.49 us -> 9.28 us  [body(): tok, held = (lax.ppermute(tok, AXES, ring), lax.ppermute(held, AXES, ring))]
    ppermute x3 -> x6, waiting for transfers between devices: 11.2 us -> 7.78 us  [body(): tok, held = (lax.ppermute(tok, AXES, ring), lax.ppermute(held, AXES, ring))]
    ppermute x15, waiting for transfers between devices: 16.8 us -> 14.9 us  [turn(): lax.ppermute(rows[i + 1], AXES, flips[i])]
    ppermute x15, starting transfers between devices: 18.6 us -> 19.8 us  [turn(): lax.ppermute(rows[i + 1], AXES, flips[i])]
  transfers between devices with their start and end apart: 38 -> 41, of which waited for: 17 -> 17; matrix products, arithmetic and copies ran while one was open for 9% -> 9% of each run, Pallas kernels for 1% -> 3%
where the time goes in v6:
time: 108 us; the launch traced here: 107 us
  starting transfers between devices  48.4 us (45%)
  waiting for transfers between devices  36.1 us (33%)
  matrix products  15.8 us (15%)
  Pallas kernels  3.61 us (3%)
  local copies, waits for them, and re-layouts  1.73 us (2%)
  between operations  1.23 us (1%)
    ppermute x15, starting transfers between devices, turn(): lax.ppermute(rows[i + 1], AXES, flips[i])  19.8 us
    ppermute x15, waiting for transfers between devices, turn(): lax.ppermute(rows[i + 1], AXES, flips[i])  14.9 us
    ppermute x12, starting transfers between devices, body(): lax.ppermute(both[n], AXES, flip)  14.3 us
    ppermute x6, starting transfers between devices, body(): tok, held = (lax.ppermute(tok, AXES, ring), lax.ppermute(held, AXES, ring))  9.28 us
    ppermute x6, waiting for transfers between devices, body(): tok, held = (lax.ppermute(tok, AXES, ring), lax.ppermute(held, AXES, ring))  7.78 us
    ppermute x12, waiting for transfers between devices, body(): lax.ppermute(both[n], AXES, flip)  5.71 us
    dot_general x1, matrix products, body(): lax.dot_general(hidden, dy_rows, (((0,), (0,)), ((), ())), preferred_elem...  4.54 us
    ppermute x3, starting transfers between devices, body(): sums[dest].append(lax.ppermute(total, AXES, perm))  4.23 us
  transfers between devices with their start and end apart: 41, of which 17 were waited for; matrix products, arithmetic and copies ran while one was open for 9% of the time, Pallas kernels for 3%

profile of v6, /device:TPU:0, one launch (start us, length us, event | category | flops | bytes accessed | tf_op | source)
XLA Modules:
  0.0 107.4 jit_solution(8745531373269071287)
XLA Ops:
  0.6 3.1 %collective-permute-start.5 = (bf16[32,4096]{1,0:T(8,128)(2,1)}, bf16[32,4096]{1,0:T(8,128)(2,1)S(1)}, u32[]{:S(2)}, u32[]{:S(2)}) collective-permute-start(bf16[32,4096]{1,0:T(8,128)(2,1)} %refs_3_.1), channel_id=1, source_target_pairs={{0,8},{1,9},{2,10},{3,11},{4,12},{5,13},{6,14},{7,15},{8,24},{9,25... | collective-permute-start | bytes 786440 | tf_op jit(solution)/shard_map/ppermute | solution.py:213
  3.8 2.1 %first_rows.1 = (bf16[2,16,4096]{2,1,0:T(8,128)(2,1)S(1)}, bf16[2,16,4096]{2,1,0:T(8,128)(2,1)S(1)}, bf16[2,16,4096]{2,1,0:T(8,128)(2,1)S(1)}, bf16[2,16,4096]{2...) custom-call(s32[2]{0:T(128)S(1)} %pad_add_fusion.spot, ...), custom_call_target="tpu_custom_call" | custom-call | tf_op jit(solution)/shard_map/first_rows/pallas_call | solution.py:132
  5.9 2.6 %collective-permute-start = (bf16[32,4224]{1,0:T(8,128)(2,1)S(1)}, bf16[32,4224]{1,0:T(8,128)(2,1)S(1)}, u32[]{:S(2)}, u32[]{:S(2)}) collective-permute-start(bf16[32,4224]{1,0:T(8,128)(2,1)S(1)} %get-tuple-element.52), channel_id=1, source_target_pairs={{0,8},{1,9},{2,10},{3,11},{4,12},{5,13},{6,14},{7,15},{8,24},{9,25... | collective-permute-start | bytes 811016 | tf_op jit(solution)/shard_map/ppermute | solution.py:213
  8.5 1.5 %collective-permute-start.2 = (bf16[2,16,4096]{2,1,0:T(8,128)(2,1)S(1)}, bf16[2,16,4096]{2,1,0:T(8,128)(2,1)S(1)}, u32[]{:S(2)}, u32[]{:S(2)}) collective-permute-start(bf16[2,16,4096]{2,1,0:T(8,128)(2,1)S(1)} %get-tuple-element.53), channel_id=1, source_target_pairs={{0,2},{1,3},{2,0},{3,1},{4,6},{5,7},{6,4},{7,5},{8,10},{9,11},{10,... | collective-permute-start | bytes 786440 | tf_op jit(solution)/shard_map/ppermute | solution.py:177
  10.1 1.5 %collective-permute-start.3 = (bf16[2,16,4096]{2,1,0:T(8,128)(2,1)S(1)}, bf16[2,16,4096]{2,1,0:T(8,128)(2,1)S(1)}, u32[]{:S(2)}, u32[]{:S(2)}) collective-permute-start(bf16[2,16,4096]{2,1,0:T(8,128)(2,1)S(1)} %get-tuple-element.54), channel_id=1, source_target_pairs={{0,6},{1,7},{2,4},{3,5},{4,2},{5,3},{6,0},{7,1},{8,14},{9,15},{10,... | collective-permute-start | bytes 786440 | tf_op jit(solution)/shard_map/ppermute | solution.py:177
  13.3 4.5 %collective-permute-done.held = bf16[32,4224]{1,0:T(8,128)(2,1)S(1)} collective-permute-done((bf16[32,4224]{1,0:T(8,128)(2,1)S(1)}, bf16[32,4224]{1,0:T(8,128)(2,1)S(1)}, u32[]{:S(2)}, u32[]{:S(2)}) %collective-permute-start) | collective-permute-done | bytes 270368 | tf_op jit(solution)/shard_map/ppermute | solution.py:213
  19.5 1.6 %collective-permute-start.7 = (bf16[2,16,4096]{2,1,0:T(8,128)(2,1)S(1)}, bf16[2,16,4096]{2,1,0:T(8,128)(2,1)S(1)}, u32[]{:S(2)}, u32[]{:S(2)}) collective-permute-start(bf16[2,16,4096]{2,1,0:T(8,128)(2,1)S(1)} %get-tuple-element.62), channel_id=1, source_target_pairs={{0,2},{1,3},{2,0},{3,1},{4,6},{5,7},{6,4},{7,5},{8,10},{9,11},{10,... | collective-permute-start | bytes 786440 | tf_op jit(solution)/shard_map/ppermute | solution.py:177
  21.1 3.3 %collective-permute-done.3 = bf16[2,16,4096]{2,1,0:T(8,128)(2,1)S(1)} collective-permute-done((bf16[2,16,4096]{2,1,0:T(8,128)(2,1)S(1)}, bf16[2,16,4096]{2,1,0:T(8,128)(2,1)S(1)}, u32[]{:S(2)}, u32[]{:S(2)}) %collective-permute-start.3) | collective-permute-done | bytes 262176 | tf_op jit(solution)/shard_map/ppermute | solution.py:177
  25.9 1.5 %collective-permute-start.9 = (bf16[2,16,4096]{2,1,0:T(8,128)(2,1)S(1)}, bf16[2,16,4096]{2,1,0:T(8,128)(2,1)S(1)}, u32[]{:S(2)}, u32[]{:S(2)}) collective-permute-start(bf16[2,16,4096]{2,1,0:T(8,128)(2,1)S(1)} %get-tuple-element.64), channel_id=1, source_target_pairs={{0,4},{1,5},{2,6},{3,7},{4,0},{5,1},{6,2},{7,3},{8,12},{9,13},{10,... | collective-permute-start | bytes 786440 | tf_op jit(solution)/shard_map/ppermute | solution.py:177
  27.4 1.9 %collective-permute-done.1.held = bf16[32,4224]{1,0:T(8,128)(2,1)S(1)} collective-permute-done((bf16[32,4224]{1,0:T(8,128)(2,1)S(1)}, bf16[32,4224]{1,0:T(8,128)(2,1)S(1)}, u32[]{:S(2)}, u32[]{:S(2)}) %collective-permute-start.1) | collective-permute-done | bytes 270368 | tf_op jit(solution)/shard_map/ppermute | solution.py:213
  31.1 1.6 %collective-permute-start.11 = (bf16[2,16,4096]{2,1,0:T(8,128)(2,1)S(1)}, bf16[2,16,4096]{2,1,0:T(8,128)(2,1)S(1)}, u32[]{:S(2)}, u32[]{:S(2)}) collective-permute-start(bf16[2,16,4096]{2,1,0:T(8,128)(2,1)S(1)} %get-tuple-element.69), channel_id=1, source_target_pairs={{0,2},{1,3},{2,0},{3,1},{4,6},{5,7},{6,4},{7,5},{8,10},{9,11},{10,... | collective-permute-start | bytes 786440 | tf_op jit(solution)/shard_map/ppermute | solution.py:177
  32.7 2.9 %collective-permute-done.8 = bf16[2,16,4096]{2,1,0:T(8,128)(2,1)S(1)} collective-permute-done((bf16[2,16,4096]{2,1,0:T(8,128)(2,1)S(1)}, bf16[2,16,4096]{2,1,0:T(8,128)(2,1)S(1)}, u32[]{:S(2)}, u32[]{:S(2)}) %collective-permute-start.8) | collective-permute-done | bytes 262176 | tf_op jit(solution)/shard_map/ppermute | solution.py:177
  37.0 1.5 %collective-permute-start.13 = (bf16[2,16,4096]{2,1,0:T(8,128)(2,1)S(1)}, bf16[2,16,4096]{2,1,0:T(8,128)(2,1)S(1)}, u32[]{:S(2)}, u32[]{:S(2)}) collective-permute-start(bf16[2,16,4096]{2,1,0:T(8,128)(2,1)S(1)} %get-tuple-element.71), channel_id=1, source_target_pairs={{0,4},{1,5},{2,6},{3,7},{4,0},{5,1},{6,2},{7,3},{8,12},{9,13},{10,... | collective-permute-start | bytes 786440 | tf_op jit(solution)/shard_map/ppermute | solution.py:177
  40.4 1.6 %collective-permute-start.15 = (bf16[16,4096]{1,0:T(8,128)(2,1)S(1)}, bf16[16,4096]{1,0:T(8,128)(2,1)S(1)}, u32[]{:S(2)}, u32[]{:S(2)}) collective-permute-start(bf16[16,4096]{1,0:T(8,128)(2,1)S(1)} %get-tuple-element.74), channel_id=1, source_target_pairs={{0,2},{1,3},{2,0},{3,1},{4,6},{5,7},{6,4},{7,5},{8,10},{9,11},{10,... | collective-permute-start | bytes 393224 | tf_op jit(solution)/shard_map/ppermute | solution.py:177
  42.0 1.5 %collective-permute-start.16 = (bf16[16,4096]{1,0:T(8,128)(2,1)S(1)}, bf16[16,4096]{1,0:T(8,128)(2,1)S(1)}, u32[]{:S(2)}, u32[]{:S(2)}) collective-permute-start(bf16[16,4096]{1,0:T(8,128)(2,1)S(1)} %get-tuple-element.75), channel_id=1, source_target_pairs={{0,6},{1,7},{2,4},{3,5},{4,2},{5,3},{6,0},{7,1},{8,14},{9,15},{10,... | collective-permute-start | bytes 393224 | tf_op jit(solution)/shard_map/ppermute | solution.py:177
  44.1 3.0 %collective-permute-done.12 = bf16[2,16,4096]{2,1,0:T(8,128)(2,1)S(1)} collective-permute-done((bf16[2,16,4096]{2,1,0:T(8,128)(2,1)S(1)}, bf16[2,16,4096]{2,1,0:T(8,128)(2,1)S(1)}, u32[]{:S(2)}, u32[]{:S(2)}) %collective-permute-start.12) | collective-permute-done | bytes 262176 | tf_op jit(solution)/shard_map/ppermute | solution.py:177
  47.1 4.8 %collective-permute-done.13 = bf16[2,16,4096]{2,1,0:T(8,128)(2,1)S(1)} collective-permute-done((bf16[2,16,4096]{2,1,0:T(8,128)(2,1)S(1)}, bf16[2,16,4096]{2,1,0:T(8,128)(2,1)S(1)}, u32[]{:S(2)}, u32[]{:S(2)}) %collective-permute-start.13) | collective-permute-done | bytes 262176 | tf_op jit(solution)/shard_map/ppermute | solution.py:177
  53.3 1.5 %collective-permute-start.21 = (bf16[16,4096]{1,0:T(8,128)(2,1)S(1)}, bf16[16,4096]{1,0:T(8,128)(2,1)S(1)}, u32[]{:S(2)}, u32[]{:S(2)}) collective-permute-start(bf16[16,4096]{1,0:T(8,128)(2,1)S(1)} %get-tuple-element.79), channel_id=1, source_target_pairs={{0,6},{1,7},{2,4},{3,5},{4,2},{5,3},{6,0},{7,1},{8,14},{9,15},{10,... | collective-permute-start | bytes 393224 | tf_op jit(solution)/shard_map/ppermute | solution.py:177
  57.5 1.8 %fusion.4 = f32[256,768]{1,0:T(8,128)S(1)} fusion(bf16[256,4096]{1,0:T(8,128)(2,1)S(1)} %constant_dynamic-update-slice_fusion, bf16[1,4096,768]{2,1,0:T(8,128)(2,1)S(1)} %copy-done), kind=kOutput, calls=%fused_computation.5 | convolution fusion | flops 1610612736 | bytes 9175040 | tf_op jit(solution)/shard_map/dot_general | solution.py:158
  60.4 1.8 %fusion.8 = f32[256,768]{1,0:T(8,128)S(1)} fusion(bf16[256,4096]{1,0:T(8,128)(2,1)S(1)} %constant_dynamic-update-slice_fusion, bf16[1,4096,768]{2,1,0:T(8,128)(2,1)S(1)} %bitcast.151), kind=kOutput, calls=%fused_computation.9 | convolution fusion | flops 1610612736 | bytes 9175040 | tf_op jit(solution)/shard_map/dot_general | solution.py:157
  64.8 2.1 %fusion = f32[256,768]{1,0:T(8,128)S(1)} fusion(bf16[256,4096]{1,0:T(8,128)(2,1)S(1)} %constant_dynamic-update-slice_fusion.17, bf16[1,768,4096]{2,1,0:T(8,128)(2,1)S(1)} %bitcast.159), kind=kOutput, calls=%fused_computation.1 | convolution fusion | flops 1610612736 | bytes 9175040 | tf_op jit(solution)/shard_map/dot_general | solution.py:166
  66.9 1.9 %fusion.2 = f32[256,4096]{1,0:T(8,128)S(1)} fusion(bf16[1,4096,768]{2,1,0:T(8,128)(2,1)S(1)} %bitcast.161, f32[256,768]{1,0:T(8,128)S(1)} %fusion, f32[256,768]{1,0:T(8,128)S(1)} %fusion.8), kind=kOutput, calls=%fused_computation.3 | convolution fusion | flops 1611792384 | bytes 12058624 | tf_op jit(solution)/shard_map/dot_general | solution.py:171
  68.8 2.0 %fusion.13 = bf16[256,4096]{1,0:T(8,128)(2,1)S(1)} fusion(f32[256,4096]{1,0:T(8,128)S(1)} %fusion.2, bf16[1,4096,768]{2,1,0:T(8,128)(2,1)S(1)} %bitcast.151, f32[256,768]{1,0:T(8,128)S(1)} %fusion.8, f32[256,768]{1,0:T(8,128)S(1)} %fusion, f32[256,768]{1,0:T(8,128)S(1)} %fusion.4), kind=kOutput, calls=%fused_computation.12 | convolution fusion | flops 1614675968 | bytes 14942208 | tf_op jit(solution)/shard_map/dot_general | solution.py:170
  75.0 1.5 %collective-permute-start.31 = (bf16[16,4096]{1,0:T(8,128)(2,1)S(1)}, bf16[16,4096]{1,0:T(8,128)(2,1)S(1)}, u32[]{:S(2)}, u32[]{:S(2)}) collective-permute-start(bf16[16,4096]{1,0:T(8,128)(2,1)S(1)} %get-tuple-element.114), channel_id=1, source_target_pairs={{0,6},{1,7},{2,4},{3,5},{4,2},{5,3},{6,0},{7,1},{8,14},{9,15},{10,... | collective-permute-start | bytes 393224 | tf_op jit(solution)/shard_map/ppermute | solution.py:244
  80.8 1.5 %collective-permute-done.30 = bf16[16,4096]{1,0:T(8,128)(2,1)S(1)} collective-permute-done((bf16[16,4096]{1,0:T(8,128)(2,1)S(1)}, bf16[16,4096]{1,0:T(8,128)(2,1)S(1)}, u32[]{:S(2)}, u32[]{:S(2)}) %collective-permute-start.30) | collective-permute-done | bytes 131104 | tf_op jit(solution)/shard_map/ppermute | solution.py:244
  86.3 1.6 %collective-permute-done.33 = bf16[16,4096]{1,0:T(8,128)(2,1)S(1)} collective-permute-done((bf16[16,4096]{1,0:T(8,128)(2,1)S(1)}, bf16[16,4096]{1,0:T(8,128)(2,1)S(1)}, u32[]{:S(2)}, u32[]{:S(2)}) %collective-permute-start.33) | collective-permute-done | bytes 131104 | tf_op jit(solution)/shard_map/ppermute | solution.py:244
  87.9 1.6 %collective-permute-start.38 = (bf16[16,4096]{1,0:T(8,128)(2,1)S(1)}, bf16[16,4096]{1,0:T(8,128)(2,1)S(1)}, u32[]{:S(2)}, u32[]{:S(2)}) collective-permute-start(bf16[16,4096]{1,0:T(8,128)(2,1)S(1)} %get-tuple-element.106), channel_id=1, source_target_pairs={{0,6},{1,7},{2,4},{3,5},{4,2},{5,3},{6,0},{7,1},{8,14},{9,15},{10,... | collective-permute-start | bytes 393224 | tf_op jit(solution)/shard_map/ppermute | solution.py:244
  91.8 1.5 %collective-permute-start.27 = (bf16[16,4096]{1,0:T(8,128)(2,1)S(1)}, bf16[16,4096]{1,0:T(8,128)(2,1)S(1)}, u32[]{:S(2)}, u32[]{:S(2)}) collective-permute-start(bf16[16,4096]{1,0:T(8,128)(2,1)S(1)} %get-tuple-element.122), channel_id=1, source_target_pairs={{0,6},{1,7},{2,4},{3,5},{4,2},{5,3},{6,0},{7,1},{8,14},{9,15},{10,... | collective-permute-start | bytes 393224 | tf_op jit(solution)/shard_map/ppermute | solution.py:244
  93.3 1.6 %collective-permute-done.38 = bf16[16,4096]{1,0:T(8,128)(2,1)S(1)} collective-permute-done((bf16[16,4096]{1,0:T(8,128)(2,1)S(1)}, bf16[16,4096]{1,0:T(8,128)(2,1)S(1)}, u32[]{:S(2)}, u32[]{:S(2)}) %collective-permute-start.38) | collective-permute-done | bytes 131104 | tf_op jit(solution)/shard_map/ppermute | solution.py:244
  96.4 1.7 %collective-permute-start.40 = (bf16[32,4096]{1,0:T(8,128)(2,1)S(1)}, bf16[32,4096]{1,0:T(8,128)(2,1)S(1)}, u32[]{:S(2)}, u32[]{:S(2)}) collective-permute-start(bf16[32,4096]{1,0:T(8,128)(2,1)S(1)} %fusion.18), channel_id=1, source_target_pairs={{8,0},{9,1},{10,2},{11,3},{12,4},{13,5},{14,6},{15,7},{24,8},{25,9... | collective-permute-start | bytes 786440 | tf_op jit(solution)/shard_map/ppermute | solution.py:265
  98.1 4.5 %convolution_convert_fusion = bf16[768,4096]{1,0:T(8,128)(2,1)} fusion(bf16[256,768]{1,0:T(8,128)(2,1)S(1)} %multiply_convert_fusion, bf16[256,4096]{1,0:T(8,128)(2,1)S(1)} %constant_dynamic-update-slice_fusion.17), kind=kOutput, calls=%fused_computation | convolution fusion | flops 1613758464 | bytes 8781824 | tf_op jit(solution)/shard_map/dot_general | solution.py:255
  102.7 3.8 %collective-permute-done.36 = bf16[32,4096]{1,0:T(8,128)(2,1)S(1)} collective-permute-done((bf16[32,4096]{1,0:T(8,128)(2,1)S(1)}, bf16[32,4096]{1,0:T(8,128)(2,1)S(1)}, u32[]{:S(2)}, u32[]{:S(2)}) %collective-permute-start.36) | collective-permute-done | bytes 262176 | tf_op jit(solution)/shard_map/ppermute | solution.py:265
  (129 shorter events, 35.3 us)
Async XLA Ops:
  0.6 11.4 %collective-permute-start.5 = (bf16[32,4096]{1,0:T(8,128)(2,1)}, bf16[32,4096]{1,0:T(8,128)(2,1)S(1)}, u32[]{:S(2)}, u32[]{:S(2)}) collective-permute-start(bf16[32,4096]{1,0:T(8,128)(2,1)} %refs_3_.1), channel_id=1, source_target_pairs={{0,8},{1,9},{2,10},{3,11},{4,12},{5,13},{6,14},{7,15},{8,24},{9,25... | collective-permute-start | bytes 786440 | tf_op jit(solution)/shard_map/ppermute | solution.py:213
  5.9 12.0 %collective-permute-start = (bf16[32,4224]{1,0:T(8,128)(2,1)S(1)}, bf16[32,4224]{1,0:T(8,128)(2,1)S(1)}, u32[]{:S(2)}, u32[]{:S(2)}) collective-permute-start(bf16[32,4224]{1,0:T(8,128)(2,1)S(1)} %get-tuple-element.52), channel_id=1, source_target_pairs={{0,8},{1,9},{2,10},{3,11},{4,12},{5,13},{6,14},{7,15},{8,24},{9,25... | collective-permute-start | bytes 811016 | tf_op jit(solution)/shard_map/ppermute | solution.py:213
  8.5 11.0 %collective-permute-start.2 = (bf16[2,16,4096]{2,1,0:T(8,128)(2,1)S(1)}, bf16[2,16,4096]{2,1,0:T(8,128)(2,1)S(1)}, u32[]{:S(2)}, u32[]{:S(2)}) collective-permute-start(bf16[2,16,4096]{2,1,0:T(8,128)(2,1)S(1)} %get-tuple-element.53), channel_id=1, source_target_pairs={{0,2},{1,3},{2,0},{3,1},{4,6},{5,7},{6,4},{7,5},{8,10},{9,11},{10,... | collective-permute-start | bytes 786440 | tf_op jit(solution)/shard_map/ppermute | solution.py:177
  10.1 14.3 %collective-permute-start.3 = (bf16[2,16,4096]{2,1,0:T(8,128)(2,1)S(1)}, bf16[2,16,4096]{2,1,0:T(8,128)(2,1)S(1)}, u32[]{:S(2)}, u32[]{:S(2)}) collective-permute-start(bf16[2,16,4096]{2,1,0:T(8,128)(2,1)S(1)} %get-tuple-element.54), channel_id=1, source_target_pairs={{0,6},{1,7},{2,4},{3,5},{4,2},{5,3},{6,0},{7,1},{8,14},{9,15},{10,... | collective-permute-start | bytes 786440 | tf_op jit(solution)/shard_map/ppermute | solution.py:177
  11.5 14.3 %collective-permute-start.4 = (bf16[2,16,4096]{2,1,0:T(8,128)(2,1)S(1)}, bf16[2,16,4096]{2,1,0:T(8,128)(2,1)S(1)}, u32[]{:S(2)}, u32[]{:S(2)}) collective-permute-start(bf16[2,16,4096]{2,1,0:T(8,128)(2,1)S(1)} %get-tuple-element.55), channel_id=1, source_target_pairs={{0,4},{1,5},{2,6},{3,7},{4,0},{5,1},{6,2},{7,3},{8,12},{9,13},{10,... | collective-permute-start | bytes 786440 | tf_op jit(solution)/shard_map/ppermute | solution.py:177
  12.1 15.3 %collective-permute-start.10 = (bf16[32,4096]{1,0:T(8,128)(2,1)S(1)}, bf16[32,4096]{1,0:T(8,128)(2,1)S(1)}, u32[]{:S(2)}, u32[]{:S(2)}) collective-permute-start(bf16[32,4096]{1,0:T(8,128)(2,1)S(1)} %collective-permute-done.5.tok), channel_id=1, source_target_pairs={{0,8},{1,9},{2,10},{3,11},{4,12},{5,13},{6,14},{7,15},{8,24},{9,25... | collective-permute-start | bytes 786440 | tf_op jit(solution)/shard_map/ppermute | solution.py:213
  17.9 11.4 %collective-permute-start.1 = (bf16[32,4224]{1,0:T(8,128)(2,1)S(1)}, bf16[32,4224]{1,0:T(8,128)(2,1)S(1)}, u32[]{:S(2)}, u32[]{:S(2)}) collective-permute-start(bf16[32,4224]{1,0:T(8,128)(2,1)S(1)} %collective-permute-done.held), channel_id=1, source_target_pairs={{0,8},{1,9},{2,10},{3,11},{4,12},{5,13},{6,14},{7,15},{8,24},{9,25... | collective-permute-start | bytes 811016 | tf_op jit(solution)/shard_map/ppermute | solution.py:213
  19.5 11.5 %collective-permute-start.7 = (bf16[2,16,4096]{2,1,0:T(8,128)(2,1)S(1)}, bf16[2,16,4096]{2,1,0:T(8,128)(2,1)S(1)}, u32[]{:S(2)}, u32[]{:S(2)}) collective-permute-start(bf16[2,16,4096]{2,1,0:T(8,128)(2,1)S(1)} %get-tuple-element.62), channel_id=1, source_target_pairs={{0,2},{1,3},{2,0},{3,1},{4,6},{5,7},{6,4},{7,5},{8,10},{9,11},{10,... | collective-permute-start | bytes 786440 | tf_op jit(solution)/shard_map/ppermute | solution.py:177
  24.4 11.2 %collective-permute-start.8 = (bf16[2,16,4096]{2,1,0:T(8,128)(2,1)S(1)}, bf16[2,16,4096]{2,1,0:T(8,128)(2,1)S(1)}, u32[]{:S(2)}, u32[]{:S(2)}) collective-permute-start(bf16[2,16,4096]{2,1,0:T(8,128)(2,1)S(1)} %get-tuple-element.63), channel_id=1, source_target_pairs={{0,6},{1,7},{2,4},{3,5},{4,2},{5,3},{6,0},{7,1},{8,14},{9,15},{10,... | collective-permute-start | bytes 786440 | tf_op jit(solution)/shard_map/ppermute | solution.py:177
  25.9 11.1 %collective-permute-start.9 = (bf16[2,16,4096]{2,1,0:T(8,128)(2,1)S(1)}, bf16[2,16,4096]{2,1,0:T(8,128)(2,1)S(1)}, u32[]{:S(2)}, u32[]{:S(2)}) collective-permute-start(bf16[2,16,4096]{2,1,0:T(8,128)(2,1)S(1)} %get-tuple-element.64), channel_id=1, source_target_pairs={{0,4},{1,5},{2,6},{3,7},{4,0},{5,1},{6,2},{7,3},{8,12},{9,13},{10,... | collective-permute-start | bytes 786440 | tf_op jit(solution)/shard_map/ppermute | solution.py:177
  27.4 12.5 %collective-permute-start.14 = (bf16[32,4096]{1,0:T(8,128)(2,1)S(1)}, bf16[32,4096]{1,0:T(8,128)(2,1)S(1)}, u32[]{:S(2)}, u32[]{:S(2)}) collective-permute-start(bf16[32,4096]{1,0:T(8,128)(2,1)S(1)} %collective-permute-done.10.tok), channel_id=1, source_target_pairs={{0,8},{1,9},{2,10},{3,11},{4,12},{5,13},{6,14},{7,15},{8,24},{9,25... | collective-permute-start | bytes 786440 | tf_op jit(solution)/shard_map/ppermute | solution.py:213
  29.3 10.6 %collective-permute-start.6 = (bf16[32,4224]{1,0:T(8,128)(2,1)S(1)}, bf16[32,4224]{1,0:T(8,128)(2,1)S(1)}, u32[]{:S(2)}, u32[]{:S(2)}) collective-permute-start(bf16[32,4224]{1,0:T(8,128)(2,1)S(1)} %collective-permute-done.1.held), channel_id=1, source_target_pairs={{0,8},{1,9},{2,10},{3,11},{4,12},{5,13},{6,14},{7,15},{8,24},{9,25... | collective-permute-start | bytes 811016 | tf_op jit(solution)/shard_map/ppermute | solution.py:213
  31.1 12.5 %collective-permute-start.11 = (bf16[2,16,4096]{2,1,0:T(8,128)(2,1)S(1)}, bf16[2,16,4096]{2,1,0:T(8,128)(2,1)S(1)}, u32[]{:S(2)}, u32[]{:S(2)}) collective-permute-start(bf16[2,16,4096]{2,1,0:T(8,128)(2,1)S(1)} %get-tuple-element.69), channel_id=1, source_target_pairs={{0,2},{1,3},{2,0},{3,1},{4,6},{5,7},{6,4},{7,5},{8,10},{9,11},{10,... | collective-permute-start | bytes 786440 | tf_op jit(solution)/shard_map/ppermute | solution.py:177
  35.6 11.5 %collective-permute-start.12 = (bf16[2,16,4096]{2,1,0:T(8,128)(2,1)S(1)}, bf16[2,16,4096]{2,1,0:T(8,128)(2,1)S(1)}, u32[]{:S(2)}, u32[]{:S(2)}) collective-permute-start(bf16[2,16,4096]{2,1,0:T(8,128)(2,1)S(1)} %get-tuple-element.70), channel_id=1, source_target_pairs={{0,6},{1,7},{2,4},{3,5},{4,2},{5,3},{6,0},{7,1},{8,14},{9,15},{10,... | collective-permute-start | bytes 786440 | tf_op jit(solution)/shard_map/ppermute | solution.py:177
  37.0 14.9 %collective-permute-start.13 = (bf16[2,16,4096]{2,1,0:T(8,128)(2,1)S(1)}, bf16[2,16,4096]{2,1,0:T(8,128)(2,1)S(1)}, u32[]{:S(2)}, u32[]{:S(2)}) collective-permute-start(bf16[2,16,4096]{2,1,0:T(8,128)(2,1)S(1)} %get-tuple-element.71), channel_id=1, source_target_pairs={{0,4},{1,5},{2,6},{3,7},{4,0},{5,1},{6,2},{7,3},{8,12},{9,13},{10,... | collective-permute-start | bytes 786440 | tf_op jit(solution)/shard_map/ppermute | solution.py:177
  40.4 12.9 %collective-permute-start.15 = (bf16[16,4096]{1,0:T(8,128)(2,1)S(1)}, bf16[16,4096]{1,0:T(8,128)(2,1)S(1)}, u32[]{:S(2)}, u32[]{:S(2)}) collective-permute-start(bf16[16,4096]{1,0:T(8,128)(2,1)S(1)} %get-tuple-element.74), channel_id=1, source_target_pairs={{0,2},{1,3},{2,0},{3,1},{4,6},{5,7},{6,4},{7,5},{8,10},{9,11},{10,... | collective-permute-start | bytes 393224 | tf_op jit(solution)/shard_map/ppermute | solution.py:177
  42.0 12.9 %collective-permute-start.16 = (bf16[16,4096]{1,0:T(8,128)(2,1)S(1)}, bf16[16,4096]{1,0:T(8,128)(2,1)S(1)}, u32[]{:S(2)}, u32[]{:S(2)}) collective-permute-start(bf16[16,4096]{1,0:T(8,128)(2,1)S(1)} %get-tuple-element.75), channel_id=1, source_target_pairs={{0,6},{1,7},{2,4},{3,5},{4,2},{5,3},{6,0},{7,1},{8,14},{9,15},{10,... | collective-permute-start | bytes 393224 | tf_op jit(solution)/shard_map/ppermute | solution.py:177
  43.5 12.3 %collective-permute-start.17 = (bf16[16,4096]{1,0:T(8,128)(2,1)S(1)}, bf16[16,4096]{1,0:T(8,128)(2,1)S(1)}, u32[]{:S(2)}, u32[]{:S(2)}) collective-permute-start(bf16[16,4096]{1,0:T(8,128)(2,1)S(1)} %get-tuple-element.76), channel_id=1, source_target_pairs={{0,4},{1,5},{2,6},{3,7},{4,0},{5,1},{6,2},{7,3},{8,12},{9,13},{10,... | collective-permute-start | bytes 393224 | tf_op jit(solution)/shard_map/ppermute | solution.py:177
  51.9 10.2 %collective-permute-start.20 = (bf16[16,4096]{1,0:T(8,128)(2,1)S(1)}, bf16[16,4096]{1,0:T(8,128)(2,1)S(1)}, u32[]{:S(2)}, u32[]{:S(2)}) collective-permute-start(bf16[16,4096]{1,0:T(8,128)(2,1)S(1)} %get-tuple-element.78), channel_id=1, source_target_pairs={{0,2},{1,3},{2,0},{3,1},{4,6},{5,7},{6,4},{7,5},{8,10},{9,11},{10,... | collective-permute-start | bytes 393224 | tf_op jit(solution)/shard_map/ppermute | solution.py:177
  53.3 8.9 %collective-permute-start.21 = (bf16[16,4096]{1,0:T(8,128)(2,1)S(1)}, bf16[16,4096]{1,0:T(8,128)(2,1)S(1)}, u32[]{:S(2)}, u32[]{:S(2)}) collective-permute-start(bf16[16,4096]{1,0:T(8,128)(2,1)S(1)} %get-tuple-element.79), channel_id=1, source_target_pairs={{0,6},{1,7},{2,4},{3,5},{4,2},{5,3},{6,0},{7,1},{8,14},{9,15},{10,... | collective-permute-start | bytes 393224 | tf_op jit(solution)/shard_map/ppermute | solution.py:177
  73.9 8.5 %collective-permute-start.30 = (bf16[16,4096]{1,0:T(8,128)(2,1)S(1)}, bf16[16,4096]{1,0:T(8,128)(2,1)S(1)}, u32[]{:S(2)}, u32[]{:S(2)}) collective-permute-start(bf16[16,4096]{1,0:T(8,128)(2,1)S(1)} %get-tuple-element.115), channel_id=1, source_target_pairs={{0,4},{1,5},{2,6},{3,7},{4,0},{5,1},{6,2},{7,3},{8,12},{9,13},{10,... | collective-permute-start | bytes 393224 | tf_op jit(solution)/shard_map/ppermute | solution.py:244
  75.0 8.5 %collective-permute-start.31 = (bf16[16,4096]{1,0:T(8,128)(2,1)S(1)}, bf16[16,4096]{1,0:T(8,128)(2,1)S(1)}, u32[]{:S(2)}, u32[]{:S(2)}) collective-permute-start(bf16[16,4096]{1,0:T(8,128)(2,1)S(1)} %get-tuple-element.114), channel_id=1, source_target_pairs={{0,6},{1,7},{2,4},{3,5},{4,2},{5,3},{6,0},{7,1},{8,14},{9,15},{10,... | collective-permute-start | bytes 393224 | tf_op jit(solution)/shard_map/ppermute | solution.py:244
  76.5 8.5 %collective-permute-start.32 = (bf16[16,4096]{1,0:T(8,128)(2,1)S(1)}, bf16[16,4096]{1,0:T(8,128)(2,1)S(1)}, u32[]{:S(2)}, u32[]{:S(2)}) collective-permute-start(bf16[16,4096]{1,0:T(8,128)(2,1)S(1)} %get-tuple-element.109), channel_id=1, source_target_pairs={{0,2},{1,3},{2,0},{3,1},{4,6},{5,7},{6,4},{7,5},{8,10},{9,11},{10,... | collective-permute-start | bytes 393224 | tf_op jit(solution)/shard_map/ppermute | solution.py:244
  77.4 10.4 %collective-permute-start.33 = (bf16[16,4096]{1,0:T(8,128)(2,1)S(1)}, bf16[16,4096]{1,0:T(8,128)(2,1)S(1)}, u32[]{:S(2)}, u32[]{:S(2)}) collective-permute-start(bf16[16,4096]{1,0:T(8,128)(2,1)S(1)} %get-tuple-element.111), channel_id=1, source_target_pairs={{0,4},{1,5},{2,6},{3,7},{4,0},{5,1},{6,2},{7,3},{8,12},{9,13},{10,... | collective-permute-start | bytes 393224 | tf_op jit(solution)/shard_map/ppermute | solution.py:244
  79.3 10.1 %collective-permute-start.34 = (bf16[16,4096]{1,0:T(8,128)(2,1)S(1)}, bf16[16,4096]{1,0:T(8,128)(2,1)S(1)}, u32[]{:S(2)}, u32[]{:S(2)}) collective-permute-start(bf16[16,4096]{1,0:T(8,128)(2,1)S(1)} %get-tuple-element.110), channel_id=1, source_target_pairs={{0,6},{1,7},{2,4},{3,5},{4,2},{5,3},{6,0},{7,1},{8,14},{9,15},{10,... | collective-permute-start | bytes 393224 | tf_op jit(solution)/shard_map/ppermute | solution.py:244
  82.3 8.5 %collective-permute-start.35 = (bf16[16,4096]{1,0:T(8,128)(2,1)S(1)}, bf16[16,4096]{1,0:T(8,128)(2,1)S(1)}, u32[]{:S(2)}, u32[]{:S(2)}) collective-permute-start(bf16[16,4096]{1,0:T(8,128)(2,1)S(1)} %get-tuple-element.105), channel_id=1, source_target_pairs={{0,2},{1,3},{2,0},{3,1},{4,6},{5,7},{6,4},{7,5},{8,10},{9,11},{10,... | collective-permute-start | bytes 393224 | tf_op jit(solution)/shard_map/ppermute | solution.py:244
  85.0 11.1 %collective-permute-start.39 = (bf16[32,4096]{1,0:T(8,128)(2,1)S(1)}, bf16[32,4096]{1,0:T(8,128)(2,1)S(1)}, u32[]{:S(2)}, u32[]{:S(2)}) collective-permute-start(bf16[32,4096]{1,0:T(8,128)(2,1)S(1)} %convolution_convert_fusion.2), channel_id=1, source_target_pairs={{8,0},{9,1},{10,2},{11,3},{12,4},{13,5},{14,6},{15,7},{24,8},{25,9... | collective-permute-start | bytes 786440 | tf_op jit(solution)/shard_map/ppermute | solution.py:265
  89.5 13.2 %collective-permute-start.25 = (bf16[16,4096]{1,0:T(8,128)(2,1)S(1)}, bf16[16,4096]{1,0:T(8,128)(2,1)S(1)}, u32[]{:S(2)}, u32[]{:S(2)}) collective-permute-start(bf16[16,4096]{1,0:T(8,128)(2,1)S(1)} %get-tuple-element.121), channel_id=1, source_target_pairs={{0,2},{1,3},{2,0},{3,1},{4,6},{5,7},{6,4},{7,5},{8,10},{9,11},{10,... | collective-permute-start | bytes 393224 | tf_op jit(solution)/shard_map/ppermute | solution.py:244
  90.8 11.8 %collective-permute-start.26 = (bf16[16,4096]{1,0:T(8,128)(2,1)S(1)}, bf16[16,4096]{1,0:T(8,128)(2,1)S(1)}, u32[]{:S(2)}, u32[]{:S(2)}) collective-permute-start(bf16[16,4096]{1,0:T(8,128)(2,1)S(1)} %get-tuple-element.123), channel_id=1, source_target_pairs={{0,4},{1,5},{2,6},{3,7},{4,0},{5,1},{6,2},{7,3},{8,12},{9,13},{10,... | collective-permute-start | bytes 393224 | tf_op jit(solution)/shard_map/ppermute | solution.py:244
  91.8 10.9 %collective-permute-start.27 = (bf16[16,4096]{1,0:T(8,128)(2,1)S(1)}, bf16[16,4096]{1,0:T(8,128)(2,1)S(1)}, u32[]{:S(2)}, u32[]{:S(2)}) collective-permute-start(bf16[16,4096]{1,0:T(8,128)(2,1)S(1)} %get-tuple-element.122), channel_id=1, source_target_pairs={{0,6},{1,7},{2,4},{3,5},{4,2},{5,3},{6,0},{7,1},{8,14},{9,15},{10,... | collective-permute-start | bytes 393224 | tf_op jit(solution)/shard_map/ppermute | solution.py:244
  94.9 11.6 %collective-permute-start.36 = (bf16[32,4096]{1,0:T(8,128)(2,1)S(1)}, bf16[32,4096]{1,0:T(8,128)(2,1)S(1)}, u32[]{:S(2)}, u32[]{:S(2)}) collective-permute-start(bf16[32,4096]{1,0:T(8,128)(2,1)S(1)} %convolution_convert_fusion.1), channel_id=1, source_target_pairs={{0,8},{1,9},{2,10},{3,11},{4,12},{5,13},{6,14},{7,15},{8,24},{9,25... | collective-permute-start | bytes 786440 | tf_op jit(solution)/shard_map/ppermute | solution.py:265
  96.4 10.1 %collective-permute-start.40 = (bf16[32,4096]{1,0:T(8,128)(2,1)S(1)}, bf16[32,4096]{1,0:T(8,128)(2,1)S(1)}, u32[]{:S(2)}, u32[]{:S(2)}) collective-permute-start(bf16[32,4096]{1,0:T(8,128)(2,1)S(1)} %fusion.18), channel_id=1, source_target_pairs={{8,0},{9,1},{10,2},{11,3},{12,4},{13,5},{14,6},{15,7},{24,8},{25,9... | collective-permute-start | bytes 786440 | tf_op jit(solution)/shard_map/ppermute | solution.py:265
  (16 other events, 81.3 us)
